TPU v7x, 512 devices: a whole 4x8x8 slice. The times are simulated.
512 devices in a mesh: chan: 64 (over y, x, core), rad: 8 (over z).
Axes of the slice: x: 4, y: 8, z: 8, core: 2. Of those that a mesh axis runs over, the one named last changes fastest.
Arguments:
- trial: bfloat16 [64, 256, 2048], P(None, 'chan', 'rad')
- band: bfloat16 [256, 17, 2048], P('chan', None, 'rad'), may hold values from -1.5 to 1.5
- band_width: int32 [256], P('chan'), may hold values from 1 to 8
- energies: float32 [256], P('chan'), may hold values from 0.5 to 8
- coupling: bfloat16 [2048, 2048, 256], P('chan', 'rad')
- reach: int32 [2048], P('chan'), may hold values from 1 to 8
- pair_target: int32 [2048], P('chan'), may hold values from 0 to 255, as said below
- pair_source: int32 [2048], P('chan'), may hold values from 0 to 255, as said below
- chan_slot: int32 [256], replicated, may hold values from 0 to 255, as said below
Outputs:
- residual: bfloat16 [64, 256, 2048], P(None, 'chan', 'rad')
- rayleigh: float32 [64, 64], replicated
Inputs may be any that keep to these rules, and one draw needn't show every extreme that they name: A permutation: channel c's rows stand at slot chan_slot[c]. `pair_target`: the pairs of block t of 32 pairs target channels whose slots lie in t * 4 to t * 4 + 3. `pair_source`: in each block of 32 pairs, at most 1 pair has its source slot in any one aligned group of 4 slots (so the 32 sources lie in 32 different groups).
All inputs are finite; a program needn't handle non-finite values.
Results may differ from a plain program's by a relative error of at most 0.0061.
Values may be sent and summed in bfloat16 or wider, within the bound.
No kernel may reach another device: no remote copies, remote signals or barrier semaphores. Data moves between devices by JAX's collectives and lax.ppermute only.
A program may use at most 64 MiB of HBM per device.

v0:
```python
import jax
import jax.numpy as jnp
from jax import lax
from jax.sharding import PartitionSpec as P

BW = 8
BLK = 256


def padded_2(value, sides, width):
    for axis, dim in sides:
        devices, length = (lax.axis_size(axis), value.shape[dim])
        up = [(i, (i + 1) % devices) for i in range(devices - 1)]
        down = [(j, i) for i, j in up]
        last = lax.slice_in_dim(value, length - width, length, axis=dim)
        first = lax.slice_in_dim(value, 0, width, axis=dim)
        before = lax.ppermute(last, axis, up)
        after = lax.ppermute(first, axis, down)
        value = jnp.concatenate([before, value, after], axis=dim)
    return value


def lookup(table, wanted_ids):
    match = wanted_ids[:, None] == jnp.arange(table.shape[0], dtype=jnp.int32)[None, :]
    return jnp.sum(jnp.where(match, table[None, :], 0), axis=1)


def body(trial, band, band_width, energies, coupling, reach, pair_target, pair_source, chan_slot):
    chan_dev = trial.shape[1]
    slab_rows = trial.shape[2]
    pair_count = coupling.shape[0]
    vec_count = trial.shape[0]
    correlation = lax.psum(
        jnp.einsum("kcr,lcr->kl", trial, trial, preferred_element_type=jnp.float32), ("chan", "rad")
    )
    padded = padded_2(trial, (("rad", 2),), BW)
    running = energies[None, :, None] * trial.astype(jnp.float32)
    for offset in range(2 * BW + 1):
        live_mask = (abs(offset - BW) <= band_width).astype(jnp.float32)
        running = running + (live_mask[:, None] * band[:, offset, :].astype(jnp.float32))[
            None
        ] * padded[:, :, offset : offset + slab_rows].astype(jnp.float32)
    base_slot = lax.axis_index("chan") * chan_dev
    target_local = lookup(chan_slot, pair_target) - base_slot
    source_slot = lookup(chan_slot, pair_source)
    shard_rows = lax.all_gather(trial, "chan", axis=1, tiled=True)
    picker = (
        source_slot[:, None] == jnp.arange(shard_rows.shape[1], dtype=jnp.int32)[None, :]
    ).astype(jnp.bfloat16)
    sources = jnp.einsum(
        "pc,kcr->pkr", picker, shard_rows, preferred_element_type=jnp.float32
    ).astype(jnp.bfloat16)
    blocks_here = slab_rows // BLK
    coupled = jnp.einsum(
        "pbij,pkbj->pkbi",
        coupling.reshape(pair_count, blocks_here, BLK, BLK),
        sources.reshape(pair_count, vec_count, blocks_here, BLK),
        preferred_element_type=jnp.float32,
    )
    block_ids = lax.axis_index("rad") * blocks_here + jnp.arange(blocks_here, dtype=jnp.int32)
    reach_mask = (block_ids[None, :] < reach[:, None]).astype(jnp.float32)
    coupled = (coupled * reach_mask[:, None, :, None]).reshape(pair_count, vec_count, slab_rows)
    target_hit = (target_local[:, None] == jnp.arange(chan_dev, dtype=jnp.int32)[None, :]).astype(
        jnp.float32
    )
    running = running + jnp.einsum(
        "pc,pkr->kcr", target_hit, coupled, precision=lax.Precision.HIGHEST
    )
    image = running.astype(jnp.bfloat16)
    local_proj = jnp.einsum("kcr,lcr->kl", trial, image, preferred_element_type=jnp.float32)
    projected = lax.psum(local_proj, ("chan", "rad"))
    factor = jnp.linalg.cholesky(correlation)
    halfway = lax.linalg.triangular_solve(factor, projected, left_side=True, lower=True)
    rayleigh = lax.linalg.triangular_solve(
        factor, halfway, left_side=True, lower=True, transpose_a=True
    )
    rounded = rayleigh.astype(jnp.bfloat16)
    residual = image.astype(jnp.float32) - jnp.einsum(
        "kcr,kl->lcr", trial, rounded, preferred_element_type=jnp.float32
    )
    return (residual.astype(jnp.bfloat16), rayleigh)


def solution(mesh):
    placed = (
        P(None, "chan", "rad"),
        P("chan", None, "rad"),
        P("chan"),
        P("chan"),
        P("chan", "rad", None),
        P("chan"),
        P("chan"),
        P("chan"),
        P(),
    )
    return jax.shard_map(
        body, mesh=mesh, in_specs=placed, out_specs=(P(None, "chan", "rad"), P()), check_vma=False
    )
```

profile of v0, /device:TPU:1, one launch (start us, length us, event | category | flops | bytes accessed | tf_op | source)
XLA Modules:
  0.0 238.8 jit_solution(4237499792245796679)
XLA Ops:
  7.2 0.0 all-gather.2.cloned.1.call-start
  7.2 1.6 copy.26
  8.8 0.0 all-gather.2.cloned.1.call-update
  8.8 1.0 fusion.54
  9.8 1.3 collective-permute-start.1
  11.1 5.5 %collective-permute-start = (bf16[64,4,8]{2,1,0:T(4,128)(2,1)S(1)}, bf16[64,4,8]{2,1,0:T(4,128)(2,1)S(1)}, u32[]{:S(2)}, u32[]{:S(2)}) collective-permute-start(bf16[64,4,8]{2,1,0:T(4,128)(2,1)S(1)} %get-tuple-element.7), channel_id=1, source_target_pairs={{0,1},{1,2},{2,3},{3,4},{4,5},{5,6},{6,7},{8,9},{9,10},{10,11},{11... | collective-permute-start | bytes 12296 | tf_op jit(solution)/shard_map/ppermute | solution.py:17
  16.6 0.9 select_reduce_fusion.1
  17.4 1.2 convolution_bitcast_fusion.1
  18.6 0.7 compare_convert_fusion
  19.3 0.7 compare_convert_fusion.1
  19.9 0.8 convert_multiply_fusion.17
  20.8 0.9 convert_multiply_fusion.18
  21.7 1.0 constant_dynamic-update-slice_fusion.1
  22.6 0.0 collective-permute-done.1
  22.7 83.3 %all-gather.2.cloned.1.call-done = bf16[64,256,256]{2,0,1:T(8,128)(2,1)} async-done(((bf16[64,4,256]{2,0,1:T(8,128)(2,1)}), bf16[64,256,256]{2,0,1:T(8,128)(2,1)}) %all-gather.2.cloned.1.call-update) | async-done | bytes 8388624 | tf_op jit(solution)/shard_map/all_gather | solution.py:46
  106.0 0.0 copy-start
  106.0 8.4 %fusion.4 = bf16[32,64,256]{2,0,1:T(8,128)(2,1)S(1)} fusion(bf16[64,256,256]{2,0,1:T(8,128)(2,1)} %all-gather.2.cloned.1.call-done, s32[32]{0:T(128)S(1)} %get-tuple-element.3), kind=kOutput, calls=%fused_computation.5 | convolution fusion | flops 268967936 | bytes 9437312 | tf_op jit(solution)/shard_map/pc,kcr->pkr/dot_general | solution.py:50
  114.4 0.0 copy-done
  114.4 0.0 copy-start.1
  114.4 0.0 copy-start.3
  114.4 1.3 convolution_multiply_fusion
  115.7 0.0 collective-permute-done
  115.7 0.0 copy-done.1
  115.8 0.0 copy-done.3
  115.8 4.2 %add_convert_fusion = bf16[64,4,256]{2,1,0:T(4,128)(2,1)S(1)} fusion(bf16[64,4,256]{2,1,0:T(4,128)(2,1)S(1)} %copy-done.1, bf16[64,4,8]{2,1,0:T(4,128)(2,1)S(1)} %collective-permute-done, bf16[64,4,264]{2,1,0:T(4,128)(2,1)S(1)} %constant_dynamic-update-slice_fusion, f32[4,256]{1,0:T(4,128)S(1)} %get-tuple-element.9, f32[4,256]{1,0:T(4,128)S(1)} %get-tuple-element.11, ...), kind=kOutput, calls=%fused_computation.33 | convolution fusion | flops 30277760 | bytes 3481744 | tf_op jit(solution)/shard_map/pc,pkr->kcr/dot_general | solution.py:66
  119.9 0.2 convolution_bitcast_fusion
  120.1 98.1 %all-reduce = (f32[64,64]{0,1:T(8,128)S(1)}, f32[64,64]{0,1:T(8,128)S(1)}) all-reduce(f32[64,64]{0,1:T(8,128)S(1)} %convolution_bitcast_fusion, f32[64,64]{0,1:T(8,128)S(1)} %convolution_bitcast_fusion.1), channel_id=1, replica_groups=mesh['chan'=64,'rad'=8] {'chan','rad'}, use_global_device_ids=true, to_apply=%region_5.6 | all-reduce | flops 8192 | bytes 65536 | tf_op jit(solution)/shard_map/psum | solution.py:71
  218.3 0.1 copy.33
  218.3 5.8 %cholesky.16 = f32[64,64]{1,0:T(8,128)S(1)} custom-call(f32[64,64]{1,0:T(8,128)S(1)} %fusion.37), custom_call_target="Cholesky" | custom-call | tf_op jit(solution)/shard_map/jit(cholesky)/cholesky | solution.py:72
  224.2 0.6 compare_reduce_fusion
  224.9 0.7 fusion.32
  225.5 4.9 %custom-call.8 = f32[1,64,64]{1,2,0:T(8,128)S(1)} custom-call(f32[1,64,64]{2,1,0:T(8,128)S(1)} %fusion.32), custom_call_target="InvertDiagBlocksLowerTriangular" | custom-call | tf_op jit(solution)/shard_map/triangular_solve | solution.py:74
  230.4 0.2 fusion.35
  230.7 0.2 fusion.33
  230.9 0.0 copy-start.2
  230.9 0.2 fusion.40
  231.1 0.9 fusion.23
  231.9 0.0 copy-done.2
  (4 shorter events, 0.1 us)
Async XLA Ops:
  7.2 98.8 %all-gather.2.cloned.1.call-start = ((), (), s32[]{:S(2)}) async-start(), calls=%async_computation | async-start | bytes 8519680 | tf_op jit(solution)/shard_map/all_gather | solution.py:46
  9.8 12.8 %collective-permute-start.1 = (bf16[64,4,8]{2,1,0:T(4,128)(2,1)S(1)}, bf16[64,4,8]{2,1,0:T(4,128)(2,1)S(1)}, u32[]{:S(2)}, u32[]{:S(2)}) collective-permute-start(bf16[64,4,8]{2,1,0:T(4,128)(2,1)S(1)} %get-tuple-element.6), channel_id=1, source_target_pairs={{1,0},{2,1},{3,2},{4,3},{5,4},{6,5},{7,6},{9,8},{10,9},{11,10},{12... | collective-permute-start | bytes 12296 | tf_op jit(solution)/shard_map/ppermute | solution.py:18
  11.1 104.6 %collective-permute-start = (bf16[64,4,8]{2,1,0:T(4,128)(2,1)S(1)}, bf16[64,4,8]{2,1,0:T(4,128)(2,1)S(1)}, u32[]{:S(2)}, u32[]{:S(2)}) collective-permute-start(bf16[64,4,8]{2,1,0:T(4,128)(2,1)S(1)} %get-tuple-element.7), channel_id=1, source_target_pairs={{0,1},{1,2},{2,3},{3,4},{4,5},{5,6},{6,7},{8,9},{9,10},{10,11},{11... | collective-permute-start | bytes 12296 | tf_op jit(solution)/shard_map/ppermute | solution.py:17
  106.0 8.4 %copy-start = (bf16[32,256,256]{2,1,0:T(8,128)(2,1)S(1)}, bf16[32,256,256]{2,1,0:T(8,128)(2,1)}, u32[]{:S(2)}) copy-start(bf16[32,256,256]{2,1,0:T(8,128)(2,1)} %param.13) | copy-start | bytes 12582916
  114.4 1.4 copy-start.1
  114.4 1.4 copy-start.3
  230.9 1.1 copy-start.2
Sparse Core Ops, SparseCore 0:
  11.9 94.0 all-gather.1
where the time goes:
time: 239 us
  blocking collectives  98.1 us (41%)
  waiting for transfers between devices  83.3 us (35%)
  other arithmetic  16.9 us (7%)
  matrix products  15.8 us (7%)
  between operations  14.2 us (6%)
  starting transfers between devices  6.79 us (3%)
  local copies, waits for them, and re-layouts  3.65 us (2%)
    psum x1, blocking collectives, body(): projected = lax.psum(local_proj, ('chan', 'rad'))  98.1 us
    all_gather x1, waiting for transfers between devices, body(): shard_rows = lax.all_gather(trial, 'chan', axis=1, tiled=True)  83.3 us
    dot_general x1, matrix products, body(): jnp.einsum('pc,kcr->pkr', picker, shard_rows, preferred_element_type=jnp....  8.38 us
    another operation x3, other arithmetic, body(): factor = jnp.linalg.cholesky(correlation)  6.52 us
    another operation x2, other arithmetic, body(): lax.linalg.triangular_solve(factor, halfway, left_side=True, lower=True,...  5.55 us
    ppermute x1, starting transfers between devices, padded_2(): before = lax.ppermute(last, axis, up)  5.46 us
  transfers between devices with their start and end apart: 3, of which 1 were waited for; matrix products, arithmetic and copies ran while one was open for 7% of the time, Pallas kernels for 0%

commit v1 on v0

v1 whole, which is shorter than its diff:
```python
import functools

import jax
import jax.numpy as jnp
from jax import lax
from jax.experimental import pallas as pl
from jax.experimental.pallas import tpu as pltpu
from jax.sharding import Mesh, PartitionSpec as P

BW = 8
BLK = 256
CORES = 2
X_CHIPS = 4
VMEM = pl.BlockSpec(memory_space=pltpu.VMEM)
SMEM = pl.BlockSpec(memory_space=pltpu.SMEM)
NT = (((1,), (1,)), ((), ()))
HIGH = lax.Precision.HIGHEST
PARAMS = pltpu.CompilerParams(vmem_limit_bytes=40 * 1024 * 1024)


def pick_kernel(per_group, want, rows, out):
    @pl.loop(0, out.shape[0])
    def _(i):
        group = lax.rem(i, rows.shape[0] // per_group)
        out[i] = rows[group * per_group + want[i]]


def image_kernel(slot, target, live, rows, coupling, banded, trial, image, proj, total):
    total[...] = banded[...]

    @pl.loop(0, coupling.shape[0])
    def _(p):
        part = lax.dot_general(
            rows[slot[p]], coupling[p], NT, preferred_element_type=jnp.float32
        )
        total[target[p]] += part * live[p]

    acc = jnp.zeros(proj.shape, jnp.float32)
    for c in range(total.shape[0]):
        rounded = total[c].astype(jnp.bfloat16)
        image[c] = rounded
        acc += lax.dot_general(trial[c], rounded, NT, preferred_element_type=jnp.float32)
    proj[...] = acc


def residual_kernel(inverse, projected, trial, image, residual, rayleigh):
    inv = inverse[...]
    half = jnp.dot(inv, projected[...], precision=HIGH, preferred_element_type=jnp.float32)
    full = lax.dot_general(
        inv, half, (((0,), (0,)), ((), ())), precision=HIGH, preferred_element_type=jnp.float32
    )
    rayleigh[...] = full
    flipped = full.T.astype(jnp.bfloat16)
    for c in range(trial.shape[0]):
        fit = jnp.dot(flipped, trial[c], preferred_element_type=jnp.float32)
        residual[c] = (image[c].astype(jnp.float32) - fit).astype(jnp.bfloat16)


def total_of(part):
    size = part.shape[0]
    inner = lax.axis_size("x") * lax.axis_size("core")
    outer = lax.axis_size("y") * lax.axis_size("rad")
    pieces = part.reshape(inner, size // inner, size)
    mine = jnp.sum(lax.all_to_all(pieces, ("x", "core"), 0, 0, tiled=True), axis=0)
    spread = jnp.broadcast_to(mine[None], (outer,) + mine.shape)
    mine = jnp.sum(lax.all_to_all(spread, ("y", "rad"), 0, 0, tiled=True), axis=0)
    spread = jnp.broadcast_to(mine[None], (inner,) + mine.shape)
    return lax.all_to_all(spread, ("x", "core"), 0, 0, tiled=True).reshape(size, size)


def lookup(table, wanted_ids):
    match = wanted_ids[:, None] == jnp.arange(table.shape[0], dtype=jnp.int32)[None, :]
    return jnp.sum(jnp.where(match, table[None, :], 0), axis=1)


def body(trial, band, band_width, energies, coupling, reach, pair_target, pair_source, chan_slot):
    vecs, slots, slab = trial.shape
    ys, xs, cores, slabs = (lax.axis_size(a) for a in ("y", "x", "core", "rad"))
    me = (lax.axis_index("y") * xs + lax.axis_index("x")) * cores + lax.axis_index("core")
    columns = xs * cores

    source_slot = lookup(chan_slot, pair_source)
    target_local = lookup(chan_slot, pair_target) - me * slots
    group = source_slot // slots
    member = source_slot - group * slots
    hit = group[:, None] == jnp.arange(ys * columns, dtype=jnp.int32)[None, :]
    need = jnp.sum(jnp.where(hit, member[:, None], 0), axis=0).reshape(ys, columns)
    want = lax.all_to_all(need.T, ("x", "core"), 0, 0, tiled=True).reshape(-1)
    where_held = lax.rem(group, columns) * ys + group // columns
    live = (lax.axis_index("rad") < reach).astype(jnp.float32)

    by_slot = jnp.transpose(trial, (1, 0, 2))
    column = lax.all_gather(by_slot, "y", axis=0, tiled=True)
    picked = pl.pallas_call(
        functools.partial(pick_kernel, slots),
        out_shape=jax.ShapeDtypeStruct((columns * ys, vecs, slab), jnp.bfloat16),
        in_specs=[SMEM, VMEM],
        out_specs=VMEM,
        compiler_params=PARAMS,
        name="pick",
    )(want, column)
    rows = lax.all_to_all(picked, ("x", "core"), 0, 0, tiled=True)

    gram = total_of(
        lax.dot_general(
            trial, trial, (((1, 2), (1, 2)), ((), ())), preferred_element_type=jnp.float32
        )
    )
    factor = jnp.linalg.cholesky(gram)
    inverse = lax.linalg.triangular_solve(
        factor, jnp.eye(vecs, dtype=jnp.float32), left_side=True, lower=True
    )

    up = [(i, i + 1) for i in range(slabs - 1)]
    before = lax.ppermute(by_slot[:, :, slab - BW :], "rad", up)
    after = lax.ppermute(by_slot[:, :, :BW], "rad", [(j, i) for i, j in up])
    padded = jnp.concatenate([before, by_slot, after], axis=2)
    banded = energies[:, None, None] * by_slot.astype(jnp.float32)
    for offset in range(2 * BW + 1):
        inside = (abs(offset - BW) <= band_width).astype(jnp.float32)
        weight = inside[:, None] * band[:, offset, :].astype(jnp.float32)
        banded += weight[:, None] * padded[:, :, offset : offset + slab].astype(jnp.float32)

    image, part = pl.pallas_call(
        image_kernel,
        out_shape=(
            jax.ShapeDtypeStruct(by_slot.shape, jnp.bfloat16),
            jax.ShapeDtypeStruct((vecs, vecs), jnp.float32),
        ),
        in_specs=[SMEM, SMEM, SMEM, VMEM, VMEM, VMEM, VMEM],
        out_specs=(VMEM, VMEM),
        scratch_shapes=[pltpu.VMEM(by_slot.shape, jnp.float32)],
        compiler_params=PARAMS,
        name="image",
    )(where_held, target_local, live, rows, coupling, banded, by_slot)
    projected = total_of(part)
    residual, rayleigh = pl.pallas_call(
        residual_kernel,
        out_shape=(
            jax.ShapeDtypeStruct(by_slot.shape, jnp.bfloat16),
            jax.ShapeDtypeStruct((vecs, vecs), jnp.float32),
        ),
        in_specs=[VMEM] * 4,
        out_specs=(VMEM, VMEM),
        compiler_params=PARAMS,
        name="residual",
    )(inverse, projected, by_slot, image)
    return jnp.transpose(residual, (1, 0, 2)), rayleigh


def solution(mesh):
    chan, rad = mesh.shape["chan"], mesh.shape["rad"]
    fine = Mesh(
        mesh.devices.reshape(chan // (X_CHIPS * CORES), X_CHIPS, CORES, rad),
        ("y", "x", "core", "rad"),
    )
    over = ("y", "x", "core")
    placed = (
        P(None, over, "rad"),
        P(over, None, "rad"),
        P(over),
        P(over),
        P(over, "rad", None),
        P(over),
        P(over),
        P(over),
        P(),
    )
    return jax.shard_map(
        body, mesh=fine, in_specs=placed, out_specs=(P(None, over, "rad"), P()), check_vma=False
    )
```

time: 239 us -> 161 us (0.67)
  blocking collectives: 98.1 us -> 0 us
  starting transfers between devices: 6.79 us -> 56.5 us
  waiting for transfers between devices: 83.3 us -> 44.8 us
  matrix products: 15.8 us -> 1.36 us
  local copies, waits for them, and re-layouts: 3.65 us -> 14.2 us
  Pallas kernels: 0 us -> 8.8 us
  other arithmetic: 16.9 us -> 19.9 us
    psum x1 -> x0, blocking collectives: 98.1 us -> none  [body(): projected = lax.psum(local_proj, ('chan', 'rad'))]
    all_gather x1, waiting for transfers between devices: 83.3 us -> 0.01 us  [body(): column = lax.all_gather(by_slot, 'y', axis=0, tiled=True)]
    all_to_all x0 -> x8, starting transfers between devices: none -> 51.2 us  [the longest x2 16.6 us: total_of(): lax.all_to_all(spread, ('y', 'rad'), 0, 0, tiled=True)]
    all_to_all x0 -> x8, waiting for transfers between devices: none -> 43.7 us  [the longest x2 16.3 us: total_of(): lax.all_to_all(spread, ('y', 'rad'), 0, 0, tiled=True)]
    dot_general x6 -> x1, matrix products: 15.4 us -> 1.15 us  [body(): lax.dot_general(trial, trial, (((1, 2), (1, 2)), ((), ())), preferred_ele...]
    unnamed x10 -> x30, local copies, waits for them, and re-layouts: 2.55 us -> 12.1 us
    pallas_call x0 -> x3, Pallas kernels: none -> 8.8 us  [the longest x1 6.8 us: body(): pl.pallas_call(image_kernel, out_shape=(jax.ShapeDtypeStruct(by_slot.shap...]
    all_to_all x0 -> x7, other arithmetic: none -> 5.49 us  [the longest x2 1.97 us: total_of(): lax.all_to_all(spread, ('y', 'rad'), 0, 0, tiled=True)]
  transfers between devices with their start and end apart: 3 -> 11, of which waited for: 1 -> 9; matrix products, arithmetic and copies ran while one was open for 7% -> 15% of each run, Pallas kernels for 0% -> 1%
where the time goes in v1:
time: 161 us; the launch traced here: 160 us
  starting transfers between devices  56.5 us (35%)
  waiting for transfers between devices  44.8 us (28%)
  other arithmetic  19.9 us (12%)
  between operations  14.3 us (9%)
  local copies, waits for them, and re-layouts  14.2 us (9%)
  Pallas kernels  8.8 us (5%)
    all_to_all x2, starting transfers between devices, total_of(): lax.all_to_all(spread, ('y', 'rad'), 0, 0, tiled=True)  16.6 us
    all_to_all x2, waiting for transfers between devices, total_of(): lax.all_to_all(spread, ('y', 'rad'), 0, 0, tiled=True)  16.3 us
    all_to_all x2, starting transfers between devices, total_of(): lax.all_to_all(pieces, ('x', 'core'), 0, 0, tiled=True)  14.2 us
    unnamed x30, local copies, waits for them, and re-layouts  12.1 us
    all_to_all x1, waiting for transfers between devices, body(): rows = lax.all_to_all(picked, ('x', 'core'), 0, 0, tiled=True)  11.8 us
    all_to_all x2, starting transfers between devices, total_of(): lax.all_to_all(spread, ('x', 'core'), 0, 0, tiled=True).reshape(size, size)  9.26 us
    all_to_all x2, waiting for transfers between devices, total_of(): lax.all_to_all(pieces, ('x', 'core'), 0, 0, tiled=True)  8.45 us
    pallas_call x1, Pallas kernels, body(): pl.pallas_call(image_kernel, out_shape=(jax.ShapeDtypeStruct(by_slot.shap...  6.8 us
  transfers between devices with their start and end apart: 11, of which 9 were waited for; matrix products, arithmetic and copies ran while one was open for 15% of the time, Pallas kernels for 1%

profile of v1, /device:TPU:1, one launch (start us, length us, event | category | flops | bytes accessed | tf_op | source)
XLA Modules:
  0.0 159.9 jit_solution(696312992867855894)
XLA Ops:
  7.2 1.6 copy.42
  8.8 1.2 convolution_bitcast_fusion
  10.0 0.7 reshape.165
  10.7 10.1 %all-to-all-start = ((f32[8,1,512]{2,1,0:T(1,128)}), f32[8,1,512]{2,1,0:T(1,128)S(1)}, u32[]{:S(2)}, u32[]{:S(2)}) async-start(f32[8,1,512]{2,1,0:T(1,128)} %reshape.165), calls=%async_computation | async-start | bytes 32768 | tf_op jit(solution)/shard_map/all_to_all | solution.py:64
  20.8 0.9 select_reduce_fusion
  21.6 3.8 %all-to-all-done = f32[8,1,512]{2,1,0:T(1,128)S(1)} async-done(((f32[8,1,512]{2,1,0:T(1,128)}), f32[8,1,512]{2,1,0:T(1,128)S(1)}, u32[]{:S(2)}, u32[]{:S(2)}) %all-to-all-start) | async-done | bytes 16416 | tf_op jit(solution)/shard_map/all_to_all | solution.py:64
  25.4 0.6 broadcast.230
  26.0 0.7 reduce.10
  26.7 0.1 reshape.166
  26.9 0.8 reshape.167
  27.7 12.0 %all-to-all-start.1 = ((f32[64,1,512]{2,1,0:T(1,128)}), f32[64,1,512]{2,1,0:T(1,128)S(1)}, u32[]{:S(2)}, u32[]{:S(2)}) async-start(f32[64,1,512]{2,1,0:T(1,128)} %reshape.167), calls=%async_computation.1 | async-start | bytes 262144 | tf_op jit(solution)/shard_map/all_to_all | solution.py:66
  39.7 0.1 select_reduce_fusion.3
  39.8 0.1 reshape.151
  39.9 0.7 copy.34
  40.5 10.8 %all-to-all-done.1 = f32[64,1,512]{2,1,0:T(1,128)S(1)} async-done(((f32[64,1,512]{2,1,0:T(1,128)}), f32[64,1,512]{2,1,0:T(1,128)S(1)}, u32[]{:S(2)}, u32[]{:S(2)}) %all-to-all-start.1) | async-done | bytes 131104 | tf_op jit(solution)/shard_map/all_to_all | solution.py:66
  51.4 6.1 %all-to-all-start.3 = ((s32[8,1,8]{2,1,0:T(1,128)}), s32[8,1,8]{2,1,0:T(1,128)S(1)}, u32[]{:S(2)}, u32[]{:S(2)}) async-start(s32[8,1,8]{2,1,0:T(1,128)} %copy.34), calls=%async_computation.3 | async-start | bytes 8192 | tf_op jit(solution)/shard_map/all_to_all | solution.py:88
  57.5 1.0 reduce.11
  58.5 0.1 reshape.168
  58.7 0.7 reshape.169
  59.4 2.7 %all-to-all-done.3 = s32[8,1,8]{2,1,0:T(1,128)S(1)} async-done(((s32[8,1,8]{2,1,0:T(1,128)}), s32[8,1,8]{2,1,0:T(1,128)S(1)}, u32[]{:S(2)}, u32[]{:S(2)}) %all-to-all-start.3) | async-done | bytes 288 | tf_op jit(solution)/shard_map/all_to_all | solution.py:88
  62.1 3.9 %all-to-all-start.2 = ((f32[8,1,512]{2,1,0:T(1,128)}), f32[8,1,512]{2,1,0:T(1,128)S(1)}, u32[]{:S(2)}, u32[]{:S(2)}) async-start(f32[8,1,512]{2,1,0:T(1,128)} %reshape.169), calls=%async_computation.2 | async-start | bytes 32768 | tf_op jit(solution)/shard_map/all_to_all | solution.py:68
  66.0 0.5 broadcast.227
  66.6 0.7 reduce.9
  67.2 0.1 reshape.152.want
  67.3 1.2 copy-done.3
  68.5 1.0 pick.1
  69.6 1.3 copy-done
  71.0 5.0 %all-to-all-start.4 = ((bf16[64,64,256]{2,1,0:T(8,128)(2,1)}), bf16[64,64,256]{2,1,0:T(8,128)(2,1)S(1)}, u32[]{:S(2)}, u32[]{:S(2)}) async-start(bf16[64,64,256]{2,1,0:T(8,128)(2,1)} %copy-done), calls=%async_computation.4 | async-start | bytes 4194304 | tf_op jit(solution)/shard_map/all_to_all | solution.py:102
  75.9 0.1 fusion.36
  76.0 1.3 collective-permute-start.1
  77.3 4.0 %collective-permute-start = (bf16[4,64,8]{2,1,0:T(8,128)(2,1)S(1)}, bf16[4,64,8]{2,1,0:T(8,128)(2,1)S(1)}, u32[]{:S(2)}, u32[]{:S(2)}) collective-permute-start(bf16[4,64,8]{2,1,0:T(8,128)(2,1)S(1)} %get-tuple-element.22), channel_id=1, source_target_pairs={{0,1},{1,2},{2,3},{3,4},{4,5},{5,6},{6,7},{8,9},{9,10},{10,11},{11... | collective-permute-start | bytes 12296 | tf_op jit(solution)/shard_map/ppermute | solution.py:115
  81.4 0.1 multiply_bitcast_fusion.15
  81.5 0.1 multiply_bitcast_fusion.16
  81.6 0.1 collective-permute-done.1
  81.6 1.0 collective-permute-done
  82.6 1.0 fusion.16.banded
  83.7 0.7 reduce.12
  84.4 0.1 reshape.170
  84.5 0.1 copy.32
  84.6 5.8 %cholesky.17 = f32[64,64]{1,0:T(8,128)S(1)} custom-call(f32[64,64]{1,0:T(8,128)S(1)} %fusion.35), custom_call_target="Cholesky" | custom-call | tf_op jit(solution)/shard_map/jit(cholesky)/cholesky | solution.py:109
  90.4 11.8 %all-to-all-done.4.rows = bf16[64,64,256]{2,1,0:T(8,128)(2,1)S(1)} async-done(((bf16[64,64,256]{2,1,0:T(8,128)(2,1)}), bf16[64,64,256]{2,1,0:T(8,128)(2,1)S(1)}, u32[]{:S(2)}, u32[]{:S(2)}) %all-to-all-start.4) | async-done | bytes 2097184 | tf_op jit(solution)/shard_map/all_to_all | solution.py:102
  102.3 2.2 %copy-done.2 = bf16[32,256,256]{2,1,0:T(8,128)(2,1)S(1)} copy-done((bf16[32,256,256]{2,1,0:T(8,128)(2,1)S(1)}, bf16[32,256,256]{2,1,0:T(8,128)(2,1)}, u32[]{:S(2)}) %copy-start.2) | copy-done | bytes 4194328
  104.5 6.8 %image.1 = (bf16[4,64,256]{2,1,0:T(8,128)(2,1)S(1)}, f32[64,64]{1,0:T(8,128)S(1)}) custom-call(s32[32]{0:T(128)S(1)} %get-tuple-element.62.slot, s32[32]{0:T(128)S(1)} %get-tuple-element.63.target, f32[32]{0:T(128)S(1)} %compare_convert_fusion.9.live, bf16[64,64,256]{2,1,0:T(8,128)(2,1)S(1)} %all-to-all-done.4.rows, bf16[32,256,256]{2,1,0:T(8,128)(2,1)S(1)} %copy-done.2, ...), custom_call_target="tpu_custom_call" | custom-call | tf_op jit(solution)/shard_map/image/pallas_call | solution.py:124
  111.3 0.7 reshape.171
  112.0 4.1 %all-to-all-start.5 = ((f32[8,1,512]{2,1,0:T(1,128)}), f32[8,1,512]{2,1,0:T(1,128)S(1)}, u32[]{:S(2)}, u32[]{:S(2)}) async-start(f32[8,1,512]{2,1,0:T(1,128)} %reshape.171), calls=%async_computation.5 | async-start | bytes 32768 | tf_op jit(solution)/shard_map/all_to_all | solution.py:64
  116.1 4.6 %all-to-all-done.5 = f32[8,1,512]{2,1,0:T(1,128)S(1)} async-done(((f32[8,1,512]{2,1,0:T(1,128)}), f32[8,1,512]{2,1,0:T(1,128)S(1)}, u32[]{:S(2)}, u32[]{:S(2)}) %all-to-all-start.5) | async-done | bytes 16416 | tf_op jit(solution)/shard_map/all_to_all | solution.py:64
  120.7 0.7 reduce.13
  121.5 0.1 reshape.172
  121.6 0.8 reshape.173
  122.4 4.6 %all-to-all-start.6 = ((f32[64,1,512]{2,1,0:T(1,128)}), f32[64,1,512]{2,1,0:T(1,128)S(1)}, u32[]{:S(2)}, u32[]{:S(2)}) async-start(f32[64,1,512]{2,1,0:T(1,128)} %reshape.173), calls=%async_computation.6 | async-start | bytes 262144 | tf_op jit(solution)/shard_map/all_to_all | solution.py:66
  127.1 0.6 compare_reduce_fusion
  127.7 0.7 fusion.32
  128.3 4.9 %custom-call.6 = f32[1,64,64]{1,2,0:T(8,128)S(1)} custom-call(f32[1,64,64]{2,1,0:T(8,128)S(1)} %fusion.32), custom_call_target="InvertDiagBlocksLowerTriangular" | custom-call | tf_op jit(solution)/shard_map/triangular_solve | solution.py:110
  133.2 5.4 %all-to-all-done.6 = f32[64,1,512]{2,1,0:T(1,128)S(1)} async-done(((f32[64,1,512]{2,1,0:T(1,128)}), f32[64,1,512]{2,1,0:T(1,128)S(1)}, u32[]{:S(2)}, u32[]{:S(2)}) %all-to-all-start.6) | async-done | bytes 131104 | tf_op jit(solution)/shard_map/all_to_all | solution.py:66
  138.7 1.0 reduce.14
  139.7 0.1 reshape.174
  139.8 0.7 reshape.175
  140.5 5.3 %all-to-all-start.7 = ((f32[8,1,512]{2,1,0:T(1,128)}), f32[8,1,512]{2,1,0:T(1,128)S(1)}, u32[]{:S(2)}, u32[]{:S(2)}) async-start(f32[8,1,512]{2,1,0:T(1,128)} %reshape.175), calls=%async_computation.7 | async-start | bytes 32768 | tf_op jit(solution)/shard_map/all_to_all | solution.py:68
  145.9 0.2 fusion.33.inverse
  146.1 4.5 %all-to-all-done.7 = f32[8,1,512]{2,1,0:T(1,128)S(1)} async-done(((f32[8,1,512]{2,1,0:T(1,128)}), f32[8,1,512]{2,1,0:T(1,128)S(1)}, u32[]{:S(2)}, u32[]{:S(2)}) %all-to-all-start.7) | async-done | bytes 16416 | tf_op jit(solution)/shard_map/all_to_all | solution.py:68
  150.5 0.7 reduce.15
  151.3 0.1 reshape.176
  151.3 1.0 residual.1
  152.3 0.8 copy.36
  (31 shorter events, 0.4 us)
Async XLA Ops:
  7.2 60.1 %all-gather.2.cloned.1.call-start = ((), (), s32[]{:S(2)}) async-start(), calls=%async_computation.8 | async-start | bytes 1179648 | tf_op jit(solution)/shard_map/all_gather | solution.py:93
  10.7 14.8 %all-to-all-start = ((f32[8,1,512]{2,1,0:T(1,128)}), f32[8,1,512]{2,1,0:T(1,128)S(1)}, u32[]{:S(2)}, u32[]{:S(2)}) async-start(f32[8,1,512]{2,1,0:T(1,128)} %reshape.165), calls=%async_computation | async-start | bytes 32768 | tf_op jit(solution)/shard_map/all_to_all | solution.py:64
  27.7 23.7 %all-to-all-start.1 = ((f32[64,1,512]{2,1,0:T(1,128)}), f32[64,1,512]{2,1,0:T(1,128)S(1)}, u32[]{:S(2)}, u32[]{:S(2)}) async-start(f32[64,1,512]{2,1,0:T(1,128)} %reshape.167), calls=%async_computation.1 | async-start | bytes 262144 | tf_op jit(solution)/shard_map/all_to_all | solution.py:66
  51.4 10.7 %all-to-all-start.3 = ((s32[8,1,8]{2,1,0:T(1,128)}), s32[8,1,8]{2,1,0:T(1,128)S(1)}, u32[]{:S(2)}, u32[]{:S(2)}) async-start(s32[8,1,8]{2,1,0:T(1,128)} %copy.34), calls=%async_computation.3 | async-start | bytes 8192 | tf_op jit(solution)/shard_map/all_to_all | solution.py:88
  62.1 8.9 %all-to-all-start.2 = ((f32[8,1,512]{2,1,0:T(1,128)}), f32[8,1,512]{2,1,0:T(1,128)S(1)}, u32[]{:S(2)}, u32[]{:S(2)}) async-start(f32[8,1,512]{2,1,0:T(1,128)} %reshape.169), calls=%async_computation.2 | async-start | bytes 32768 | tf_op jit(solution)/shard_map/all_to_all | solution.py:68
  67.3 1.2 copy-start.3
  69.6 1.4 copy-start
  70.9 5.0 %copy-start.1 = (bf16[64,4,256]{2,0,1:T(8,128)(2,1)S(1)}, bf16[64,4,256]{2,0,1:T(8,128)(2,1)}, u32[]{:S(2)}) copy-start(bf16[64,4,256]{2,0,1:T(8,128)(2,1)} %copy.42) | copy-start | bytes 393220
  70.9 10.4 %copy-start.5 = (s32[4]{0:T(128)S(1)}, s32[4]{0:T(128)}, u32[]{:S(2)}) copy-start(s32[4]{0:T(128)} %param.11) | copy-start | bytes 52
  70.9 10.4 %copy-start.4 = (bf16[4,17,256]{2,0,1:T(4,128)(2,1)S(1)}, bf16[4,17,256]{2,0,1:T(4,128)(2,1)}, u32[]{:S(2)}) copy-start(bf16[4,17,256]{2,0,1:T(4,128)(2,1)} %param.10) | copy-start | bytes 104452
  70.9 10.6 %copy-start.7 = (s32[32]{0:T(128)S(1)}, s32[32]{0:T(128)}, u32[]{:S(2)}) copy-start(s32[32]{0:T(128)} %param.14) | copy-start | bytes 388
  71.0 11.7 %copy-start.6 = (f32[4]{0:T(128)S(1)}, f32[4]{0:T(128)}, u32[]{:S(2)}) copy-start(f32[4]{0:T(128)} %param.12) | copy-start | bytes 52
  71.0 31.3 %all-to-all-start.4 = ((bf16[64,64,256]{2,1,0:T(8,128)(2,1)}), bf16[64,64,256]{2,1,0:T(8,128)(2,1)S(1)}, u32[]{:S(2)}, u32[]{:S(2)}) async-start(bf16[64,64,256]{2,1,0:T(8,128)(2,1)} %copy-done), calls=%async_computation.4 | async-start | bytes 4194304 | tf_op jit(solution)/shard_map/all_to_all | solution.py:102
  76.0 5.6 %collective-permute-start.1 = (bf16[4,64,8]{2,1,0:T(8,128)(2,1)S(1)}, bf16[4,64,8]{2,1,0:T(8,128)(2,1)S(1)}, u32[]{:S(2)}, u32[]{:S(2)}) collective-permute-start(bf16[4,64,8]{2,1,0:T(8,128)(2,1)S(1)} %get-tuple-element.23), channel_id=1, source_target_pairs={{1,0},{2,1},{3,2},{4,3},{5,4},{6,5},{7,6},{9,8},{10,9},{11,10},{12... | collective-permute-start | bytes 12296 | tf_op jit(solution)/shard_map/ppermute | solution.py:116
  77.3 5.3 %collective-permute-start = (bf16[4,64,8]{2,1,0:T(8,128)(2,1)S(1)}, bf16[4,64,8]{2,1,0:T(8,128)(2,1)S(1)}, u32[]{:S(2)}, u32[]{:S(2)}) collective-permute-start(bf16[4,64,8]{2,1,0:T(8,128)(2,1)S(1)} %get-tuple-element.22), channel_id=1, source_target_pairs={{0,1},{1,2},{2,3},{3,4},{4,5},{5,6},{6,7},{8,9},{9,10},{10,11},{11... | collective-permute-start | bytes 12296 | tf_op jit(solution)/shard_map/ppermute | solution.py:115
  102.3 2.2 %copy-start.2 = (bf16[32,256,256]{2,1,0:T(8,128)(2,1)S(1)}, bf16[32,256,256]{2,1,0:T(8,128)(2,1)}, u32[]{:S(2)}) copy-start(bf16[32,256,256]{2,1,0:T(8,128)(2,1)} %coupling.1) | copy-start | bytes 12582916
  112.0 8.8 %all-to-all-start.5 = ((f32[8,1,512]{2,1,0:T(1,128)}), f32[8,1,512]{2,1,0:T(1,128)S(1)}, u32[]{:S(2)}, u32[]{:S(2)}) async-start(f32[8,1,512]{2,1,0:T(1,128)} %reshape.171), calls=%async_computation.5 | async-start | bytes 32768 | tf_op jit(solution)/shard_map/all_to_all | solution.py:64
  122.4 16.2 %all-to-all-start.6 = ((f32[64,1,512]{2,1,0:T(1,128)}), f32[64,1,512]{2,1,0:T(1,128)S(1)}, u32[]{:S(2)}, u32[]{:S(2)}) async-start(f32[64,1,512]{2,1,0:T(1,128)} %reshape.173), calls=%async_computation.6 | async-start | bytes 262144 | tf_op jit(solution)/shard_map/all_to_all | solution.py:66
  140.5 10.0 %all-to-all-start.7 = ((f32[8,1,512]{2,1,0:T(1,128)}), f32[8,1,512]{2,1,0:T(1,128)S(1)}, u32[]{:S(2)}, u32[]{:S(2)}) async-start(f32[8,1,512]{2,1,0:T(1,128)} %reshape.175), calls=%async_computation.7 | async-start | bytes 32768 | tf_op jit(solution)/shard_map/all_to_all | solution.py:68
Sparse Core Ops, SparseCore 0:
  10.1 43.5 all-gather.1

commit v2 on v1

v2 whole, which is shorter than its diff:
```python
import functools

import jax
import jax.numpy as jnp
from jax import lax
from jax.experimental import pallas as pl
from jax.experimental.pallas import tpu as pltpu
from jax.sharding import Mesh, PartitionSpec as P

BW = 8
BLK = 256
CORES = 2
X_CHIPS = 4
UNROLL = 8
DIRECT = 16
CHAN = ("y", "x", "core")
VMEM = pl.BlockSpec(memory_space=pltpu.VMEM)
SMEM = pl.BlockSpec(memory_space=pltpu.SMEM)
NT = (((1,), (1,)), ((), ()))
HIGH = lax.Precision.HIGHEST
PARAMS = pltpu.CompilerParams(vmem_limit_bytes=40 * 1024 * 1024)


def pick_kernel(per_group, want, rows, out):
    @pl.loop(0, out.shape[0])
    def _(i):
        group = lax.rem(i, rows.shape[0] // per_group)
        out[i] = rows[group * per_group + want[i]]


def pack(square):
    half = square.shape[0] // 2
    return jnp.concatenate([square[:half], square[half:]], axis=1)


def unpack(packed):
    half = packed.shape[1] // 2
    return jnp.concatenate([packed[:, :half], packed[:, half:]], axis=0)


def gram_kernel(trial, gram):
    acc = jnp.zeros((trial.shape[1], trial.shape[1]), jnp.float32)
    for c in range(trial.shape[0]):
        acc += lax.dot_general(trial[c], trial[c], NT, preferred_element_type=jnp.float32)
    gram[...] = pack(acc)


def image_kernel(
    slot, group, target, live, relayed, direct, coupling, banded, trial, image, proj, total
):
    total[...] = banded[...]

    @pl.loop(0, coupling.shape[0], step=UNROLL)
    def _(first):
        for i in range(UNROLL):
            p = first + i
            rows = jnp.concatenate([relayed[slot[p]], direct[group[p]]], axis=0)
            part = lax.dot_general(rows, coupling[p], NT, preferred_element_type=jnp.float32)
            total[target[p]] += part * live[p]

    acc = jnp.zeros((trial.shape[1], trial.shape[1]), jnp.float32)
    for c in range(total.shape[0]):
        rounded = total[c].astype(jnp.bfloat16)
        image[c] = rounded
        acc += lax.dot_general(trial[c], rounded, NT, preferred_element_type=jnp.float32)
    proj[...] = pack(acc)


def residual_kernel(inverse, projected, trial, image, residual, rayleigh):
    inv = inverse[...]
    half = jnp.dot(inv, unpack(projected[...]), precision=HIGH, preferred_element_type=jnp.float32)
    full = lax.dot_general(
        inv, half, (((0,), (0,)), ((), ())), precision=HIGH, preferred_element_type=jnp.float32
    )
    rayleigh[...] = full
    flipped = full.T.astype(jnp.bfloat16)
    for c in range(trial.shape[0]):
        fit = jnp.dot(flipped, trial[c], preferred_element_type=jnp.float32)
        residual[c] = (image[c].astype(jnp.float32) - fit).astype(jnp.bfloat16)


def scatter(packed, axes):
    count = lax.axis_size(axes)
    pieces = packed.reshape(count, packed.shape[0] // count, packed.shape[1])
    return jnp.sum(lax.all_to_all(pieces, axes, 0, 0, tiled=True), axis=0)


def exchange(piece, axes):
    spread = jnp.broadcast_to(piece[None], (lax.axis_size(axes),) + piece.shape)
    return lax.all_to_all(spread, axes, 0, 0, tiled=True)


def gather(piece, axes):
    return exchange(piece, axes).reshape(-1, piece.shape[1])


def pick(want, rows, per_group):
    return pl.pallas_call(
        functools.partial(pick_kernel, per_group),
        out_shape=jax.ShapeDtypeStruct(want.shape + rows.shape[1:], rows.dtype),
        in_specs=[SMEM, VMEM],
        out_specs=VMEM,
        compiler_params=PARAMS,
        name="pick",
    )(want, rows)


def lookup(table, wanted_ids):
    match = wanted_ids[:, None] == jnp.arange(table.shape[0], dtype=jnp.int32)[None, :]
    return jnp.sum(jnp.where(match, table[None, :], 0), axis=1)


def body(trial, band, band_width, energies, coupling, reach, pair_target, pair_source, chan_slot):
    vecs, slots, slab = trial.shape
    ys, xs, cores, slabs = (lax.axis_size(a) for a in ("y", "x", "core", "rad"))
    me = (lax.axis_index("y") * xs + lax.axis_index("x")) * cores + lax.axis_index("core")
    columns = xs * cores
    relays = vecs - DIRECT

    source_slot = lookup(chan_slot, pair_source)
    target_local = lookup(chan_slot, pair_target) - me * slots
    group = source_slot // slots
    member = source_slot - group * slots
    hit = group[:, None] == jnp.arange(ys * columns, dtype=jnp.int32)[None, :]
    need = jnp.sum(jnp.where(hit, member[:, None], 0), axis=0)
    want = lax.all_to_all(need.reshape(ys, columns).T, ("x", "core"), 0, 0, tiled=True)
    want_direct = lax.all_to_all(need[:, None], CHAN, 0, 0, tiled=True)
    slot = lax.rem(group, columns) * ys + group // columns
    live = (lax.axis_index("rad") < reach).astype(jnp.float32)

    by_slot = jnp.transpose(trial, (1, 0, 2))
    column = lax.all_gather(by_slot[:, :relays], "y", axis=0, tiled=True)
    straight = lax.all_to_all(
        pick(want_direct.reshape(-1), by_slot[:, relays:], slots), CHAN, 0, 0, tiled=True
    )
    gram = pl.pallas_call(
        gram_kernel,
        out_shape=jax.ShapeDtypeStruct((vecs // 2, 2 * vecs), jnp.float32),
        in_specs=[VMEM],
        out_specs=VMEM,
        compiler_params=PARAMS,
        name="gram",
    )(by_slot)
    piece = scatter(gram, "rad")
    piece = jnp.sum(exchange(piece, ("x", "core")), axis=0)
    picked = pick(want.reshape(-1), column, slots)
    piece, picked = lax.optimization_barrier((piece, picked))
    relayed = lax.all_to_all(picked, ("x", "core"), 0, 0, tiled=True)
    piece = jnp.sum(exchange(piece, "y"), axis=0)
    factor = jnp.linalg.cholesky(unpack(gather(piece, "rad")))
    inverse = lax.linalg.triangular_solve(
        factor, jnp.eye(vecs, dtype=jnp.float32), left_side=True, lower=True
    )

    up = [(i, i + 1) for i in range(slabs - 1)]
    before = lax.ppermute(by_slot[:, :, slab - BW :], "rad", up)
    after = lax.ppermute(by_slot[:, :, :BW], "rad", [(j, i) for i, j in up])
    padded = jnp.concatenate([before, by_slot, after], axis=2)
    banded = energies[:, None, None] * by_slot.astype(jnp.float32)
    for offset in range(2 * BW + 1):
        inside = (abs(offset - BW) <= band_width).astype(jnp.float32)
        weight = inside[:, None] * band[:, offset, :].astype(jnp.float32)
        banded += weight[:, None] * padded[:, :, offset : offset + slab].astype(jnp.float32)

    image, part = pl.pallas_call(
        image_kernel,
        out_shape=(
            jax.ShapeDtypeStruct(by_slot.shape, jnp.bfloat16),
            jax.ShapeDtypeStruct((vecs // 2, 2 * vecs), jnp.float32),
        ),
        in_specs=[SMEM] * 4 + [VMEM] * 5,
        out_specs=(VMEM, VMEM),
        scratch_shapes=[pltpu.VMEM(by_slot.shape, jnp.float32)],
        compiler_params=PARAMS,
        name="image",
    )(slot, group, target_local, live, relayed, straight, coupling, banded, by_slot)
    piece = scatter(part, ("x", "core"))
    piece = jnp.sum(exchange(piece, ("y", "rad")), axis=0)
    projected = gather(piece, ("x", "core"))
    residual, rayleigh = pl.pallas_call(
        residual_kernel,
        out_shape=(
            jax.ShapeDtypeStruct(by_slot.shape, jnp.bfloat16),
            jax.ShapeDtypeStruct((vecs, vecs), jnp.float32),
        ),
        in_specs=[VMEM] * 4,
        out_specs=(VMEM, VMEM),
        compiler_params=PARAMS,
        name="residual",
    )(inverse, projected, by_slot, image)
    return jnp.transpose(residual, (1, 0, 2)), rayleigh


def solution(mesh):
    chan, rad = mesh.shape["chan"], mesh.shape["rad"]
    fine = Mesh(
        mesh.devices.reshape(chan // (X_CHIPS * CORES), X_CHIPS, CORES, rad),
        ("y", "x", "core", "rad"),
    )
    placed = (
        P(None, CHAN, "rad"),
        P(CHAN, None, "rad"),
        P(CHAN),
        P(CHAN),
        P(CHAN, "rad", None),
        P(CHAN),
        P(CHAN),
        P(CHAN),
        P(),
    )
    return jax.shard_map(
        body, mesh=fine, in_specs=placed, out_specs=(P(None, CHAN, "rad"), P()), check_vma=False
    )
```

time: 161 us -> 199 us (1.24)
  waiting for transfers between devices: 44.8 us -> 68 us
  blocking collectives: 0 us -> 21.7 us
  starting transfers between devices: 56.5 us -> 72.6 us
  between operations: 14.3 us -> 0.84 us
  local copies, waits for them, and re-layouts: 14.2 us -> 9.46 us
  other arithmetic: 19.9 us -> 16.5 us
    all_to_all x8 -> x11, waiting for transfers between devices: 43.7 us -> 68 us  [the longest x5 19.2 us: exchange(): return lax.all_to_all(spread, axes, 0, 0, tiled=True)]
    all_gather x0 -> x1, blocking collectives: none -> 21.7 us  [body(): column = lax.all_gather(by_slot[:, :relays], 'y', axis=0, tiled=True)]
    all_to_all x8 -> x11, starting transfers between devices: 51.2 us -> 67.4 us  [the longest x5 23.6 us: exchange(): return lax.all_to_all(spread, axes, 0, 0, tiled=True)]
    unnamed x30 -> x14, local copies, waits for them, and re-layouts: 12.1 us -> 4.04 us
    pallas_call x1 -> x3, Pallas kernels: 1.05 us -> 4.89 us  [the longest x2 4.04 us: pick(): pl.pallas_call(functools.partial(pick_kernel, per_group), out_shape=jax.S...]
    all_to_all x7 -> x2, other arithmetic: 5.49 us -> 1.88 us  [the longest x1 1.22 us: body(): want_direct = lax.all_to_all(need[:, None], CHAN, 0, 0, tiled=True)]
    pallas_call x1, Pallas kernels: 6.8 us -> 3.24 us  [body(): pl.pallas_call(image_kernel, out_shape=(jax.ShapeDtypeStruct(by_slot.shap...]
    broadcast_in_dim x4 -> x5, local copies, waits for them, and re-layouts: 0.06 us -> 3.11 us  [exchange(): spread = jnp.broadcast_to(piece[None], (lax.axis_size(axes),) + piece.shape)]
  transfers between devices with their start and end apart: 11 -> 13, of which waited for: 9 -> 10; matrix products, arithmetic and copies ran while one was open for 15% -> 10% of each run, Pallas kernels for 1% -> 2%
where the time goes in v2:
time: 199 us; the launch traced here: 198 us
  starting transfers between devices  72.6 us (36%)
  waiting for transfers between devices  68 us (34%)
  blocking collectives  21.7 us (11%)
  other arithmetic  16.5 us (8%)
  local copies, waits for them, and re-layouts  9.46 us (5%)
  Pallas kernels  9.15 us (5%)
    all_to_all x5, starting transfers between devices, exchange(): return lax.all_to_all(spread, axes, 0, 0, tiled=True)  23.6 us
    all_gather x1, blocking collectives, body(): column = lax.all_gather(by_slot[:, :relays], 'y', axis=0, tiled=True)  21.7 us
    all_to_all x5, waiting for transfers between devices, exchange(): return lax.all_to_all(spread, axes, 0, 0, tiled=True)  19.2 us
    all_to_all x2, starting transfers between devices, scatter(): return jnp.sum(lax.all_to_all(pieces, axes, 0, 0, tiled=True), axis=0)  15 us
    all_to_all x1, waiting for transfers between devices, body(): relayed = lax.all_to_all(picked, ('x', 'core'), 0, 0, tiled=True)  13.2 us
    all_to_all x1, waiting for transfers between devices, body(): lax.all_to_all(pick(want_direct.reshape(-1), by_slot[:, relays:], slots),...  12.3 us
    all_to_all x1, starting transfers between devices, body(): want_direct = lax.all_to_all(need[:, None], CHAN, 0, 0, tiled=True)  11.9 us
    all_to_all x2, waiting for transfers between devices, scatter(): return jnp.sum(lax.all_to_all(pieces, axes, 0, 0, tiled=True), axis=0)  9.52 us
  transfers between devices with their start and end apart: 13, of which 10 were waited for; matrix products, arithmetic and copies ran while one was open for 10% of the time, Pallas kernels for 2%

profile of v2, /device:TPU:1, one launch (start us, length us, event | category | flops | bytes accessed | tf_op | source)
XLA Modules:
  0.0 198.5 jit_solution(5662191590732238641)
XLA Ops:
  0.6 0.9 copy.64
  1.6 0.8 gram.1
  2.4 10.9 %all-to-all-start = ((f32[8,4,128]{2,1,0:T(4,128)}), f32[8,4,128]{2,1,0:T(4,128)S(1)}, u32[]{:S(2)}, u32[]{:S(2)}) async-start(f32[8,4,128]{2,1,0:T(4,128)} %bitcast.1), calls=%async_computation | async-start | bytes 32768 | tf_op jit(solution)/shard_map/all_to_all | solution.py:85
  13.3 0.9 select_reduce_fusion
  14.2 0.1 select_reduce_fusion.3
  14.3 0.1 reshape.158
  14.3 0.7 copy.48
  15.0 4.9 %all-to-all-done = f32[8,4,128]{2,1,0:T(4,128)S(1)} async-done(((f32[8,4,128]{2,1,0:T(4,128)}), f32[8,4,128]{2,1,0:T(4,128)S(1)}, u32[]{:S(2)}, u32[]{:S(2)}) %all-to-all-start) | async-done | bytes 16416 | tf_op jit(solution)/shard_map/all_to_all | solution.py:85
  19.9 6.4 %all-to-all-start.2 = ((s32[8,1,8]{2,1,0:T(1,128)}), s32[8,1,8]{2,1,0:T(1,128)S(1)}, u32[]{:S(2)}, u32[]{:S(2)}) async-start(s32[8,1,8]{2,1,0:T(1,128)} %copy.48), calls=%async_computation.2 | async-start | bytes 8192 | tf_op jit(solution)/shard_map/all_to_all | solution.py:126
  26.3 4.5 %all-to-all-done.2 = s32[8,1,8]{2,1,0:T(1,128)S(1)} async-done(((s32[8,1,8]{2,1,0:T(1,128)}), s32[8,1,8]{2,1,0:T(1,128)S(1)}, u32[]{:S(2)}, u32[]{:S(2)}) %all-to-all-start.2) | async-done | bytes 288 | tf_op jit(solution)/shard_map/all_to_all | solution.py:126
  30.8 0.6 broadcast_in_dim.40
  31.4 3.9 %all-to-all-start.1 = ((f32[8,4,128]{2,1,0:T(4,128)}), f32[8,4,128]{2,1,0:T(4,128)S(1)}, u32[]{:S(2)}, u32[]{:S(2)}) async-start(f32[8,4,128]{2,1,0:T(4,128)} %broadcast_in_dim.40), calls=%async_computation.1 | async-start | bytes 32768 | tf_op jit(solution)/shard_map/all_to_all | solution.py:90
  35.3 21.7 %all_gather.3.rows = bf16[32,48,256]{2,1,0:T(8,128)(2,1)S(1)} all-gather(bf16[4,48,256]{2,1,0:T(8,128)(2,1)S(1)} %slice.182), channel_id=1, replica_groups=mesh['y'=8,'x'=4,'core'=2,'rad'=8] {'y'}, dimensions={0}, use_global_device_ids=true | all-gather | bytes 884736 | tf_op jit(solution)/shard_map/all_gather | solution.py:132
  57.0 0.5 broadcast.229
  57.5 0.7 reduce.10
  58.2 0.1 reshape.159.want
  58.3 2.3 %pick.2 = bf16[64,48,256]{2,1,0:T(8,128)(2,1)} custom-call(s32[64]{0:T(128)S(1)} %reshape.159.want, bf16[32,48,256]{2,1,0:T(8,128)(2,1)S(1)} %all_gather.3.rows), custom_call_target="tpu_custom_call" | custom-call | tf_op jit(solution)/shard_map/pick/pallas_call | solution.py:98
  60.6 0.0 all-to-all-done.1
  60.6 0.6 broadcast_in_dim.45
  61.2 6.1 %all-to-all-start.3 = ((f32[8,4,128]{2,1,0:T(4,128)}), f32[8,4,128]{2,1,0:T(4,128)S(1)}, u32[]{:S(2)}, u32[]{:S(2)}) async-start(f32[8,4,128]{2,1,0:T(4,128)} %broadcast_in_dim.45), calls=%async_computation.3 | async-start | bytes 32768 | tf_op jit(solution)/shard_map/all_to_all | solution.py:90
  67.4 0.7 copy.53
  68.1 5.9 %all-to-all-done.3 = f32[8,4,128]{2,1,0:T(4,128)S(1)} async-done(((f32[8,4,128]{2,1,0:T(4,128)}), f32[8,4,128]{2,1,0:T(4,128)S(1)}, u32[]{:S(2)}, u32[]{:S(2)}) %all-to-all-start.3) | async-done | bytes 16416 | tf_op jit(solution)/shard_map/all_to_all | solution.py:90
  74.0 11.9 %all-to-all-start.6 = ((s32[64,1,1]{2,1,0:T(1,128)}), s32[64,1,1]{2,1,0:T(1,128)S(1)}, u32[]{:S(2)}, u32[]{:S(2)}) async-start(s32[64,1,1]{2,1,0:T(1,128)} %copy.53), calls=%async_computation.6 | async-start | bytes 65536 | tf_op jit(solution)/shard_map/all_to_all | solution.py:127
  85.9 9.3 %all-to-all-done.6 = s32[64,1,1]{2,1,0:T(1,128)S(1)} async-done(((s32[64,1,1]{2,1,0:T(1,128)}), s32[64,1,1]{2,1,0:T(1,128)S(1)}, u32[]{:S(2)}, u32[]{:S(2)}) %all-to-all-start.6) | async-done | bytes 288 | tf_op jit(solution)/shard_map/all_to_all | solution.py:127
  95.2 0.6 broadcast_in_dim.46
  95.8 3.3 %all-to-all-start.4 = ((f32[8,4,128]{2,1,0:T(4,128)}), f32[8,4,128]{2,1,0:T(4,128)S(1)}, u32[]{:S(2)}, u32[]{:S(2)}) async-start(f32[8,4,128]{2,1,0:T(4,128)} %broadcast_in_dim.46), calls=%async_computation.4 | async-start | bytes 32768 | tf_op jit(solution)/shard_map/all_to_all | solution.py:90
  99.1 1.2 reduce.7.want
  100.4 1.8 pick.3
  102.1 3.6 %all-to-all-done.4 = f32[8,4,128]{2,1,0:T(4,128)S(1)} async-done(((f32[8,4,128]{2,1,0:T(4,128)}), f32[8,4,128]{2,1,0:T(4,128)S(1)}, u32[]{:S(2)}, u32[]{:S(2)}) %all-to-all-start.4) | async-done | bytes 16416 | tf_op jit(solution)/shard_map/all_to_all | solution.py:90
  105.7 5.9 %all-to-all-start.7 = ((bf16[64,16,256]{2,1,0:T(8,128)(2,1)}), bf16[64,16,256]{2,1,0:T(8,128)(2,1)S(1)}, u32[]{:S(2)}, u32[]{:S(2)}) async-start(bf16[64,16,256]{2,1,0:T(8,128)(2,1)} %pick.3), calls=%async_computation.7 | async-start | bytes 1048576 | tf_op jit(solution)/shard_map/all_to_all | solution.py:133
  111.6 0.1 fusion.35
  111.7 1.3 collective-permute-start.1
  113.0 4.0 %collective-permute-start = (bf16[4,64,8]{2,1,0:T(8,128)(2,1)S(1)}, bf16[4,64,8]{2,1,0:T(8,128)(2,1)S(1)}, u32[]{:S(2)}, u32[]{:S(2)}) collective-permute-start(bf16[4,64,8]{2,1,0:T(8,128)(2,1)S(1)} %get-tuple-element.30), channel_id=1, source_target_pairs={{0,1},{1,2},{2,3},{3,4},{4,5},{5,6},{6,7},{8,9},{9,10},{10,11},{11... | collective-permute-start | bytes 12296 | tf_op jit(solution)/shard_map/ppermute | solution.py:156
  117.0 0.1 multiply_bitcast_fusion.15
  117.1 12.3 %all-to-all-done.7.direct = bf16[64,16,256]{2,1,0:T(8,128)(2,1)S(1)} async-done(((bf16[64,16,256]{2,1,0:T(8,128)(2,1)}), bf16[64,16,256]{2,1,0:T(8,128)(2,1)S(1)}, u32[]{:S(2)}, u32[]{:S(2)}) %all-to-all-start.7) | async-done | bytes 524320 | tf_op jit(solution)/shard_map/all_to_all | solution.py:133
  129.4 4.6 %all-to-all-start.5 = ((bf16[64,48,256]{2,1,0:T(8,128)(2,1)}), bf16[64,48,256]{2,1,0:T(8,128)(2,1)S(1)}, u32[]{:S(2)}, u32[]{:S(2)}) async-start(bf16[64,48,256]{2,1,0:T(8,128)(2,1)} %pick.2), calls=%async_computation.5 | async-start | bytes 3145728 | tf_op jit(solution)/shard_map/all_to_all | solution.py:148
  134.0 0.1 multiply_bitcast_fusion.16
  134.1 0.0 collective-permute-done.1
  134.2 1.0 fusion.16.banded
  135.2 0.1 fusion.36
  135.3 0.1 copy.62
  135.4 0.1 copy.61
  135.5 0.1 pad_maximum_fusion.2
  135.5 0.1 copy.52
  135.6 0.1 fusion.34
  135.7 5.9 %cholesky.17 = f32[64,64]{1,0:T(8,128)S(1)} custom-call(f32[64,64]{1,0:T(8,128)S(1)} %fusion.34), custom_call_target="Cholesky" | custom-call | tf_op jit(solution)/shard_map/jit(cholesky)/cholesky | solution.py:150
  141.6 13.2 %all-to-all-done.5.relayed = bf16[64,48,256]{2,1,0:T(8,128)(2,1)S(1)} async-done(((bf16[64,48,256]{2,1,0:T(8,128)(2,1)}), bf16[64,48,256]{2,1,0:T(8,128)(2,1)S(1)}, u32[]{:S(2)}, u32[]{:S(2)}) %all-to-all-start.5) | async-done | bytes 1572896 | tf_op jit(solution)/shard_map/all_to_all | solution.py:148
  154.8 2.2 %copy-done = bf16[32,256,256]{2,1,0:T(8,128)(2,1)S(1)} copy-done((bf16[32,256,256]{2,1,0:T(8,128)(2,1)S(1)}, bf16[32,256,256]{2,1,0:T(8,128)(2,1)}, u32[]{:S(2)}) %copy-start) | copy-done | bytes 4194328
  157.0 3.2 %image.1 = (bf16[4,64,256]{2,1,0:T(8,128)(2,1)S(1)}, f32[32,128]{1,0:T(8,128)}) custom-call(s32[32]{0:T(128)S(1)} %get-tuple-element.28.slot, s32[32]{0:T(128)S(1)} %get-tuple-element.29.group, s32[32]{0:T(128)S(1)} %broadcast_subtract_fusion.target, f32[32]{0:T(128)S(1)} %compare_convert_fusion.9.live, bf16[64,48,256]{2,1,0:T(8,128)(2,1)S(1)} %all-to-all-done.5.relayed, ...), custom_call_target="tpu_custom_call" | custom-call | tf_op jit(solution)/shard_map/image/pallas_call | solution.py:165
  160.2 4.1 %all-to-all-start.8 = ((f32[8,4,128]{2,1,0:T(4,128)}), f32[8,4,128]{2,1,0:T(4,128)S(1)}, u32[]{:S(2)}, u32[]{:S(2)}) async-start(f32[8,4,128]{2,1,0:T(4,128)} %bitcast.26), calls=%async_computation.8 | async-start | bytes 32768 | tf_op jit(solution)/shard_map/all_to_all | solution.py:85
  164.3 4.6 %all-to-all-done.8 = f32[8,4,128]{2,1,0:T(4,128)S(1)} async-done(((f32[8,4,128]{2,1,0:T(4,128)}), f32[8,4,128]{2,1,0:T(4,128)S(1)}, u32[]{:S(2)}, u32[]{:S(2)}) %all-to-all-start.8) | async-done | bytes 16416 | tf_op jit(solution)/shard_map/all_to_all | solution.py:85
  169.0 0.7 broadcast_in_dim.47
  169.7 4.7 %all-to-all-start.9 = ((f32[64,4,128]{2,1,0:T(4,128)}), f32[64,4,128]{2,1,0:T(4,128)S(1)}, u32[]{:S(2)}, u32[]{:S(2)}) async-start(f32[64,4,128]{2,1,0:T(4,128)} %broadcast_in_dim.47), calls=%async_computation.9 | async-start | bytes 262144 | tf_op jit(solution)/shard_map/all_to_all | solution.py:90
  174.4 0.6 compare_reduce_fusion
  175.0 0.7 fusion.31
  175.7 4.9 %custom-call.6 = f32[1,64,64]{1,2,0:T(8,128)S(1)} custom-call(f32[1,64,64]{2,1,0:T(8,128)S(1)} %fusion.31), custom_call_target="InvertDiagBlocksLowerTriangular" | custom-call | tf_op jit(solution)/shard_map/triangular_solve | solution.py:151
  180.6 5.3 %all-to-all-done.9 = f32[64,4,128]{2,1,0:T(4,128)S(1)} async-done(((f32[64,4,128]{2,1,0:T(4,128)}), f32[64,4,128]{2,1,0:T(4,128)S(1)}, u32[]{:S(2)}, u32[]{:S(2)}) %all-to-all-start.9) | async-done | bytes 131104 | tf_op jit(solution)/shard_map/all_to_all | solution.py:90
  185.9 0.1 reduce_sum.79
  186.0 0.6 broadcast_in_dim.48
  186.6 5.4 %all-to-all-start.10 = ((f32[8,4,128]{2,1,0:T(4,128)}), f32[8,4,128]{2,1,0:T(4,128)S(1)}, u32[]{:S(2)}, u32[]{:S(2)}) async-start(f32[8,4,128]{2,1,0:T(4,128)} %broadcast_in_dim.48), calls=%async_computation.10 | async-start | bytes 32768 | tf_op jit(solution)/shard_map/all_to_all | solution.py:90
  192.0 0.2 fusion.32.inverse
  192.2 4.5 %all-to-all-done.10 = f32[8,4,128]{2,1,0:T(4,128)S(1)} async-done(((f32[8,4,128]{2,1,0:T(4,128)}), f32[8,4,128]{2,1,0:T(4,128)S(1)}, u32[]{:S(2)}, u32[]{:S(2)}) %all-to-all-start.10) | async-done | bytes 16416 | tf_op jit(solution)/shard_map/all_to_all | solution.py:90
  196.7 1.0 residual.1
  197.7 0.8 copy.55
  (22 shorter events, 0.2 us)
Async XLA Ops:
  2.4 17.5 %all-to-all-start = ((f32[8,4,128]{2,1,0:T(4,128)}), f32[8,4,128]{2,1,0:T(4,128)S(1)}, u32[]{:S(2)}, u32[]{:S(2)}) async-start(f32[8,4,128]{2,1,0:T(4,128)} %bitcast.1), calls=%async_computation | async-start | bytes 32768 | tf_op jit(solution)/shard_map/all_to_all | solution.py:85
  19.9 10.9 %all-to-all-start.2 = ((s32[8,1,8]{2,1,0:T(1,128)}), s32[8,1,8]{2,1,0:T(1,128)S(1)}, u32[]{:S(2)}, u32[]{:S(2)}) async-start(s32[8,1,8]{2,1,0:T(1,128)} %copy.48), calls=%async_computation.2 | async-start | bytes 8192 | tf_op jit(solution)/shard_map/all_to_all | solution.py:126
  31.4 29.2 %all-to-all-start.1 = ((f32[8,4,128]{2,1,0:T(4,128)}), f32[8,4,128]{2,1,0:T(4,128)S(1)}, u32[]{:S(2)}, u32[]{:S(2)}) async-start(f32[8,4,128]{2,1,0:T(4,128)} %broadcast_in_dim.40), calls=%async_computation.1 | async-start | bytes 32768 | tf_op jit(solution)/shard_map/all_to_all | solution.py:90
  60.6 56.4 %copy-start.2 = (s32[4]{0:T(128)S(1)}, s32[4]{0:T(128)}, u32[]{:S(2)}) copy-start(s32[4]{0:T(128)} %param.11) | copy-start | bytes 52
  60.6 56.4 %copy-start.1 = (bf16[4,17,256]{2,0,1:T(4,128)(2,1)S(1)}, bf16[4,17,256]{2,0,1:T(4,128)(2,1)}, u32[]{:S(2)}) copy-start(bf16[4,17,256]{2,0,1:T(4,128)(2,1)} %param.10) | copy-start | bytes 104452
  61.2 12.8 %all-to-all-start.3 = ((f32[8,4,128]{2,1,0:T(4,128)}), f32[8,4,128]{2,1,0:T(4,128)S(1)}, u32[]{:S(2)}, u32[]{:S(2)}) async-start(f32[8,4,128]{2,1,0:T(4,128)} %broadcast_in_dim.45), calls=%async_computation.3 | async-start | bytes 32768 | tf_op jit(solution)/shard_map/all_to_all | solution.py:90
  74.0 21.2 %all-to-all-start.6 = ((s32[64,1,1]{2,1,0:T(1,128)}), s32[64,1,1]{2,1,0:T(1,128)S(1)}, u32[]{:S(2)}, u32[]{:S(2)}) async-start(s32[64,1,1]{2,1,0:T(1,128)} %copy.53), calls=%async_computation.6 | async-start | bytes 65536 | tf_op jit(solution)/shard_map/all_to_all | solution.py:127
  95.8 9.9 %all-to-all-start.4 = ((f32[8,4,128]{2,1,0:T(4,128)}), f32[8,4,128]{2,1,0:T(4,128)S(1)}, u32[]{:S(2)}, u32[]{:S(2)}) async-start(f32[8,4,128]{2,1,0:T(4,128)} %broadcast_in_dim.46), calls=%async_computation.4 | async-start | bytes 32768 | tf_op jit(solution)/shard_map/all_to_all | solution.py:90
  105.7 23.7 %all-to-all-start.7 = ((bf16[64,16,256]{2,1,0:T(8,128)(2,1)}), bf16[64,16,256]{2,1,0:T(8,128)(2,1)S(1)}, u32[]{:S(2)}, u32[]{:S(2)}) async-start(bf16[64,16,256]{2,1,0:T(8,128)(2,1)} %pick.3), calls=%async_computation.7 | async-start | bytes 1048576 | tf_op jit(solution)/shard_map/all_to_all | solution.py:133
  111.7 22.5 %collective-permute-start.1 = (bf16[4,64,8]{2,1,0:T(8,128)(2,1)S(1)}, bf16[4,64,8]{2,1,0:T(8,128)(2,1)S(1)}, u32[]{:S(2)}, u32[]{:S(2)}) collective-permute-start(bf16[4,64,8]{2,1,0:T(8,128)(2,1)S(1)} %get-tuple-element.31), channel_id=1, source_target_pairs={{1,0},{2,1},{3,2},{4,3},{5,4},{6,5},{7,6},{9,8},{10,9},{11,10},{12... | collective-permute-start | bytes 12296 | tf_op jit(solution)/shard_map/ppermute | solution.py:157
  113.0 21.2 %collective-permute-start = (bf16[4,64,8]{2,1,0:T(8,128)(2,1)S(1)}, bf16[4,64,8]{2,1,0:T(8,128)(2,1)S(1)}, u32[]{:S(2)}, u32[]{:S(2)}) collective-permute-start(bf16[4,64,8]{2,1,0:T(8,128)(2,1)S(1)} %get-tuple-element.30), channel_id=1, source_target_pairs={{0,1},{1,2},{2,3},{3,4},{4,5},{5,6},{6,7},{8,9},{9,10},{10,11},{11... | collective-permute-start | bytes 12296 | tf_op jit(solution)/shard_map/ppermute | solution.py:156
  117.1 17.0 %copy-start.4 = (s32[32]{0:T(128)S(1)}, s32[32]{0:T(128)}, u32[]{:S(2)}) copy-start(s32[32]{0:T(128)} %param.14) | copy-start | bytes 388
  117.1 17.1 %copy-start.3 = (f32[4]{0:T(128)S(1)}, f32[4]{0:T(128)}, u32[]{:S(2)}) copy-start(f32[4]{0:T(128)} %param.12) | copy-start | bytes 52
  129.4 25.4 %all-to-all-start.5 = ((bf16[64,48,256]{2,1,0:T(8,128)(2,1)}), bf16[64,48,256]{2,1,0:T(8,128)(2,1)S(1)}, u32[]{:S(2)}, u32[]{:S(2)}) async-start(bf16[64,48,256]{2,1,0:T(8,128)(2,1)} %pick.2), calls=%async_computation.5 | async-start | bytes 3145728 | tf_op jit(solution)/shard_map/all_to_all | solution.py:148
  154.8 2.2 %copy-start = (bf16[32,256,256]{2,1,0:T(8,128)(2,1)S(1)}, bf16[32,256,256]{2,1,0:T(8,128)(2,1)}, u32[]{:S(2)}) copy-start(bf16[32,256,256]{2,1,0:T(8,128)(2,1)} %coupling.1) | copy-start | bytes 12582916
  160.2 8.8 %all-to-all-start.8 = ((f32[8,4,128]{2,1,0:T(4,128)}), f32[8,4,128]{2,1,0:T(4,128)S(1)}, u32[]{:S(2)}, u32[]{:S(2)}) async-start(f32[8,4,128]{2,1,0:T(4,128)} %bitcast.26), calls=%async_computation.8 | async-start | bytes 32768 | tf_op jit(solution)/shard_map/all_to_all | solution.py:85
  169.7 16.2 %all-to-all-start.9 = ((f32[64,4,128]{2,1,0:T(4,128)}), f32[64,4,128]{2,1,0:T(4,128)S(1)}, u32[]{:S(2)}, u32[]{:S(2)}) async-start(f32[64,4,128]{2,1,0:T(4,128)} %broadcast_in_dim.47), calls=%async_computation.9 | async-start | bytes 262144 | tf_op jit(solution)/shard_map/all_to_all | solution.py:90
  186.6 10.1 %all-to-all-start.10 = ((f32[8,4,128]{2,1,0:T(4,128)}), f32[8,4,128]{2,1,0:T(4,128)S(1)}, u32[]{:S(2)}, u32[]{:S(2)}) async-start(f32[8,4,128]{2,1,0:T(4,128)} %broadcast_in_dim.48), calls=%async_computation.10 | async-start | bytes 32768 | tf_op jit(solution)/shard_map/all_to_all | solution.py:90

commit v3 on v2

v3 whole, which is shorter than its diff:
```python
import functools

import jax
import jax.numpy as jnp
from jax import lax
from jax.experimental import pallas as pl
from jax.experimental.pallas import tpu as pltpu
from jax.sharding import Mesh, PartitionSpec as P

BW = 8
BLK = 256
CORES = 2
X_CHIPS = 4
UNROLL = 8
INNER = ("x", "core")
CHAN = ("y", "x", "core")
VMEM = pl.BlockSpec(memory_space=pltpu.VMEM)
SMEM = pl.BlockSpec(memory_space=pltpu.SMEM)
NT = (((1,), (1,)), ((), ()))
HIGH = lax.Precision.HIGHEST
PARAMS = pltpu.CompilerParams(vmem_limit_bytes=40 * 1024 * 1024)


def pack(square):
    half = square.shape[0] // 2
    return jnp.concatenate([square[:half], square[half:]], axis=1)


def unpack(packed):
    half = packed.shape[1] // 2
    return jnp.concatenate([packed[:, :half], packed[:, half:]], axis=0)


def gram_of(rows):
    acc = None
    for c in range(rows.shape[0]):
        term = lax.dot_general(rows[c], rows[c], NT, preferred_element_type=jnp.float32)
        acc = term if acc is None else acc + term
    return acc


def pick_kernel(per_group, want, rows, out, gram):
    @pl.loop(0, out.shape[0])
    def _(i):
        group = lax.rem(i, rows.shape[0] // per_group)
        out[i] = rows[group * per_group + want[i]]

    gram[...] = pack(gram_of(rows))


def image_kernel(slot, target, live, rows, coupling, banded, trial, gram, image, sent, total):
    total[...] = banded[...]

    @pl.loop(0, coupling.shape[0], step=UNROLL)
    def _(first):
        for i in range(UNROLL):
            p = first + i
            part = lax.dot_general(
                rows[slot[p]], coupling[p], NT, preferred_element_type=jnp.float32
            )
            total[target[p]] += part * live[p]

    acc = jnp.zeros((trial.shape[1], trial.shape[1]), jnp.float32)
    for c in range(total.shape[0]):
        rounded = total[c].astype(jnp.bfloat16)
        image[c] = rounded
        acc += lax.dot_general(trial[c], rounded, NT, preferred_element_type=jnp.float32)
    packed = pack(acc)
    summed = jnp.sum(gram[...], axis=0)
    piece = sent.shape[1] - summed.shape[0]
    for j in range(sent.shape[0]):
        sent[j, :piece] = packed[j * piece : (j + 1) * piece]
        sent[j, piece:] = summed


def middle_kernel(received, spread, gram):
    whole = jnp.sum(received[...], axis=0)
    piece = spread.shape[1]
    for j in range(spread.shape[0]):
        spread[j] = whole[:piece]
    gram[...] = unpack(whole[piece:])


def spread_kernel(received, spread):
    whole = jnp.sum(received[...], axis=0)
    for j in range(spread.shape[0]):
        spread[j] = whole


def residual_kernel(inverse, projected, trial, image, residual, rayleigh):
    inv = inverse[...]
    half = jnp.dot(inv, unpack(projected[...]), precision=HIGH, preferred_element_type=jnp.float32)
    full = lax.dot_general(
        inv, half, (((0,), (0,)), ((), ())), precision=HIGH, preferred_element_type=jnp.float32
    )
    rayleigh[...] = full
    flipped = full.T.astype(jnp.bfloat16)
    for c in range(trial.shape[0]):
        fit = jnp.dot(flipped, trial[c], preferred_element_type=jnp.float32)
        residual[c] = (image[c].astype(jnp.float32) - fit).astype(jnp.bfloat16)


def call(kernel, name, shapes, specs, *operands, scratch=()):
    several = isinstance(shapes, tuple)
    return pl.pallas_call(
        kernel,
        out_shape=shapes,
        in_specs=specs,
        out_specs=(VMEM,) * len(shapes) if several else VMEM,
        scratch_shapes=scratch,
        compiler_params=PARAMS,
        name=name,
    )(*operands)


def f32(*shape):
    return jax.ShapeDtypeStruct(shape, jnp.float32)


def bf16(*shape):
    return jax.ShapeDtypeStruct(shape, jnp.bfloat16)


def lookup(table, wanted_ids):
    match = wanted_ids[:, None] == jnp.arange(table.shape[0], dtype=jnp.int32)[None, :]
    return jnp.sum(jnp.where(match, table[None, :], 0), axis=1)


def body(trial, band, band_width, energies, coupling, reach, pair_target, pair_source, chan_slot):
    vecs, slots, slab = trial.shape
    ys, xs, cores, slabs = (lax.axis_size(a) for a in ("y", "x", "core", "rad"))
    me = (lax.axis_index("y") * xs + lax.axis_index("x")) * cores + lax.axis_index("core")
    columns = xs * cores

    source_slot = lookup(chan_slot, pair_source)
    target_local = lookup(chan_slot, pair_target) - me * slots
    group = source_slot // slots
    member = source_slot - group * slots
    hit = group[:, None] == jnp.arange(ys * columns, dtype=jnp.int32)[None, :]
    need = jnp.sum(jnp.where(hit, member[:, None], 0), axis=0)
    want = lax.all_to_all(need.reshape(ys, columns).T, INNER, 0, 0, tiled=True)
    slot = lax.rem(group, columns) * ys + group // columns
    live = (lax.axis_index("rad") < reach).astype(jnp.float32)

    by_slot = jnp.transpose(trial, (1, 0, 2))
    column = lax.all_gather(by_slot, "y", axis=0, tiled=True)
    picked, gram = call(
        functools.partial(pick_kernel, slots),
        "pick",
        (bf16(columns * ys, vecs, slab), f32(vecs // 2, 2 * vecs)),
        [SMEM, VMEM],
        want.reshape(-1),
        column,
    )
    rows = lax.all_to_all(picked, INNER, 0, 0, tiled=True)
    gram = lax.all_gather(gram, "rad")

    up = [(i, i + 1) for i in range(slabs - 1)]
    before = lax.ppermute(by_slot[:, :, slab - BW :], "rad", up)
    after = lax.ppermute(by_slot[:, :, :BW], "rad", [(j, i) for i, j in up])
    padded = jnp.concatenate([before, by_slot, after], axis=2)
    banded = energies[:, None, None] * by_slot.astype(jnp.float32)
    for offset in range(2 * BW + 1):
        inside = (abs(offset - BW) <= band_width).astype(jnp.float32)
        weight = inside[:, None] * band[:, offset, :].astype(jnp.float32)
        banded += weight[:, None] * padded[:, :, offset : offset + slab].astype(jnp.float32)

    half = vecs // 2
    piece = half // columns
    image, sent = call(
        image_kernel,
        "image",
        (bf16(*by_slot.shape), f32(columns, piece + half, 2 * vecs)),
        [SMEM] * 3 + [VMEM] * 5,
        slot,
        target_local,
        live,
        rows,
        coupling,
        banded,
        by_slot,
        gram,
        scratch=[pltpu.VMEM(by_slot.shape, jnp.float32)],
    )
    received = lax.all_to_all(sent, INNER, 0, 0, tiled=True)
    spread, gram = call(
        middle_kernel, "middle", (f32(ys * slabs, piece, 2 * vecs), f32(vecs, vecs)), [VMEM], received
    )
    received = lax.all_to_all(spread, ("y", "rad"), 0, 0, tiled=True)
    factor = jnp.linalg.cholesky(gram)
    inverse = lax.linalg.triangular_solve(
        factor, jnp.eye(vecs, dtype=jnp.float32), left_side=True, lower=True
    )
    spread = call(spread_kernel, "spread", f32(columns, piece, 2 * vecs), [VMEM], received)
    projected = lax.all_to_all(spread, INNER, 0, 0, tiled=True).reshape(half, 2 * vecs)
    residual, rayleigh = call(
        residual_kernel,
        "residual",
        (bf16(*by_slot.shape), f32(vecs, vecs)),
        [VMEM] * 4,
        inverse,
        projected,
        by_slot,
        image,
    )
    return jnp.transpose(residual, (1, 0, 2)), rayleigh


def solution(mesh):
    chan, rad = mesh.shape["chan"], mesh.shape["rad"]
    fine = Mesh(
        mesh.devices.reshape(chan // (X_CHIPS * CORES), X_CHIPS, CORES, rad),
        ("y", "x", "core", "rad"),
    )
    placed = (
        P(None, CHAN, "rad"),
        P(CHAN, None, "rad"),
        P(CHAN),
        P(CHAN),
        P(CHAN, "rad", None),
        P(CHAN),
        P(CHAN),
        P(CHAN),
        P(),
    )
    return jax.shard_map(
        body, mesh=fine, in_specs=placed, out_specs=(P(None, CHAN, "rad"), P()), check_vma=False
    )
```

time: 199 us -> 165 us (0.83)
  starting transfers between devices: 72.6 us -> 29.5 us
  blocking collectives: 21.7 us -> 53.3 us
  waiting for transfers between devices: 68 us -> 38.3 us
  between operations: 0.84 us -> 14.2 us
  Pallas kernels: 9.15 us -> 6.49 us
    all_to_all x11 -> x3, waiting for transfers between devices: 68 us -> 9.85 us  [the longest x1 5.39 us: body(): received = lax.all_to_all(spread, ('y', 'rad'), 0, 0, tiled=True)]
    all_to_all x11 -> x3, starting transfers between devices: 67.4 us -> 24.2 us  [the longest x1 9.82 us: body(): rows = lax.all_to_all(picked, INNER, 0, 0, tiled=True)]
    all_to_all x0 -> x2, blocking collectives: none -> 30 us  [the longest x1 16.2 us: body(): received = lax.all_to_all(sent, INNER, 0, 0, tiled=True)]
    all_gather x0 -> x1, waiting for transfers between devices: none -> 27.3 us  [body(): column = lax.all_gather(by_slot, 'y', axis=0, tiled=True)]
    broadcast_in_dim x5 -> x0, local copies, waits for them, and re-layouts: 3.11 us -> none  [exchange(): spread = jnp.broadcast_to(piece[None], (lax.axis_size(axes),) + piece.shape)]
    unnamed x14 -> x18, local copies, waits for them, and re-layouts: 4.04 us -> 7.13 us
    pallas_call x5, Pallas kernels: 9.15 us -> 6.49 us  [call(): pl.pallas_call(kernel, out_shape=shapes, in_specs=specs, out_specs=(VMEM,...]
  transfers between devices with their start and end apart: 13 -> 6, of which waited for: 10 -> 5; matrix products, arithmetic and copies ran while one was open for 10% -> 6% of each run, Pallas kernels for 2% -> 0%
where the time goes in v3:
time: 165 us
  blocking collectives  53.3 us (32%)
  waiting for transfers between devices  38.3 us (23%)
  starting transfers between devices  29.5 us (18%)
  other arithmetic  14.9 us (9%)
  between operations  14.2 us (9%)
  local copies, waits for them, and re-layouts  8.03 us (5%)
  Pallas kernels  6.49 us (4%)
    all_gather x1, waiting for transfers between devices, body(): column = lax.all_gather(by_slot, 'y', axis=0, tiled=True)  27.3 us
    all_gather x1, blocking collectives, body(): gram = lax.all_gather(gram, 'rad')  23.3 us
    all_to_all x1, blocking collectives, body(): received = lax.all_to_all(sent, INNER, 0, 0, tiled=True)  16.2 us
    all_to_all x1, blocking collectives, body(): want = lax.all_to_all(need.reshape(ys, columns).T, INNER, 0, 0, tiled=True)  13.8 us
    all_to_all x1, starting transfers between devices, body(): rows = lax.all_to_all(picked, INNER, 0, 0, tiled=True)  9.82 us
    all_to_all x1, starting transfers between devices, body(): received = lax.all_to_all(spread, ('y', 'rad'), 0, 0, tiled=True)  8.98 us
    unnamed x18, local copies, waits for them, and re-layouts  7.13 us
    another operation x3, other arithmetic, body(): factor = jnp.linalg.cholesky(gram)  6.51 us
  transfers between devices with their start and end apart: 6, of which 5 were waited for; matrix products, arithmetic and copies ran while one was open for 6% of the time, Pallas kernels for 0%

profile of v3, /device:TPU:1, one launch (start us, length us, event | category | flops | bytes accessed | tf_op | source)
XLA Modules:
  0.0 164.9 jit_solution(3544438474763259540)
XLA Ops:
  7.2 0.0 all-gather.3.cloned.1.call-start
  7.2 1.6 copy.28
  8.8 0.0 all-gather.3.cloned.1.call-update
  8.8 0.9 select_reduce_fusion.1
  9.7 0.1 select_reduce_fusion.3
  9.8 0.1 reshape.136
  9.9 0.1 copy.21
  9.9 13.8 %all_to_all.29 = s32[8,1,8]{2,1,0:T(1,128)S(1)} all-to-all(s32[8,1,8]{2,1,0:T(1,128)S(1)} %copy.21), channel_id=1, replica_groups=mesh['y'=8,'x'=4,'core'=2,'rad'=8] {'x','core'}, dimensions={0} | all-to-all | bytes 512 | tf_op jit(solution)/shard_map/all_to_all | solution.py:141
  23.8 0.5 broadcast.223
  24.3 0.7 reduce.9
  24.9 0.1 reshape.137.want
  25.0 27.3 %all-gather.3.cloned.1.call-done.rows = bf16[32,64,256]{2,1,0:T(8,128)(2,1)} async-done(((bf16[4,64,256]{2,1,0:T(8,128)(2,1)}), bf16[32,64,256]{2,1,0:T(8,128)(2,1)}) %all-gather.3.cloned.1.call-update) | async-done | bytes 1048592 | tf_op jit(solution)/shard_map/all_gather | solution.py:146
  52.3 0.0 copy-start.3
  52.3 1.2 copy-done.3
  53.5 1.5 pick.1
  55.0 0.0 copy-start.2
  55.0 1.4 copy-done.2
  56.4 0.0 copy-start
  56.4 0.0 copy-start.5
  56.4 0.0 copy-start.4
  56.4 0.0 copy-start.7
  56.4 0.0 copy-start.6
  56.4 9.8 %all-to-all-start.1 = ((bf16[64,64,256]{2,1,0:T(8,128)(2,1)}), bf16[64,64,256]{2,1,0:T(8,128)(2,1)S(1)}, u32[]{:S(2)}, u32[]{:S(2)}) async-start(bf16[64,64,256]{2,1,0:T(8,128)(2,1)} %copy-done.2), calls=%async_computation.1 | async-start | bytes 4194304 | tf_op jit(solution)/shard_map/all_to_all | solution.py:155
  66.2 0.0 copy-done
  66.2 0.1 fusion.35
  66.3 1.3 collective-permute-start.1
  67.6 4.0 %collective-permute-start = (bf16[4,64,8]{2,1,0:T(8,128)(2,1)S(1)}, bf16[4,64,8]{2,1,0:T(8,128)(2,1)S(1)}, u32[]{:S(2)}, u32[]{:S(2)}) collective-permute-start(bf16[4,64,8]{2,1,0:T(8,128)(2,1)S(1)} %get-tuple-element.28), channel_id=1, source_target_pairs={{0,1},{1,2},{2,3},{3,4},{4,5},{5,6},{6,7},{8,9},{9,10},{10,11},{11... | collective-permute-start | bytes 12296 | tf_op jit(solution)/shard_map/ppermute | solution.py:159
  71.7 0.0 copy-done.5
  71.7 0.0 copy-done.4
  71.7 0.1 multiply_bitcast_fusion.15
  71.8 0.1 multiply_bitcast_fusion.16
  71.9 0.0 copy-done.7
  71.9 0.1 collective-permute-done.1
  72.0 1.0 collective-permute-done
  73.0 0.0 copy-done.6
  73.0 1.0 fusion.16.banded
  74.0 23.3 %all-gather = f32[256,128]{1,0:T(8,128)S(1)} all-gather(f32[32,128]{1,0:T(8,128)S(1)} %get-tuple-element.11), channel_id=2, replica_groups=mesh['y'=8,'x'=4,'core'=2,'rad'=8] {'rad'}, dimensions={0}, use_global_device_ids=true | all-gather | bytes 147456 | tf_op jit(solution)/shard_map/all_gather | solution.py:156
  97.3 0.0 all-to-all-done.1.rows
  97.3 0.0 copy-start.1
  97.3 2.2 %copy-done.1 = bf16[32,256,256]{2,1,0:T(8,128)(2,1)S(1)} copy-done((bf16[32,256,256]{2,1,0:T(8,128)(2,1)S(1)}, bf16[32,256,256]{2,1,0:T(8,128)(2,1)}, u32[]{:S(2)}) %copy-start.1) | copy-done | bytes 4194328
  99.5 2.6 %image.1 = (bf16[4,64,256]{2,1,0:T(8,128)(2,1)S(1)}, f32[8,36,128]{2,1,0:T(8,128)S(1)}) custom-call(s32[32]{0:T(128)S(1)} %get-tuple-element.68.slot, s32[32]{0:T(128)S(1)} %get-tuple-element.69.target, f32[32]{0:T(128)S(1)} %compare_convert_fusion.9.live, bf16[64,64,256]{2,1,0:T(8,128)(2,1)S(1)} %all-to-all-done.1.rows, ...), custom_call_target="tpu_custom_call" | custom-call | tf_op jit(solution)/shard_map/image/pallas_call | solution.py:105
  102.1 16.2 %all_to_all.30.received = f32[8,36,128]{2,1,0:T(8,128)S(1)} all-to-all(f32[8,36,128]{2,1,0:T(8,128)S(1)} %get-tuple-element.12), channel_id=1, replica_groups=mesh['y'=8,'x'=4,'core'=2,'rad'=8] {'x','core'}, dimensions={0} | all-to-all | bytes 294912 | tf_op jit(solution)/shard_map/all_to_all | solution.py:185
  118.3 0.7 middle.1
  119.0 0.1 copy.23
  119.1 5.8 %cholesky.17 = f32[64,64]{1,0:T(8,128)S(1)} custom-call(f32[64,64]{1,0:T(8,128)S(1)} %fusion.34), custom_call_target="Cholesky" | custom-call | tf_op jit(solution)/shard_map/jit(cholesky)/cholesky | solution.py:190
  125.0 9.0 %all-to-all-start.3 = ((f32[64,4,128]{2,1,0:T(4,128)}), f32[64,4,128]{2,1,0:T(4,128)S(1)}, u32[]{:S(2)}, u32[]{:S(2)}) async-start(f32[64,4,128]{2,1,0:T(4,128)} %get-tuple-element.14), calls=%async_computation.3 | async-start | bytes 262144 | tf_op jit(solution)/shard_map/all_to_all | solution.py:189
  133.9 0.6 compare_reduce_fusion
  134.6 0.7 fusion.31
  135.2 4.9 %custom-call.6 = f32[1,64,64]{1,2,0:T(8,128)S(1)} custom-call(f32[1,64,64]{2,1,0:T(8,128)S(1)} %fusion.31), custom_call_target="InvertDiagBlocksLowerTriangular" | custom-call | tf_op jit(solution)/shard_map/triangular_solve | solution.py:191
  140.1 5.4 %all-to-all-done.3.received = f32[64,4,128]{2,1,0:T(4,128)S(1)} async-done(((f32[64,4,128]{2,1,0:T(4,128)}), f32[64,4,128]{2,1,0:T(4,128)S(1)}, u32[]{:S(2)}, u32[]{:S(2)}) %all-to-all-start.3) | async-done | bytes 131104 | tf_op jit(solution)/shard_map/all_to_all | solution.py:189
  145.5 0.7 spread.1
  146.2 5.4 %all-to-all-start.4 = ((f32[8,4,128]{2,1,0:T(4,128)}), f32[8,4,128]{2,1,0:T(4,128)S(1)}, u32[]{:S(2)}, u32[]{:S(2)}) async-start(f32[8,4,128]{2,1,0:T(4,128)} %spread.1), calls=%async_computation.4 | async-start | bytes 32768 | tf_op jit(solution)/shard_map/all_to_all | solution.py:195
  151.6 0.2 fusion.32.inverse
  151.9 4.5 %all-to-all-done.4 = f32[8,4,128]{2,1,0:T(4,128)S(1)} async-done(((f32[8,4,128]{2,1,0:T(4,128)}), f32[8,4,128]{2,1,0:T(4,128)S(1)}, u32[]{:S(2)}, u32[]{:S(2)}) %all-to-all-start.4) | async-done | bytes 16416 | tf_op jit(solution)/shard_map/all_to_all | solution.py:195
  156.3 1.0 residual.1
  157.3 0.8 copy.24
  (6 shorter events, 0.1 us)
Async XLA Ops:
  7.2 45.2 %all-gather.3.cloned.1.call-start = ((), (), s32[]{:S(2)}) async-start(), calls=%async_computation.5 | async-start | bytes 1179648 | tf_op jit(solution)/shard_map/all_gather | solution.py:146
  52.3 1.2 copy-start.3
  55.0 1.4 copy-start.2
  56.4 9.8 %copy-start = (bf16[64,4,256]{2,0,1:T(8,128)(2,1)S(1)}, bf16[64,4,256]{2,0,1:T(8,128)(2,1)}, u32[]{:S(2)}) copy-start(bf16[64,4,256]{2,0,1:T(8,128)(2,1)} %copy.28) | copy-start | bytes 393220
  56.4 15.3 %copy-start.5 = (s32[4]{0:T(128)S(1)}, s32[4]{0:T(128)}, u32[]{:S(2)}) copy-start(s32[4]{0:T(128)} %param.11) | copy-start | bytes 52
  56.4 15.3 %copy-start.4 = (bf16[4,17,256]{2,0,1:T(4,128)(2,1)S(1)}, bf16[4,17,256]{2,0,1:T(4,128)(2,1)}, u32[]{:S(2)}) copy-start(bf16[4,17,256]{2,0,1:T(4,128)(2,1)} %param.10) | copy-start | bytes 104452
  56.4 15.4 %copy-start.7 = (s32[32]{0:T(128)S(1)}, s32[32]{0:T(128)}, u32[]{:S(2)}) copy-start(s32[32]{0:T(128)} %param.14) | copy-start | bytes 388
  56.4 16.5 %copy-start.6 = (f32[4]{0:T(128)S(1)}, f32[4]{0:T(128)}, u32[]{:S(2)}) copy-start(f32[4]{0:T(128)} %param.12) | copy-start | bytes 52
  56.4 40.8 %all-to-all-start.1 = ((bf16[64,64,256]{2,1,0:T(8,128)(2,1)}), bf16[64,64,256]{2,1,0:T(8,128)(2,1)S(1)}, u32[]{:S(2)}, u32[]{:S(2)}) async-start(bf16[64,64,256]{2,1,0:T(8,128)(2,1)} %copy-done.2), calls=%async_computation.1 | async-start | bytes 4194304 | tf_op jit(solution)/shard_map/all_to_all | solution.py:155
  66.3 5.6 %collective-permute-start.1 = (bf16[4,64,8]{2,1,0:T(8,128)(2,1)S(1)}, bf16[4,64,8]{2,1,0:T(8,128)(2,1)S(1)}, u32[]{:S(2)}, u32[]{:S(2)}) collective-permute-start(bf16[4,64,8]{2,1,0:T(8,128)(2,1)S(1)} %get-tuple-element.29), channel_id=1, source_target_pairs={{1,0},{2,1},{3,2},{4,3},{5,4},{6,5},{7,6},{9,8},{10,9},{11,10},{12... | collective-permute-start | bytes 12296 | tf_op jit(solution)/shard_map/ppermute | solution.py:160
  67.6 5.3 %collective-permute-start = (bf16[4,64,8]{2,1,0:T(8,128)(2,1)S(1)}, bf16[4,64,8]{2,1,0:T(8,128)(2,1)S(1)}, u32[]{:S(2)}, u32[]{:S(2)}) collective-permute-start(bf16[4,64,8]{2,1,0:T(8,128)(2,1)S(1)} %get-tuple-element.28), channel_id=1, source_target_pairs={{0,1},{1,2},{2,3},{3,4},{4,5},{5,6},{6,7},{8,9},{9,10},{10,11},{11... | collective-permute-start | bytes 12296 | tf_op jit(solution)/shard_map/ppermute | solution.py:159
  97.3 2.2 %copy-start.1 = (bf16[32,256,256]{2,1,0:T(8,128)(2,1)S(1)}, bf16[32,256,256]{2,1,0:T(8,128)(2,1)}, u32[]{:S(2)}) copy-start(bf16[32,256,256]{2,1,0:T(8,128)(2,1)} %coupling.1) | copy-start | bytes 12582916
  125.0 20.6 %all-to-all-start.3 = ((f32[64,4,128]{2,1,0:T(4,128)}), f32[64,4,128]{2,1,0:T(4,128)S(1)}, u32[]{:S(2)}, u32[]{:S(2)}) async-start(f32[64,4,128]{2,1,0:T(4,128)} %get-tuple-element.14), calls=%async_computation.3 | async-start | bytes 262144 | tf_op jit(solution)/shard_map/all_to_all | solution.py:189
  146.2 10.1 %all-to-all-start.4 = ((f32[8,4,128]{2,1,0:T(4,128)}), f32[8,4,128]{2,1,0:T(4,128)S(1)}, u32[]{:S(2)}, u32[]{:S(2)}) async-start(f32[8,4,128]{2,1,0:T(4,128)} %spread.1), calls=%async_computation.4 | async-start | bytes 32768 | tf_op jit(solution)/shard_map/all_to_all | solution.py:195
Sparse Core Ops, SparseCore 0:
  10.7 41.6 all-gather.2

commit v4 on v3

--- a/solution.py
+++ b/solution.py
@@ -15,10 +15,11 @@
 INNER = ("x", "core")
 CHAN = ("y", "x", "core")
 VMEM = pl.BlockSpec(memory_space=pltpu.VMEM)
+ANY = pl.BlockSpec(memory_space=pl.ANY)
 SMEM = pl.BlockSpec(memory_space=pltpu.SMEM)
 NT = (((1,), (1,)), ((), ()))
 HIGH = lax.Precision.HIGHEST
-PARAMS = pltpu.CompilerParams(vmem_limit_bytes=40 * 1024 * 1024)
+MIB = 1024 * 1024
 
 
 def pack(square):
@@ -39,24 +40,62 @@
     return acc
 
 
-def pick_kernel(per_group, want, rows, out, gram):
+def pick_kernel(mine, need, rows, out, sems):
+    receivers = need.shape[0]
+    groups = out.shape[0] // receivers
+    per_group = rows.shape[0] // groups
+    columns = need.shape[1] // groups
+
+    def copy(i):
+        receiver, group = lax.div(i, groups), lax.rem(i, groups)
+        chosen = group * per_group + need[receiver, group * columns + mine[0]]
+        return pltpu.make_async_copy(rows.at[chosen], out.at[i], sems.at[i])
+
     @pl.loop(0, out.shape[0])
     def _(i):
-        group = lax.rem(i, rows.shape[0] // per_group)
-        out[i] = rows[group * per_group + want[i]]
-
+        copy(i).start()
+
+    @pl.loop(0, out.shape[0])
+    def _(i):
+        copy(i).wait()
+
+
+def gram_kernel(rows, gram):
     gram[...] = pack(gram_of(rows))
 
 
-def image_kernel(slot, target, live, rows, coupling, banded, trial, gram, image, sent, total):
+def inverse_kernel(square, inverse):
+    size = square.shape[0]
+    down = lax.broadcasted_iota(jnp.int32, (size, size), 0)
+    across = lax.broadcasted_iota(jnp.int32, (size, size), 1)
+    value = square[...]
+    for k in range(size):
+        scale = 1.0 / value[k : k + 1, k : k + 1]
+        row = jnp.where(across[:1] == k, 1.0, value[k : k + 1]) * scale
+        column = jnp.where(down[:, :1] == k, -1.0, value[:, k : k + 1])
+        rest = jnp.where((down == k) | (across == k), 0.0, value)
+        value = rest - column * row
+    inverse[...] = value
+
+
+def image_kernel(slot, target, live, rows, coupling, banded, trial, gram, image, sent, total, held, sems):
+    def copy(p):
+        return pltpu.make_async_copy(coupling.at[p], held.at[p], sems.at[p])
+
+    @pl.loop(0, coupling.shape[0])
+    def _(p):
+        copy(p).start()
+
     total[...] = banded[...]
 
     @pl.loop(0, coupling.shape[0], step=UNROLL)
     def _(first):
         for i in range(UNROLL):
+            copy(first + i).wait()
+        for i in range(UNROLL):
             p = first + i
             part = lax.dot_general(
-                rows[slot[p]], coupling[p], NT, preferred_element_type=jnp.float32
+                rows[slot[p]], held[p], NT, preferred_element_type=jnp.float32
             )
             total[target[p]] += part * live[p]
 
@@ -88,10 +127,11 @@
 
 
 def residual_kernel(inverse, projected, trial, image, residual, rayleigh):
-    inv = inverse[...]
-    half = jnp.dot(inv, unpack(projected[...]), precision=HIGH, preferred_element_type=jnp.float32)
-    full = lax.dot_general(
-        inv, half, (((0,), (0,)), ((), ())), precision=HIGH, preferred_element_type=jnp.float32
+    full = jnp.dot(
+        inverse[...],
+        unpack(projected[...]),
+        precision=HIGH,
+        preferred_element_type=jnp.float32,
     )
     rayleigh[...] = full
     flipped = full.T.astype(jnp.bfloat16)
@@ -100,15 +140,15 @@
         residual[c] = (image[c].astype(jnp.float32) - fit).astype(jnp.bfloat16)
 
 
-def call(kernel, name, shapes, specs, *operands, scratch=()):
+def call(kernel, name, shapes, specs, *operands, out=VMEM, scratch=(), limit=40):
     several = isinstance(shapes, tuple)
     return pl.pallas_call(
         kernel,
         out_shape=shapes,
         in_specs=specs,
-        out_specs=(VMEM,) * len(shapes) if several else VMEM,
+        out_specs=(VMEM,) * len(shapes) if several else out,
         scratch_shapes=scratch,
-        compiler_params=PARAMS,
+        compiler_params=pltpu.CompilerParams(vmem_limit_bytes=limit * MIB),
         name=name,
     )(*operands)
 
@@ -138,22 +178,14 @@
     member = source_slot - group * slots
     hit = group[:, None] == jnp.arange(ys * columns, dtype=jnp.int32)[None, :]
     need = jnp.sum(jnp.where(hit, member[:, None], 0), axis=0)
-    want = lax.all_to_all(need.reshape(ys, columns).T, INNER, 0, 0, tiled=True)
+    needed = lax.all_gather(need, INNER)
     slot = lax.rem(group, columns) * ys + group // columns
     live = (lax.axis_index("rad") < reach).astype(jnp.float32)
 
     by_slot = jnp.transpose(trial, (1, 0, 2))
-    column = lax.all_gather(by_slot, "y", axis=0, tiled=True)
-    picked, gram = call(
-        functools.partial(pick_kernel, slots),
-        "pick",
-        (bf16(columns * ys, vecs, slab), f32(vecs // 2, 2 * vecs)),
-        [SMEM, VMEM],
-        want.reshape(-1),
-        column,
-    )
-    rows = lax.all_to_all(picked, INNER, 0, 0, tiled=True)
-    gram = lax.all_gather(gram, "rad")
+    column = lax.all_to_all(
+        jnp.broadcast_to(by_slot[None], (ys,) + by_slot.shape), "y", 0, 0, tiled=True
+    ).reshape(ys * slots, vecs, slab)
 
     up = [(i, i + 1) for i in range(slabs - 1)]
     before = lax.ppermute(by_slot[:, :, slab - BW :], "rad", up)
@@ -165,13 +197,30 @@
         weight = inside[:, None] * band[:, offset, :].astype(jnp.float32)
         banded += weight[:, None] * padded[:, :, offset : offset + slab].astype(jnp.float32)
 
+    column, banded = lax.optimization_barrier((column, banded))
+    mine = (lax.axis_index("x") * cores + lax.axis_index("core")).reshape(1)
+    picked = call(
+        pick_kernel,
+        "pick",
+        bf16(columns * ys, vecs, slab),
+        [SMEM, SMEM, ANY],
+        mine,
+        needed,
+        column,
+        out=ANY,
+        scratch=[pltpu.SemaphoreType.DMA((columns * ys,))],
+    )
+    column, picked = lax.optimization_barrier((column, picked))
+    rows = lax.all_to_all(picked, INNER, 0, 0, tiled=True)
+    gram = lax.all_gather(call(gram_kernel, "gram", f32(vecs // 2, 2 * vecs), [VMEM], column), "rad")
+
     half = vecs // 2
     piece = half // columns
     image, sent = call(
         image_kernel,
         "image",
         (bf16(*by_slot.shape), f32(columns, piece + half, 2 * vecs)),
-        [SMEM] * 3 + [VMEM] * 5,
+        [SMEM] * 3 + [VMEM, ANY] + [VMEM] * 3,
         slot,
         target_local,
         live,
@@ -180,17 +229,19 @@
         banded,
         by_slot,
         gram,
-        scratch=[pltpu.VMEM(by_slot.shape, jnp.float32)],
+        scratch=[
+            pltpu.VMEM(by_slot.shape, jnp.float32),
+            pltpu.VMEM(coupling.shape, jnp.bfloat16),
+            pltpu.SemaphoreType.DMA(coupling.shape[:1]),
+        ],
+        limit=50,
     )
     received = lax.all_to_all(sent, INNER, 0, 0, tiled=True)
     spread, gram = call(
         middle_kernel, "middle", (f32(ys * slabs, piece, 2 * vecs), f32(vecs, vecs)), [VMEM], received
     )
     received = lax.all_to_all(spread, ("y", "rad"), 0, 0, tiled=True)
-    factor = jnp.linalg.cholesky(gram)
-    inverse = lax.linalg.triangular_solve(
-        factor, jnp.eye(vecs, dtype=jnp.float32), left_side=True, lower=True
-    )
+    inverse = call(inverse_kernel, "inverse", f32(vecs, vecs), [VMEM], gram)
     spread = call(spread_kernel, "spread", f32(columns, piece, 2 * vecs), [VMEM], received)
     projected = lax.all_to_all(spread, INNER, 0, 0, tiled=True).reshape(half, 2 * vecs)
     residual, rayleigh = call(

time: 165 us -> 127 us (0.77)
  waiting for transfers between devices: 38.3 us -> 9.23 us
  other arithmetic: 14.9 us -> 1.52 us
  between operations: 14.2 us -> 1.49 us
  blocking collectives: 53.3 us -> 66 us
  Pallas kernels: 6.49 us -> 16.9 us
  starting transfers between devices: 29.5 us -> 25.3 us
  local copies, waits for them, and re-layouts: 8.03 us -> 5.84 us
    all_gather x1 -> x0, waiting for transfers between devices: 27.3 us -> none  [body(): column = lax.all_gather(by_slot, 'y', axis=0, tiled=True)]
    another operation x5 -> x0, other arithmetic: 12.1 us -> none  [the longest x3 6.51 us: body(): factor = jnp.linalg.cholesky(gram)]
    pallas_call x5 -> x7, Pallas kernels: 6.49 us -> 16.9 us  [call(): pl.pallas_call(kernel, out_shape=shapes, in_specs=specs, out_specs=(VMEM,...]
    unnamed x0 -> x1, blocking collectives: none -> 8.83 us
    all_to_all x1, waiting for transfers between devices: 4.45 us -> 0.03 us  [body(): lax.all_to_all(spread, INNER, 0, 0, tiled=True).reshape(half, 2 * vecs)]
    all_to_all x1, waiting for transfers between devices: 5.39 us -> 9.13 us  [body(): lax.all_to_all(jnp.broadcast_to(by_slot[None], (ys,) + by_slot.shape), 'y...]
    all_to_all x1, starting transfers between devices: 9.82 us -> 6.93 us  [body(): rows = lax.all_to_all(picked, INNER, 0, 0, tiled=True)]
    unnamed x18 -> x21, local copies, waits for them, and re-layouts: 7.13 us -> 4.58 us
  transfers between devices with their start and end apart: 6 -> 5, of which waited for: 5 -> 2; matrix products, arithmetic and copies ran while one was open for 6% -> 3% of each run, Pallas kernels for 0% -> 5%
where the time goes in v4:
time: 127 us; the launch traced here: 126 us
  blocking collectives  66 us (52%)
  starting transfers between devices  25.3 us (20%)
  Pallas kernels  16.9 us (13%)
  waiting for transfers between devices  9.23 us (7%)
  local copies, waits for them, and re-layouts  5.84 us (5%)
  other arithmetic  1.52 us (1%)
  between operations  1.49 us (1%)
    all_gather x1, blocking collectives, body(): lax.all_gather(call(gram_kernel, 'gram', f32(vecs // 2, 2 * vecs), [VMEM]...  25.8 us
    pallas_call x7, Pallas kernels, call(): pl.pallas_call(kernel, out_shape=shapes, in_specs=specs, out_specs=(VMEM,...  16.9 us
    all_to_all x1, blocking collectives, body(): received = lax.all_to_all(spread, ('y', 'rad'), 0, 0, tiled=True)  16.1 us
    all_to_all x1, blocking collectives, body(): received = lax.all_to_all(sent, INNER, 0, 0, tiled=True)  15.3 us
    all_to_all x1, waiting for transfers between devices, body(): lax.all_to_all(jnp.broadcast_to(by_slot[None], (ys,) + by_slot.shape), 'y...  9.13 us
    unnamed x1, blocking collectives  8.83 us
    all_to_all x1, starting transfers between devices, body(): lax.all_to_all(jnp.broadcast_to(by_slot[None], (ys,) + by_slot.shape), 'y...  7.65 us
    all_to_all x1, starting transfers between devices, body(): rows = lax.all_to_all(picked, INNER, 0, 0, tiled=True)  6.93 us
  transfers between devices with their start and end apart: 5, of which 2 were waited for; matrix products, arithmetic and copies ran while one was open for 3% of the time, Pallas kernels for 5%

profile of v4, /device:TPU:1, one launch (start us, length us, event | category | flops | bytes accessed | tf_op | source)
XLA Modules:
  0.0 126.2 jit_solution(3733365806309286889)
XLA Ops:
  0.6 0.0 copy-start.4
  0.6 0.0 copy-start.5
  0.7 0.0 copy-start.2
  0.7 0.0 copy-start.3
  0.7 0.0 copy-start.1
  0.7 0.0 copy-start.6
  0.7 1.0 copy.16
  1.6 1.1 broadcast_in_dim.32
  2.7 7.7 %all-to-all-start = ((bf16[8,4,64,256]{3,2,1,0:T(8,128)(2,1)}), bf16[8,4,64,256]{3,2,1,0:T(8,128)(2,1)S(1)}, u32[]{:S(2)}, u32[]{:S(2)}) async-start(bf16[8,4,64,256]{3,2,1,0:T(8,128)(2,1)} %broadcast_in_dim.32), calls=%async_computation | async-start | bytes 2097152 | tf_op jit(solution)/shard_map/all_to_all | solution.py:186
  10.4 0.1 fusion.31
  10.5 4.0 %collective-permute-start = (bf16[4,64,8]{2,1,0:T(8,128)(2,1)S(1)}, bf16[4,64,8]{2,1,0:T(8,128)(2,1)S(1)}, u32[]{:S(2)}, u32[]{:S(2)}) collective-permute-start(bf16[4,64,8]{2,1,0:T(8,128)(2,1)S(1)} %get-tuple-element.30), channel_id=1, source_target_pairs={{0,1},{1,2},{2,3},{3,4},{4,5},{5,6},{6,7},{8,9},{9,10},{10,11},{11... | collective-permute-start | bytes 12296 | tf_op jit(solution)/shard_map/ppermute | solution.py:191
  14.5 1.3 %collective-permute-start.1 = (bf16[4,64,8]{2,1,0:T(8,128)(2,1)S(1)}, bf16[4,64,8]{2,1,0:T(8,128)(2,1)S(1)}, u32[]{:S(2)}, u32[]{:S(2)}) collective-permute-start(bf16[4,64,8]{2,1,0:T(8,128)(2,1)S(1)} %get-tuple-element.31), channel_id=1, source_target_pairs={{1,0},{2,1},{3,2},{4,3},{5,4},{6,5},{7,6},{9,8},{10,9},{11,10},{12... | collective-permute-start | bytes 12296 | tf_op jit(solution)/shard_map/ppermute | solution.py:192
  15.8 0.0 copy-done.4
  15.8 0.0 copy-done.5
  15.8 0.0 copy-done.2
  15.8 0.2 select_reduce_fusion
  16.0 0.0 copy-done.3
  16.1 0.0 copy-done.1
  16.1 0.1 multiply_bitcast_fusion.15
  16.1 0.1 multiply_bitcast_fusion.16
  16.2 0.1 select_reduce_fusion.2
  16.3 1.3 %dynamic-slice = u32[1]{0:T(128)} dynamic-slice(u32[512]{0:T(512)} %constant.71, u32[]{:T(128)S(6)} %add.93), dynamic_slice_sizes={1} | dynamic-slice | bytes 12
  18.2 0.2 dynamic-update-slice
  18.5 8.8 %all-reduce = s32[512]{0:T(512)S(1)} all-reduce(s32[512]{0:T(512)S(1)} %dynamic-update-slice), channel_id=2, replica_groups=mesh['y'=8,'x'=4,'core'=2,'rad'=8] {'x','core'}, use_global_device_ids=true, to_apply=%add | all-reduce | flops 512 | bytes 4096
  27.3 0.1 reshape.128.need
  27.4 0.0 collective-permute-done
  27.4 0.0 collective-permute-done.1
  27.4 0.0 copy-done.6
  27.4 1.0 fusion.16.banded
  28.4 9.1 %all-to-all-done = bf16[8,4,64,256]{3,2,1,0:T(8,128)(2,1)S(1)} async-done(((bf16[8,4,64,256]{3,2,1,0:T(8,128)(2,1)}), bf16[8,4,64,256]{3,2,1,0:T(8,128)(2,1)S(1)}, u32[]{:S(2)}, u32[]{:S(2)}) %all-to-all-start) | async-done | bytes 1048608 | tf_op jit(solution)/shard_map/all_to_all | solution.py:186
  37.6 5.3 %pick.1 = bf16[64,64,256]{2,1,0:T(8,128)(2,1)S(1)} custom-call(s32[1]{0:T(128)} %bitcast.19.mine, s32[8,64]{1,0:T(8,128)S(1)} %reshape.128.need, bf16[32,64,256]{2,1,0:T(8,128)(2,1)S(1)} %bitcast.43), custom_call_target="tpu_custom_call" | custom-call | tf_op jit(solution)/shard_map/pick/pallas_call | solution.py:145
  42.9 0.0 copy-start
  42.9 1.3 %copy-done = bf16[64,64,256]{2,1,0:T(8,128)(2,1)} copy-done((bf16[64,64,256]{2,1,0:T(8,128)(2,1)}, bf16[64,64,256]{2,1,0:T(8,128)(2,1)S(1)}, u32[]{:S(2)}) %copy-start) | copy-done | bytes 2097176
  44.2 0.0 copy-start.7
  44.2 6.9 %all-to-all-start.1 = ((bf16[64,64,256]{2,1,0:T(8,128)(2,1)}), bf16[64,64,256]{2,1,0:T(8,128)(2,1)S(1)}, u32[]{:S(2)}, u32[]{:S(2)}) async-start(bf16[64,64,256]{2,1,0:T(8,128)(2,1)} %copy-done), calls=%async_computation.1 | async-start | bytes 4194304 | tf_op jit(solution)/shard_map/all_to_all | solution.py:214
  51.1 0.0 copy-done.7
  51.2 0.5 gram.1
  51.6 25.8 %all-gather.1 = f32[256,128]{1,0:T(8,128)S(1)} all-gather(f32[32,128]{1,0:T(8,128)S(1)} %gram.1), channel_id=3, replica_groups=mesh['y'=8,'x'=4,'core'=2,'rad'=8] {'rad'}, dimensions={0}, use_global_device_ids=true | all-gather | bytes 147456 | tf_op jit(solution)/shard_map/all_gather | solution.py:215
  77.4 0.1 all-to-all-done.1.rows
  77.5 4.2 %image.1 = (bf16[4,64,256]{2,1,0:T(8,128)(2,1)S(1)}, f32[8,36,128]{2,1,0:T(8,128)S(1)}) custom-call(s32[32]{0:T(128)S(1)} %multiply_add_fusion.slot, s32[32]{0:T(128)S(1)} %broadcast_subtract_fusion.target, f32[32]{0:T(128)S(1)} %compare_convert_fusion.9.live, bf16[64,64,256]{2,1,0:T(8,128)(2,1)S(1)} %all-to-all-done.1.rows, bf16[32,256,256]{2,1,0:T(8,128)(2,1)} %coupling.1, ...), custom_call_target="tpu_custom_call" | custom-call | tf_op jit(solution)/shard_map/image/pallas_call | solution.py:145
  81.7 15.3 %all_to_all.25.received = f32[8,36,128]{2,1,0:T(8,128)S(1)} all-to-all(f32[8,36,128]{2,1,0:T(8,128)S(1)} %get-tuple-element.16), channel_id=1, replica_groups=mesh['y'=8,'x'=4,'core'=2,'rad'=8] {'x','core'}, dimensions={0} | all-to-all | bytes 294912 | tf_op jit(solution)/shard_map/all_to_all | solution.py:239
  97.0 0.1 middle.1
  97.1 16.1 %all_to_all.26.received = f32[64,4,128]{2,1,0:T(4,128)S(1)} all-to-all(f32[64,4,128]{2,1,0:T(4,128)S(1)} %get-tuple-element.18), channel_id=1, replica_groups=mesh['y'=8,'x'=4,'core'=2,'rad'=8] {'y','rad'}, dimensions={0} | all-to-all | bytes 262144 | tf_op jit(solution)/shard_map/all_to_all | solution.py:243
  113.1 0.7 spread.1
  113.8 5.4 %all-to-all-start.4 = ((f32[8,4,128]{2,1,0:T(4,128)}), f32[8,4,128]{2,1,0:T(4,128)S(1)}, u32[]{:S(2)}, u32[]{:S(2)}) async-start(f32[8,4,128]{2,1,0:T(4,128)} %spread.1), calls=%async_computation.4 | async-start | bytes 32768 | tf_op jit(solution)/shard_map/all_to_all | solution.py:246
  119.3 5.3 %inverse.1 = f32[64,64]{1,0:T(8,128)S(1)} custom-call(f32[64,64]{1,0:T(8,128)S(1)} %get-tuple-element.17.square), custom_call_target="tpu_custom_call" | custom-call | tf_op jit(solution)/shard_map/inverse/pallas_call | solution.py:145
  124.6 0.0 all-to-all-done.4
  124.6 0.9 residual.1
  125.5 0.8 copy.14
  (6 shorter events, 0.0 us)
Async XLA Ops:
  0.6 15.2 %copy-start.4 = (s32[32]{0:T(128)S(1)}, s32[32]{0:T(128)}, u32[]{:S(2)}) copy-start(s32[32]{0:T(128)} %param.15) | copy-start | bytes 388
  0.6 15.2 %copy-start.5 = (s32[32]{0:T(128)S(1)}, s32[32]{0:T(128)}, u32[]{:S(2)}) copy-start(s32[32]{0:T(128)} %param.16) | copy-start | bytes 388
  0.7 15.2 %copy-start.2 = (s32[256]{0:T(256)S(1)}, s32[256]{0:T(256)}, u32[]{:S(2)}) copy-start(s32[256]{0:T(256)} %param.17) | copy-start | bytes 3076
  0.7 15.4 %copy-start.3 = (s32[4]{0:T(128)S(1)}, s32[4]{0:T(128)}, u32[]{:S(2)}) copy-start(s32[4]{0:T(128)} %param.11) | copy-start | bytes 52
  0.7 15.4 %copy-start.1 = (bf16[4,17,256]{2,0,1:T(4,128)(2,1)S(1)}, bf16[4,17,256]{2,0,1:T(4,128)(2,1)}, u32[]{:S(2)}) copy-start(bf16[4,17,256]{2,0,1:T(4,128)(2,1)} %param.10) | copy-start | bytes 104452
  0.7 26.7 %copy-start.6 = (f32[4]{0:T(128)S(1)}, f32[4]{0:T(128)}, u32[]{:S(2)}) copy-start(f32[4]{0:T(128)} %param.12) | copy-start | bytes 52
  2.7 34.8 %all-to-all-start = ((bf16[8,4,64,256]{3,2,1,0:T(8,128)(2,1)}), bf16[8,4,64,256]{3,2,1,0:T(8,128)(2,1)S(1)}, u32[]{:S(2)}, u32[]{:S(2)}) async-start(bf16[8,4,64,256]{3,2,1,0:T(8,128)(2,1)} %broadcast_in_dim.32), calls=%async_computation | async-start | bytes 2097152 | tf_op jit(solution)/shard_map/all_to_all | solution.py:186
  10.5 16.9 %collective-permute-start = (bf16[4,64,8]{2,1,0:T(8,128)(2,1)S(1)}, bf16[4,64,8]{2,1,0:T(8,128)(2,1)S(1)}, u32[]{:S(2)}, u32[]{:S(2)}) collective-permute-start(bf16[4,64,8]{2,1,0:T(8,128)(2,1)S(1)} %get-tuple-element.30), channel_id=1, source_target_pairs={{0,1},{1,2},{2,3},{3,4},{4,5},{5,6},{6,7},{8,9},{9,10},{10,11},{11... | collective-permute-start | bytes 12296 | tf_op jit(solution)/shard_map/ppermute | solution.py:191
  14.5 12.9 %collective-permute-start.1 = (bf16[4,64,8]{2,1,0:T(8,128)(2,1)S(1)}, bf16[4,64,8]{2,1,0:T(8,128)(2,1)S(1)}, u32[]{:S(2)}, u32[]{:S(2)}) collective-permute-start(bf16[4,64,8]{2,1,0:T(8,128)(2,1)S(1)} %get-tuple-element.31), channel_id=1, source_target_pairs={{1,0},{2,1},{3,2},{4,3},{5,4},{6,5},{7,6},{9,8},{10,9},{11,10},{12... | collective-permute-start | bytes 12296 | tf_op jit(solution)/shard_map/ppermute | solution.py:192
  42.9 1.3 %copy-start = (bf16[64,64,256]{2,1,0:T(8,128)(2,1)}, bf16[64,64,256]{2,1,0:T(8,128)(2,1)S(1)}, u32[]{:S(2)}) copy-start(bf16[64,64,256]{2,1,0:T(8,128)(2,1)S(1)} %pick.1) | copy-start | bytes 6291460
  44.2 7.0 %copy-start.7 = (s32[32]{0:T(128)S(1)}, s32[32]{0:T(128)}, u32[]{:S(2)}) copy-start(s32[32]{0:T(128)} %param.14) | copy-start | bytes 388
  44.2 33.3 %all-to-all-start.1 = ((bf16[64,64,256]{2,1,0:T(8,128)(2,1)}), bf16[64,64,256]{2,1,0:T(8,128)(2,1)S(1)}, u32[]{:S(2)}, u32[]{:S(2)}) async-start(bf16[64,64,256]{2,1,0:T(8,128)(2,1)} %copy-done), calls=%async_computation.1 | async-start | bytes 4194304 | tf_op jit(solution)/shard_map/all_to_all | solution.py:214
  113.8 10.8 %all-to-all-start.4 = ((f32[8,4,128]{2,1,0:T(4,128)}), f32[8,4,128]{2,1,0:T(4,128)S(1)}, u32[]{:S(2)}, u32[]{:S(2)}) async-start(f32[8,4,128]{2,1,0:T(4,128)} %spread.1), calls=%async_computation.4 | async-start | bytes 32768 | tf_op jit(solution)/shard_map/all_to_all | solution.py:246

commit v5 on v4

--- a/solution.py
+++ b/solution.py
@@ -11,7 +11,7 @@
 BLK = 256
 CORES = 2
 X_CHIPS = 4
-UNROLL = 8
+CHUNK = 8
 INNER = ("x", "core")
 CHAN = ("y", "x", "core")
 VMEM = pl.BlockSpec(memory_space=pltpu.VMEM)
@@ -40,24 +40,17 @@
     return acc
 
 
-def pick_kernel(mine, need, rows, out, sems):
+def pick_kernel(mine, need, rows, out):
     receivers = need.shape[0]
     groups = out.shape[0] // receivers
     per_group = rows.shape[0] // groups
     columns = need.shape[1] // groups
 
-    def copy(i):
-        receiver, group = lax.div(i, groups), lax.rem(i, groups)
-        chosen = group * per_group + need[receiver, group * columns + mine[0]]
-        return pltpu.make_async_copy(rows.at[chosen], out.at[i], sems.at[i])
-
-    @pl.loop(0, out.shape[0])
-    def _(i):
-        copy(i).start()
-
-    @pl.loop(0, out.shape[0])
-    def _(i):
-        copy(i).wait()
+    @pl.loop(0, receivers)
+    def _(receiver):
+        for group in range(groups):
+            chosen = group * per_group + need[receiver, group * columns + mine[0]]
+            out[receiver * groups + group] = rows[chosen]
 
 
 def gram_kernel(rows, gram):
@@ -78,22 +71,22 @@
     inverse[...] = value
 
 
-def image_kernel(slot, target, live, rows, coupling, banded, trial, gram, image, sent, total, held, sems):
-    def copy(p):
-        return pltpu.make_async_copy(coupling.at[p], held.at[p], sems.at[p])
-
-    @pl.loop(0, coupling.shape[0])
-    def _(p):
-        copy(p).start()
-
+def image_kernel(
+    slot, target, live, rows, coupling, banded, trial, image, sent, total, held, sems
+):
+    def copy(chunk):
+        part = pl.ds(chunk * CHUNK, CHUNK)
+        return pltpu.make_async_copy(coupling.at[part], held.at[part], sems.at[chunk])
+
+    for chunk in range(sems.shape[0]):
+        copy(chunk).start()
     total[...] = banded[...]
 
-    @pl.loop(0, coupling.shape[0], step=UNROLL)
-    def _(first):
-        for i in range(UNROLL):
-            copy(first + i).wait()
-        for i in range(UNROLL):
-            p = first + i
+    @pl.loop(0, sems.shape[0])
+    def _(chunk):
+        copy(chunk).wait()
+        for i in range(CHUNK):
+            p = chunk * CHUNK + i
             part = lax.dot_general(
                 rows[slot[p]], held[p], NT, preferred_element_type=jnp.float32
             )
@@ -104,26 +97,29 @@
         rounded = total[c].astype(jnp.bfloat16)
         image[c] = rounded
         acc += lax.dot_general(trial[c], rounded, NT, preferred_element_type=jnp.float32)
-    packed = pack(acc)
-    summed = jnp.sum(gram[...], axis=0)
-    piece = sent.shape[1] - summed.shape[0]
-    for j in range(sent.shape[0]):
-        sent[j, :piece] = packed[j * piece : (j + 1) * piece]
-        sent[j, piece:] = summed
-
-
-def middle_kernel(received, spread, gram):
-    whole = jnp.sum(received[...], axis=0)
-    piece = spread.shape[1]
-    for j in range(spread.shape[0]):
-        spread[j] = whole[:piece]
-    gram[...] = unpack(whole[piece:])
-
-
-def spread_kernel(received, spread):
-    whole = jnp.sum(received[...], axis=0)
+    sent[...] = pack(acc)
+
+
+def middle_kernel(received, gram, spread):
+    whole = jnp.concatenate([gram[...], jnp.sum(received[...], axis=0)], axis=0)
     for j in range(spread.shape[0]):
         spread[j] = whole
+
+
+def last_kernel(received, spread, gram):
+    piece = spread.shape[1]
+    part = received.shape[1] - piece
+    count = gram.shape[0] // 2 // part
+    over_x = received.shape[0] // count
+    found = []
+    for y in range(count):
+        found.append(jnp.sum(received[y * over_x : (y + 1) * over_x], axis=0))
+    whole = found[0][part:]
+    for y in range(1, count):
+        whole += found[y][part:]
+    for j in range(spread.shape[0]):
+        spread[j] = whole
+    gram[...] = unpack(jnp.concatenate([f[:part] for f in found], axis=0))
 
 
 def residual_kernel(inverse, projected, trial, image, residual, rayleigh):
@@ -140,13 +136,13 @@
         residual[c] = (image[c].astype(jnp.float32) - fit).astype(jnp.bfloat16)
 
 
-def call(kernel, name, shapes, specs, *operands, out=VMEM, scratch=(), limit=40):
+def call(kernel, name, shapes, specs, *operands, scratch=(), limit=40):
     several = isinstance(shapes, tuple)
     return pl.pallas_call(
         kernel,
         out_shape=shapes,
         in_specs=specs,
-        out_specs=(VMEM,) * len(shapes) if several else out,
+        out_specs=(VMEM,) * len(shapes) if several else VMEM,
         scratch_shapes=scratch,
         compiler_params=pltpu.CompilerParams(vmem_limit_bytes=limit * MIB),
         name=name,
@@ -180,7 +176,6 @@
     need = jnp.sum(jnp.where(hit, member[:, None], 0), axis=0)
     needed = lax.all_gather(need, INNER)
     slot = lax.rem(group, columns) * ys + group // columns
-    live = (lax.axis_index("rad") < reach).astype(jnp.float32)
 
     by_slot = jnp.transpose(trial, (1, 0, 2))
     column = lax.all_to_all(
@@ -200,50 +195,53 @@
     column, banded = lax.optimization_barrier((column, banded))
     mine = (lax.axis_index("x") * cores + lax.axis_index("core")).reshape(1)
     picked = call(
-        pick_kernel,
-        "pick",
-        bf16(columns * ys, vecs, slab),
-        [SMEM, SMEM, ANY],
-        mine,
-        needed,
-        column,
-        out=ANY,
-        scratch=[pltpu.SemaphoreType.DMA((columns * ys,))],
+        pick_kernel, "pick", bf16(columns * ys, vecs, slab), [SMEM, SMEM, VMEM], mine, needed, column
     )
     column, picked = lax.optimization_barrier((column, picked))
     rows = lax.all_to_all(picked, INNER, 0, 0, tiled=True)
-    gram = lax.all_gather(call(gram_kernel, "gram", f32(vecs // 2, 2 * vecs), [VMEM], column), "rad")
-
     half = vecs // 2
-    piece = half // columns
+    gram = call(gram_kernel, "gram", f32(half, 2 * vecs), [VMEM], column)
+    gram = lax.dynamic_slice_in_dim(gram, lax.axis_index("y") * (half // ys), half // ys)
+    gram = lax.psum(lax.psum(gram, "core"), "rad")
+    rows, gram = lax.optimization_barrier((rows, gram))
+
     image, sent = call(
         image_kernel,
         "image",
-        (bf16(*by_slot.shape), f32(columns, piece + half, 2 * vecs)),
-        [SMEM] * 3 + [VMEM, ANY] + [VMEM] * 3,
+        (bf16(*by_slot.shape), f32(half, 2 * vecs)),
+        [SMEM] * 3 + [VMEM, ANY] + [VMEM] * 2,
         slot,
         target_local,
-        live,
+        (lax.axis_index("rad") < reach).astype(jnp.float32),
         rows,
         coupling,
         banded,
         by_slot,
-        gram,
         scratch=[
             pltpu.VMEM(by_slot.shape, jnp.float32),
             pltpu.VMEM(coupling.shape, jnp.bfloat16),
-            pltpu.SemaphoreType.DMA(coupling.shape[:1]),
+            pltpu.SemaphoreType.DMA((coupling.shape[0] // CHUNK,)),
         ],
         limit=50,
     )
-    received = lax.all_to_all(sent, INNER, 0, 0, tiled=True)
+    shared = cores * slabs
+    piece = half // shared
+    sent = sent.reshape(shared, piece, 2 * vecs)
+    received = lax.all_to_all(sent, ("core", "rad"), 0, 0, tiled=True)
+    spread = call(
+        middle_kernel,
+        "middle",
+        f32(ys * xs, half // ys + piece, 2 * vecs),
+        [VMEM, VMEM],
+        received,
+        gram,
+    )
+    received = lax.all_to_all(spread, ("y", "x"), 0, 0, tiled=True)
     spread, gram = call(
-        middle_kernel, "middle", (f32(ys * slabs, piece, 2 * vecs), f32(vecs, vecs)), [VMEM], received
-    )
-    received = lax.all_to_all(spread, ("y", "rad"), 0, 0, tiled=True)
+        last_kernel, "last", (f32(shared, piece, 2 * vecs), f32(vecs, vecs)), [VMEM], received
+    )
     inverse = call(inverse_kernel, "inverse", f32(vecs, vecs), [VMEM], gram)
-    spread = call(spread_kernel, "spread", f32(columns, piece, 2 * vecs), [VMEM], received)
-    projected = lax.all_to_all(spread, INNER, 0, 0, tiled=True).reshape(half, 2 * vecs)
+    projected = lax.all_to_all(spread, ("core", "rad"), 0, 0, tiled=True).reshape(half, 2 * vecs)
     residual, rayleigh = call(
         residual_kernel,
         "residual",

time: 127 us -> 122 us (0.961)
  Pallas kernels: 16.9 us -> 12 us
  waiting for transfers between devices: 9.23 us -> 13.5 us
  blocking collectives: 66 us -> 62.3 us
    all_gather x1 -> x0, blocking collectives: 25.8 us -> none  [body(): lax.all_gather(call(gram_kernel, 'gram', f32(vecs // 2, 2 * vecs), [VMEM]...]
    psum x0 -> x2, blocking collectives: none -> 23.1 us  [body(): gram = lax.psum(lax.psum(gram, 'core'), 'rad')]
    pallas_call x7, Pallas kernels: 16.9 us -> 12 us  [call(): pl.pallas_call(kernel, out_shape=shapes, in_specs=specs, out_specs=(VMEM,...]
    all_to_all x1, waiting for transfers between devices: 0.06 us -> 2.72 us  [body(): rows = lax.all_to_all(picked, INNER, 0, 0, tiled=True)]
    all_to_all x1, waiting for transfers between devices: 0.03 us -> 1.62 us  [body(): lax.all_to_all(spread, ('core', 'rad'), 0, 0, tiled=True)]
  transfers between devices with their start and end apart: 5 -> 5, of which waited for: 2 -> 3; matrix products, arithmetic and copies ran while one was open for 3% -> 3% of each run, Pallas kernels for 5% -> 5%
where the time goes in v5:
time: 122 us
  blocking collectives  62.3 us (51%)
  starting transfers between devices  25.3 us (21%)
  waiting for transfers between devices  13.5 us (11%)
  Pallas kernels  12 us (10%)
  local copies, waits for them, and re-layouts  5.88 us (5%)
  other arithmetic  1.52 us (1%)
  between operations  1.5 us (1%)
    psum x2, blocking collectives, body(): gram = lax.psum(lax.psum(gram, 'core'), 'rad')  23.1 us
    all_to_all x1, blocking collectives, body(): received = lax.all_to_all(sent, ('core', 'rad'), 0, 0, tiled=True)  18 us
    all_to_all x1, blocking collectives, body(): received = lax.all_to_all(spread, ('y', 'x'), 0, 0, tiled=True)  12.4 us
    pallas_call x7, Pallas kernels, call(): pl.pallas_call(kernel, out_shape=shapes, in_specs=specs, out_specs=(VMEM,...  12 us
    all_to_all x1, waiting for transfers between devices, body(): lax.all_to_all(jnp.broadcast_to(by_slot[None], (ys,) + by_slot.shape), 'y...  9.13 us
    unnamed x1, blocking collectives  8.83 us
    all_to_all x1, starting transfers between devices, body(): lax.all_to_all(jnp.broadcast_to(by_slot[None], (ys,) + by_slot.shape), 'y...  7.65 us
    all_to_all x1, starting transfers between devices, body(): rows = lax.all_to_all(picked, INNER, 0, 0, tiled=True)  6.93 us
  transfers between devices with their start and end apart: 5, of which 3 were waited for; matrix products, arithmetic and copies ran while one was open for 3% of the time, Pallas kernels for 5%

profile of v5, /device:TPU:1, one launch (start us, length us, event | category | flops | bytes accessed | tf_op | source)
XLA Modules:
  0.0 121.9 jit_solution(6408675413380474628)
XLA Ops:
  0.6 0.0 copy-start.4
  0.6 0.0 copy-start.5
  0.7 0.0 copy-start.2
  0.7 0.0 copy-start.3
  0.7 0.0 copy-start.1
  0.7 0.0 copy-start.6
  0.7 1.0 copy.16
  1.6 1.1 broadcast_in_dim.32
  2.7 7.7 %all-to-all-start = ((bf16[8,4,64,256]{3,2,1,0:T(8,128)(2,1)}), bf16[8,4,64,256]{3,2,1,0:T(8,128)(2,1)S(1)}, u32[]{:S(2)}, u32[]{:S(2)}) async-start(bf16[8,4,64,256]{3,2,1,0:T(8,128)(2,1)} %broadcast_in_dim.32), calls=%async_computation | async-start | bytes 2097152 | tf_op jit(solution)/shard_map/all_to_all | solution.py:181
  10.4 0.1 fusion.31
  10.5 4.0 %collective-permute-start = (bf16[4,64,8]{2,1,0:T(8,128)(2,1)S(1)}, bf16[4,64,8]{2,1,0:T(8,128)(2,1)S(1)}, u32[]{:S(2)}, u32[]{:S(2)}) collective-permute-start(bf16[4,64,8]{2,1,0:T(8,128)(2,1)S(1)} %get-tuple-element.34), channel_id=1, source_target_pairs={{0,1},{1,2},{2,3},{3,4},{4,5},{5,6},{6,7},{8,9},{9,10},{10,11},{11... | collective-permute-start | bytes 12296 | tf_op jit(solution)/shard_map/ppermute | solution.py:186
  14.5 1.3 %collective-permute-start.1 = (bf16[4,64,8]{2,1,0:T(8,128)(2,1)S(1)}, bf16[4,64,8]{2,1,0:T(8,128)(2,1)S(1)}, u32[]{:S(2)}, u32[]{:S(2)}) collective-permute-start(bf16[4,64,8]{2,1,0:T(8,128)(2,1)S(1)} %get-tuple-element.35), channel_id=1, source_target_pairs={{1,0},{2,1},{3,2},{4,3},{5,4},{6,5},{7,6},{9,8},{10,9},{11,10},{12... | collective-permute-start | bytes 12296 | tf_op jit(solution)/shard_map/ppermute | solution.py:187
  15.8 0.0 copy-done.4
  15.8 0.0 copy-done.5
  15.8 0.0 copy-done.2
  15.8 0.2 select_reduce_fusion
  16.0 0.0 copy-done.3
  16.0 0.0 copy-done.1
  16.1 0.1 multiply_bitcast_fusion.15
  16.1 0.1 multiply_bitcast_fusion.16
  16.2 0.1 select_reduce_fusion.2
  16.3 1.3 %dynamic-slice = u32[1]{0:T(128)} dynamic-slice(u32[512]{0:T(512)} %constant.73, u32[]{:T(128)S(6)} %add.101), dynamic_slice_sizes={1} | dynamic-slice | bytes 12
  18.2 0.2 dynamic-update-slice
  18.5 8.8 %all-reduce = s32[512]{0:T(512)S(1)} all-reduce(s32[512]{0:T(512)S(1)} %dynamic-update-slice), channel_id=2, replica_groups=mesh['y'=8,'x'=4,'core'=2,'rad'=8] {'x','core'}, use_global_device_ids=true, to_apply=%add | all-reduce | flops 512 | bytes 4096
  27.3 0.1 reshape.132.need
  27.4 0.0 collective-permute-done
  27.4 0.0 collective-permute-done.1
  27.4 0.0 copy-done.6
  27.4 1.0 fusion.16.banded
  28.4 9.1 %all-to-all-done = bf16[8,4,64,256]{3,2,1,0:T(8,128)(2,1)S(1)} async-done(((bf16[8,4,64,256]{3,2,1,0:T(8,128)(2,1)}), bf16[8,4,64,256]{3,2,1,0:T(8,128)(2,1)S(1)}, u32[]{:S(2)}, u32[]{:S(2)}) %all-to-all-start) | async-done | bytes 1048608 | tf_op jit(solution)/shard_map/all_to_all | solution.py:181
  37.6 0.8 pick.1
  38.4 0.0 copy-start
  38.4 1.3 %copy-done = bf16[64,64,256]{2,1,0:T(8,128)(2,1)} copy-done((bf16[64,64,256]{2,1,0:T(8,128)(2,1)}, bf16[64,64,256]{2,1,0:T(8,128)(2,1)S(1)}, u32[]{:S(2)}) %copy-start) | copy-done | bytes 2097176
  39.7 0.0 copy-start.7
  39.8 6.9 %all-to-all-start.1 = ((bf16[64,64,256]{2,1,0:T(8,128)(2,1)}), bf16[64,64,256]{2,1,0:T(8,128)(2,1)S(1)}, u32[]{:S(2)}, u32[]{:S(2)}) async-start(bf16[64,64,256]{2,1,0:T(8,128)(2,1)} %copy-done), calls=%async_computation.1 | async-start | bytes 4194304 | tf_op jit(solution)/shard_map/all_to_all | solution.py:201
  46.7 0.0 copy-done.7
  46.7 0.5 gram.1
  47.2 2.5 %psum.14 = f32[4,128]{1,0:T(4,128)S(1)} all-reduce(f32[4,128]{1,0:T(4,128)S(1)} %constant_dynamic-slice_fusion), channel_id=1, replica_groups=mesh['y'=8,'x'=4,'core'=2,'rad'=8] {'core'}, use_global_device_ids=true, to_apply=%region_3.4 | all-reduce | flops 512 | bytes 4096 | tf_op jit(solution)/shard_map/psum | solution.py:205
  49.7 20.6 %psum.15.gram = f32[4,128]{1,0:T(4,128)S(1)} all-reduce(f32[4,128]{1,0:T(4,128)S(1)} %psum.14), channel_id=1, replica_groups=mesh['y'=8,'x'=4,'core'=2,'rad'=8] {'rad'}, use_global_device_ids=true, to_apply=%region_4.5 | all-reduce | flops 512 | bytes 4096 | tf_op jit(solution)/shard_map/psum | solution.py:205
  70.3 2.7 %all-to-all-done.1.rows = bf16[64,64,256]{2,1,0:T(8,128)(2,1)S(1)} async-done(((bf16[64,64,256]{2,1,0:T(8,128)(2,1)}), bf16[64,64,256]{2,1,0:T(8,128)(2,1)S(1)}, u32[]{:S(2)}, u32[]{:S(2)}) %all-to-all-start.1) | async-done | bytes 2097184 | tf_op jit(solution)/shard_map/all_to_all | solution.py:201
  73.0 3.9 %image.1 = (bf16[4,64,256]{2,1,0:T(8,128)(2,1)S(1)}, f32[32,128]{1,0:T(8,128)S(1)}) custom-call(s32[32]{0:T(128)S(1)} %multiply_add_fusion.slot, s32[32]{0:T(128)S(1)} %broadcast_subtract_fusion.target, f32[32]{0:T(128)S(1)} %compare_convert_fusion.9.live, bf16[64,64,256]{2,1,0:T(8,128)(2,1)S(1)} %all-to-all-done.1.rows, bf16[32,256,256]{2,1,0:T(8,128)(2,1)} %coupling.1, ...), custom_call_target="tpu_custom_call" | custom-call | tf_op jit(solution)/shard_map/image/pallas_call | solution.py:141
  76.9 18.0 %all_to_all.25.received = f32[16,2,128]{2,1,0:T(2,128)S(1)} all-to-all(f32[16,2,128]{2,1,0:T(2,128)S(1)} %bitcast.52), channel_id=1, replica_groups=mesh['y'=8,'x'=4,'core'=2,'rad'=8] {'core','rad'}, dimensions={0} | all-to-all | bytes 32768 | tf_op jit(solution)/shard_map/all_to_all | solution.py:230
  94.9 12.4 %all_to_all.26.received = f32[32,6,128]{2,1,0:T(8,128)S(1)} all-to-all(f32[32,6,128]{2,1,0:T(8,128)S(1)} %middle.1), channel_id=1, replica_groups=mesh['y'=8,'x'=4,'core'=2,'rad'=8] {'y','x'}, dimensions={0} | all-to-all | bytes 196608 | tf_op jit(solution)/shard_map/all_to_all | solution.py:239
  107.4 0.6 last.1
  108.0 5.4 %all-to-all-start.4 = ((f32[16,2,128]{2,1,0:T(2,128)}), f32[16,2,128]{2,1,0:T(2,128)S(1)}, u32[]{:S(2)}, u32[]{:S(2)}) async-start(f32[16,2,128]{2,1,0:T(2,128)} %get-tuple-element.22), calls=%async_computation.4 | async-start | bytes 32768 | tf_op jit(solution)/shard_map/all_to_all | solution.py:244
  113.4 5.3 %inverse.1 = f32[64,64]{1,0:T(8,128)S(1)} custom-call(f32[64,64]{1,0:T(8,128)S(1)} %get-tuple-element.21.square), custom_call_target="tpu_custom_call" | custom-call | tf_op jit(solution)/shard_map/inverse/pallas_call | solution.py:141
  118.7 1.6 %all-to-all-done.4 = f32[16,2,128]{2,1,0:T(2,128)S(1)} async-done(((f32[16,2,128]{2,1,0:T(2,128)}), f32[16,2,128]{2,1,0:T(2,128)S(1)}, u32[]{:S(2)}, u32[]{:S(2)}) %all-to-all-start.4) | async-done | bytes 16416 | tf_op jit(solution)/shard_map/all_to_all | solution.py:244
  120.3 0.9 residual.1
  121.2 0.8 copy.14
  (8 shorter events, 0.1 us)
Async XLA Ops:
  0.6 15.2 %copy-start.4 = (s32[32]{0:T(128)S(1)}, s32[32]{0:T(128)}, u32[]{:S(2)}) copy-start(s32[32]{0:T(128)} %param.15) | copy-start | bytes 388
  0.6 15.2 %copy-start.5 = (s32[32]{0:T(128)S(1)}, s32[32]{0:T(128)}, u32[]{:S(2)}) copy-start(s32[32]{0:T(128)} %param.16) | copy-start | bytes 388
  0.7 15.2 %copy-start.2 = (s32[256]{0:T(256)S(1)}, s32[256]{0:T(256)}, u32[]{:S(2)}) copy-start(s32[256]{0:T(256)} %param.17) | copy-start | bytes 3076
  0.7 15.4 %copy-start.3 = (s32[4]{0:T(128)S(1)}, s32[4]{0:T(128)}, u32[]{:S(2)}) copy-start(s32[4]{0:T(128)} %param.11) | copy-start | bytes 52
  0.7 15.4 %copy-start.1 = (bf16[4,17,256]{2,0,1:T(4,128)(2,1)S(1)}, bf16[4,17,256]{2,0,1:T(4,128)(2,1)}, u32[]{:S(2)}) copy-start(bf16[4,17,256]{2,0,1:T(4,128)(2,1)} %param.10) | copy-start | bytes 104452
  0.7 26.7 %copy-start.6 = (f32[4]{0:T(128)S(1)}, f32[4]{0:T(128)}, u32[]{:S(2)}) copy-start(f32[4]{0:T(128)} %param.12) | copy-start | bytes 52
  2.7 34.8 %all-to-all-start = ((bf16[8,4,64,256]{3,2,1,0:T(8,128)(2,1)}), bf16[8,4,64,256]{3,2,1,0:T(8,128)(2,1)S(1)}, u32[]{:S(2)}, u32[]{:S(2)}) async-start(bf16[8,4,64,256]{3,2,1,0:T(8,128)(2,1)} %broadcast_in_dim.32), calls=%async_computation | async-start | bytes 2097152 | tf_op jit(solution)/shard_map/all_to_all | solution.py:181
  10.5 16.9 %collective-permute-start = (bf16[4,64,8]{2,1,0:T(8,128)(2,1)S(1)}, bf16[4,64,8]{2,1,0:T(8,128)(2,1)S(1)}, u32[]{:S(2)}, u32[]{:S(2)}) collective-permute-start(bf16[4,64,8]{2,1,0:T(8,128)(2,1)S(1)} %get-tuple-element.34), channel_id=1, source_target_pairs={{0,1},{1,2},{2,3},{3,4},{4,5},{5,6},{6,7},{8,9},{9,10},{10,11},{11... | collective-permute-start | bytes 12296 | tf_op jit(solution)/shard_map/ppermute | solution.py:186
  14.5 12.9 %collective-permute-start.1 = (bf16[4,64,8]{2,1,0:T(8,128)(2,1)S(1)}, bf16[4,64,8]{2,1,0:T(8,128)(2,1)S(1)}, u32[]{:S(2)}, u32[]{:S(2)}) collective-permute-start(bf16[4,64,8]{2,1,0:T(8,128)(2,1)S(1)} %get-tuple-element.35), channel_id=1, source_target_pairs={{1,0},{2,1},{3,2},{4,3},{5,4},{6,5},{7,6},{9,8},{10,9},{11,10},{12... | collective-permute-start | bytes 12296 | tf_op jit(solution)/shard_map/ppermute | solution.py:187
  38.4 1.3 %copy-start = (bf16[64,64,256]{2,1,0:T(8,128)(2,1)}, bf16[64,64,256]{2,1,0:T(8,128)(2,1)S(1)}, u32[]{:S(2)}) copy-start(bf16[64,64,256]{2,1,0:T(8,128)(2,1)S(1)} %pick.1) | copy-start | bytes 6291460
  39.7 7.0 %copy-start.7 = (s32[32]{0:T(128)S(1)}, s32[32]{0:T(128)}, u32[]{:S(2)}) copy-start(s32[32]{0:T(128)} %param.14) | copy-start | bytes 388
  39.8 33.3 %all-to-all-start.1 = ((bf16[64,64,256]{2,1,0:T(8,128)(2,1)}), bf16[64,64,256]{2,1,0:T(8,128)(2,1)S(1)}, u32[]{:S(2)}, u32[]{:S(2)}) async-start(bf16[64,64,256]{2,1,0:T(8,128)(2,1)} %copy-done), calls=%async_computation.1 | async-start | bytes 4194304 | tf_op jit(solution)/shard_map/all_to_all | solution.py:201
  108.0 12.3 %all-to-all-start.4 = ((f32[16,2,128]{2,1,0:T(2,128)}), f32[16,2,128]{2,1,0:T(2,128)S(1)}, u32[]{:S(2)}, u32[]{:S(2)}) async-start(f32[16,2,128]{2,1,0:T(2,128)} %get-tuple-element.22), calls=%async_computation.4 | async-start | bytes 32768 | tf_op jit(solution)/shard_map/all_to_all | solution.py:244

commit v6 on v5

--- a/solution.py
+++ b/solution.py
@@ -11,7 +11,7 @@
 BLK = 256
 CORES = 2
 X_CHIPS = 4
-CHUNK = 8
+CHUNK = 4
 INNER = ("x", "core")
 CHAN = ("y", "x", "core")
 VMEM = pl.BlockSpec(memory_space=pltpu.VMEM)
@@ -40,21 +40,27 @@
     return acc
 
 
-def pick_kernel(mine, need, rows, out):
+def pick_kernel(mine, need, *refs):
+    *parts, out, rows = refs
+    count = len(parts)
+    for s, part in enumerate(parts):
+        rows[lax.rem(mine[1] - s + count, count)] = part[...]
     receivers = need.shape[0]
-    groups = out.shape[0] // receivers
-    per_group = rows.shape[0] // groups
-    columns = need.shape[1] // groups
+    columns = need.shape[1] // count
 
     @pl.loop(0, receivers)
     def _(receiver):
-        for group in range(groups):
-            chosen = group * per_group + need[receiver, group * columns + mine[0]]
-            out[receiver * groups + group] = rows[chosen]
-
-
-def gram_kernel(rows, gram):
-    gram[...] = pack(gram_of(rows))
+        for group in range(count):
+            chosen = need[receiver, group * columns + mine[0]]
+            out[receiver * count + group] = rows[group, chosen]
+
+
+def gram_kernel(*refs):
+    *parts, gram = refs
+    acc = gram_of(parts[0])
+    for part in parts[1:]:
+        acc += gram_of(part)
+    gram[...] = pack(acc)
 
 
 def inverse_kernel(square, inverse):
@@ -178,9 +184,9 @@
     slot = lax.rem(group, columns) * ys + group // columns
 
     by_slot = jnp.transpose(trial, (1, 0, 2))
-    column = lax.all_to_all(
-        jnp.broadcast_to(by_slot[None], (ys,) + by_slot.shape), "y", 0, 0, tiled=True
-    ).reshape(ys * slots, vecs, slab)
+    column = [by_slot] * ys
+    for s in sorted(range(1, ys), key=lambda s: min(s, ys - s), reverse=True):
+        column[s] = lax.ppermute(by_slot, "y", [(i, (i + s) % ys) for i in range(ys)])
 
     up = [(i, i + 1) for i in range(slabs - 1)]
     before = lax.ppermute(by_slot[:, :, slab - BW :], "rad", up)
@@ -193,14 +199,23 @@
         banded += weight[:, None] * padded[:, :, offset : offset + slab].astype(jnp.float32)
 
     column, banded = lax.optimization_barrier((column, banded))
-    mine = (lax.axis_index("x") * cores + lax.axis_index("core")).reshape(1)
+    mine = jnp.stack(
+        [lax.axis_index("x") * cores + lax.axis_index("core"), lax.axis_index("y")]
+    )
     picked = call(
-        pick_kernel, "pick", bf16(columns * ys, vecs, slab), [SMEM, SMEM, VMEM], mine, needed, column
+        pick_kernel,
+        "pick",
+        bf16(columns * ys, vecs, slab),
+        [SMEM, SMEM] + [VMEM] * ys,
+        mine,
+        needed,
+        *column,
+        scratch=[pltpu.VMEM((ys,) + by_slot.shape, jnp.bfloat16)],
     )
     column, picked = lax.optimization_barrier((column, picked))
     rows = lax.all_to_all(picked, INNER, 0, 0, tiled=True)
     half = vecs // 2
-    gram = call(gram_kernel, "gram", f32(half, 2 * vecs), [VMEM], column)
+    gram = call(gram_kernel, "gram", f32(half, 2 * vecs), [VMEM] * ys, *column)
     gram = lax.dynamic_slice_in_dim(gram, lax.axis_index("y") * (half // ys), half // ys)
     gram = lax.psum(lax.psum(gram, "core"), "rad")
     rows, gram = lax.optimization_barrier((rows, gram))

time: 122 us -> 149 us (1.22)
  starting transfers between devices: 25.3 us -> 45.1 us
  other arithmetic: 1.52 us -> 5.2 us
  blocking collectives: 62.3 us -> 65.4 us
    ppermute x0 -> x7, starting transfers between devices: none -> 29.2 us  [body(): lax.ppermute(by_slot, 'y', [(i, (i + s) % ys) for i in range(ys)])]
    ppermute x0 -> x7, waiting for transfers between devices: none -> 10.3 us  [body(): lax.ppermute(by_slot, 'y', [(i, (i + s) % ys) for i in range(ys)])]
    all_to_all x1 -> x0, waiting for transfers between devices: 9.13 us -> none  [body(): lax.all_to_all(jnp.broadcast_to(by_slot[None], (ys,) + by_slot.shape), 'y...]
    all_to_all x1 -> x0, starting transfers between devices: 7.65 us -> none  [body(): lax.all_to_all(jnp.broadcast_to(by_slot[None], (ys,) + by_slot.shape), 'y...]
    all_to_all x1, starting transfers between devices: 6.93 us -> 5.09 us  [body(): rows = lax.all_to_all(picked, INNER, 0, 0, tiled=True)]
    mul x2, other arithmetic: 0.15 us -> 1.74 us  [body(): weight[:, None] * padded[:, :, offset:offset + slab].astype(jnp.float32)]
    unnamed x21 -> x9, local copies, waits for them, and re-layouts: 4.6 us -> 4.54 us
  transfers between devices with their start and end apart: 5 -> 11, of which waited for: 3 -> 5; matrix products, arithmetic and copies ran while one was open for 3% -> 5% of each run, Pallas kernels for 5% -> 4%
where the time goes in v6:
time: 149 us
  blocking collectives  65.4 us (44%)
  starting transfers between devices  45.1 us (30%)
  waiting for transfers between devices  14.4 us (10%)
  Pallas kernels  12.5 us (8%)
  other arithmetic  5.2 us (3%)
  local copies, waits for them, and re-layouts  4.73 us (3%)
  between operations  1.5 us (1%)
    ppermute x7, starting transfers between devices, body(): lax.ppermute(by_slot, 'y', [(i, (i + s) % ys) for i in range(ys)])  29.2 us
    psum x2, blocking collectives, body(): gram = lax.psum(lax.psum(gram, 'core'), 'rad')  23.3 us
    all_to_all x1, blocking collectives, body(): received = lax.all_to_all(sent, ('core', 'rad'), 0, 0, tiled=True)  19.5 us
    all_to_all x1, blocking collectives, body(): received = lax.all_to_all(spread, ('y', 'x'), 0, 0, tiled=True)  13.8 us
    pallas_call x7, Pallas kernels, call(): pl.pallas_call(kernel, out_shape=shapes, in_specs=specs, out_specs=(VMEM,...  12.5 us
    ppermute x7, waiting for transfers between devices, body(): lax.ppermute(by_slot, 'y', [(i, (i + s) % ys) for i in range(ys)])  10.3 us
    unnamed x1, blocking collectives  8.8 us
    all_to_all x1, starting transfers between devices, body(): lax.all_to_all(spread, ('core', 'rad'), 0, 0, tiled=True)  5.47 us
  transfers between devices with their start and end apart: 11, of which 5 were waited for; matrix products, arithmetic and copies ran while one was open for 5% of the time, Pallas kernels for 4%

profile of v6, /device:TPU:1, one launch (start us, length us, event | category | flops | bytes accessed | tf_op | source)
XLA Modules:
  0.0 148.8 jit_solution(1896677724570302634)
XLA Ops:
  0.6 0.9 copy.16
  1.6 4.0 %collective-permute-start = (bf16[4,64,256]{2,1,0:T(8,128)(2,1)S(1)}, bf16[4,64,256]{2,1,0:T(8,128)(2,1)S(1)}, u32[]{:S(2)}, u32[]{:S(2)}) collective-permute-start(bf16[4,64,256]{2,1,0:T(8,128)(2,1)S(1)} %bitcast.43), channel_id=1, source_target_pairs={{0,64},{64,128},{128,192},{192,256},{256,320},{320,384},{384,448},... | collective-permute-start | bytes 393224 | tf_op jit(solution)/shard_map/ppermute | solution.py:189
  5.6 4.2 %collective-permute-start.1 = (bf16[4,64,256]{2,1,0:T(8,128)(2,1)S(1)}, bf16[4,64,256]{2,1,0:T(8,128)(2,1)S(1)}, u32[]{:S(2)}, u32[]{:S(2)}) collective-permute-start(bf16[4,64,256]{2,1,0:T(8,128)(2,1)S(1)} %bitcast.44), channel_id=1, source_target_pairs={{0,128},{64,192},{128,256},{192,320},{256,384},{320,448},{384,0},{... | collective-permute-start | bytes 393224 | tf_op jit(solution)/shard_map/ppermute | solution.py:189
  9.8 4.6 %collective-permute-start.2 = (bf16[4,64,256]{2,1,0:T(8,128)(2,1)S(1)}, bf16[4,64,256]{2,1,0:T(8,128)(2,1)S(1)}, u32[]{:S(2)}, u32[]{:S(2)}) collective-permute-start(bf16[4,64,256]{2,1,0:T(8,128)(2,1)S(1)} %bitcast.45), channel_id=1, source_target_pairs={{0,192},{64,256},{128,320},{192,384},{256,448},{320,0},{384,64},{4... | collective-permute-start | bytes 393224 | tf_op jit(solution)/shard_map/ppermute | solution.py:189
  14.5 0.1 fusion.31
  14.6 4.0 %collective-permute-start.7 = (bf16[4,64,8]{2,1,0:T(8,128)(2,1)S(1)}, bf16[4,64,8]{2,1,0:T(8,128)(2,1)S(1)}, u32[]{:S(2)}, u32[]{:S(2)}) collective-permute-start(bf16[4,64,8]{2,1,0:T(8,128)(2,1)S(1)} %get-tuple-element.62), channel_id=1, source_target_pairs={{0,1},{1,2},{2,3},{3,4},{4,5},{5,6},{6,7},{8,9},{9,10},{10,11},{11... | collective-permute-start | bytes 12296 | tf_op jit(solution)/shard_map/ppermute | solution.py:192
  18.6 1.3 collective-permute-start.8
  19.9 0.7 compare_convert_fusion
  20.5 0.9 select_reduce_fusion
  21.4 0.8 multiply_bitcast_fusion.15
  22.3 0.9 multiply_bitcast_fusion.16
  23.2 0.1 select_reduce_fusion.2
  23.3 0.1 pad_add_fusion.mine
  23.3 1.3 dynamic-slice
  25.3 0.2 dynamic-update-slice
  25.5 8.8 %all-reduce = s32[512]{0:T(512)S(1)} all-reduce(s32[512]{0:T(512)S(1)} %dynamic-update-slice), channel_id=2, replica_groups=mesh['y'=8,'x'=4,'core'=2,'rad'=8] {'x','core'}, use_global_device_ids=true, to_apply=%add | all-reduce | flops 512 | bytes 4096
  34.3 0.1 reshape.123.need
  34.4 0.0 collective-permute-done.7
  34.4 3.5 %collective-permute-start.3 = (bf16[4,64,256]{2,1,0:T(8,128)(2,1)S(1)}, bf16[4,64,256]{2,1,0:T(8,128)(2,1)S(1)}, u32[]{:S(2)}, u32[]{:S(2)}) collective-permute-start(bf16[4,64,256]{2,1,0:T(8,128)(2,1)S(1)} %bitcast.47), channel_id=1, source_target_pairs={{0,256},{64,320},{128,384},{192,448},{256,0},{320,64},{384,128},{4... | collective-permute-start | bytes 393224 | tf_op jit(solution)/shard_map/ppermute | solution.py:189
  37.9 0.0 collective-permute-done.8
  37.9 4.9 %collective-permute-start.4 = (bf16[4,64,256]{2,1,0:T(8,128)(2,1)S(1)}, bf16[4,64,256]{2,1,0:T(8,128)(2,1)S(1)}, u32[]{:S(2)}, u32[]{:S(2)}) collective-permute-start(bf16[4,64,256]{2,1,0:T(8,128)(2,1)S(1)} %bitcast.48), channel_id=1, source_target_pairs={{0,320},{64,384},{128,448},{192,0},{256,64},{320,128},{384,192},{4... | collective-permute-start | bytes 393224 | tf_op jit(solution)/shard_map/ppermute | solution.py:189
  42.8 0.0 collective-permute-done.refs_1_
  42.8 5.0 %collective-permute-start.5 = (bf16[4,64,256]{2,1,0:T(8,128)(2,1)S(1)}, bf16[4,64,256]{2,1,0:T(8,128)(2,1)S(1)}, u32[]{:S(2)}, u32[]{:S(2)}) collective-permute-start(bf16[4,64,256]{2,1,0:T(8,128)(2,1)S(1)} %bitcast.49), channel_id=1, source_target_pairs={{0,384},{64,448},{128,0},{192,64},{256,128},{320,192},{384,256},{4... | collective-permute-start | bytes 393224 | tf_op jit(solution)/shard_map/ppermute | solution.py:189
  47.8 0.0 collective-permute-done.1.refs_2_
  47.8 3.0 %collective-permute-start.6 = (bf16[4,64,256]{2,1,0:T(8,128)(2,1)S(1)}, bf16[4,64,256]{2,1,0:T(8,128)(2,1)S(1)}, u32[]{:S(2)}, u32[]{:S(2)}) collective-permute-start(bf16[4,64,256]{2,1,0:T(8,128)(2,1)S(1)} %bitcast.50), channel_id=1, source_target_pairs={{0,448},{64,0},{128,64},{192,128},{256,192},{320,256},{384,320},{4... | collective-permute-start | bytes 393224 | tf_op jit(solution)/shard_map/ppermute | solution.py:189
  50.8 1.7 %fusion.16.banded = f32[4,64,256]{2,1,0:T(8,128)S(1)} fusion(bf16[4,64,256]{2,1,0:T(8,128)(2,1)S(1)} %bitcast.51, bf16[4,64,8]{2,1,0:T(8,128)(2,1)S(1)} %collective-permute-done.8, bf16[4,64,8]{2,1,0:T(8,128)(2,1)S(1)} %collective-permute-done.7, f32[4,256]{1,0:T(4,128)S(1)} %get-tuple-element.65, f32[4,256]{1,0:T(4,128)S(1)} %get-tuple-element.67, ...), kind=kLoop, calls=%fused_computation.32 | loop fusion | flops 6553600 | bytes 471056 | tf_op jit(solution)/shard_map/add | solution.py:199
  52.5 0.0 collective-permute-done.2.refs_3_
  52.5 0.0 collective-permute-done.3.refs_4_
  52.5 3.2 %collective-permute-done.4.refs_5_ = bf16[4,64,256]{2,1,0:T(8,128)(2,1)S(1)} collective-permute-done((bf16[4,64,256]{2,1,0:T(8,128)(2,1)S(1)}, bf16[4,64,256]{2,1,0:T(8,128)(2,1)S(1)}, u32[]{:S(2)}, u32[]{:S(2)}) %collective-permute-start.4) | collective-permute-done | bytes 131104 | tf_op jit(solution)/shard_map/ppermute | solution.py:189
  55.7 5.7 %collective-permute-done.5.refs_6_ = bf16[4,64,256]{2,1,0:T(8,128)(2,1)S(1)} collective-permute-done((bf16[4,64,256]{2,1,0:T(8,128)(2,1)S(1)}, bf16[4,64,256]{2,1,0:T(8,128)(2,1)S(1)}, u32[]{:S(2)}, u32[]{:S(2)}) %collective-permute-start.5) | collective-permute-done | bytes 131104 | tf_op jit(solution)/shard_map/ppermute | solution.py:189
  61.4 1.4 collective-permute-done.6.refs_7_
  62.8 0.9 pick.1
  63.7 0.0 copy-start
  63.7 1.3 copy-done
  65.1 0.0 copy-start.1
  65.1 5.1 %all-to-all-start = ((bf16[64,64,256]{2,1,0:T(8,128)(2,1)}), bf16[64,64,256]{2,1,0:T(8,128)(2,1)S(1)}, u32[]{:S(2)}, u32[]{:S(2)}) async-start(bf16[64,64,256]{2,1,0:T(8,128)(2,1)} %copy-done), calls=%async_computation | async-start | bytes 4194304 | tf_op jit(solution)/shard_map/all_to_all | solution.py:216
  70.2 0.0 copy-done.1
  70.2 0.5 gram.1
  70.7 2.5 %psum.14 = f32[4,128]{1,0:T(4,128)S(1)} all-reduce(f32[4,128]{1,0:T(4,128)S(1)} %constant_dynamic-slice_fusion), channel_id=1, replica_groups=mesh['y'=8,'x'=4,'core'=2,'rad'=8] {'core'}, use_global_device_ids=true, to_apply=%region_3.4 | all-reduce | flops 512 | bytes 4096 | tf_op jit(solution)/shard_map/psum | solution.py:220
  73.2 20.9 %psum.15.gram = f32[4,128]{1,0:T(4,128)S(1)} all-reduce(f32[4,128]{1,0:T(4,128)S(1)} %psum.14), channel_id=1, replica_groups=mesh['y'=8,'x'=4,'core'=2,'rad'=8] {'rad'}, use_global_device_ids=true, to_apply=%region_4.5 | all-reduce | flops 512 | bytes 4096 | tf_op jit(solution)/shard_map/psum | solution.py:220
  94.0 2.5 %all-to-all-done.rows = bf16[64,64,256]{2,1,0:T(8,128)(2,1)S(1)} async-done(((bf16[64,64,256]{2,1,0:T(8,128)(2,1)}), bf16[64,64,256]{2,1,0:T(8,128)(2,1)S(1)}, u32[]{:S(2)}, u32[]{:S(2)}) %all-to-all-start) | async-done | bytes 2097184 | tf_op jit(solution)/shard_map/all_to_all | solution.py:216
  96.5 4.3 %image.1 = (bf16[4,64,256]{2,1,0:T(8,128)(2,1)S(1)}, f32[32,128]{1,0:T(8,128)S(1)}) custom-call(s32[32]{0:T(128)S(1)} %multiply_add_fusion.slot, s32[32]{0:T(128)S(1)} %broadcast_subtract_fusion.target, f32[32]{0:T(128)S(1)} %compare_convert_fusion.9.live, bf16[64,64,256]{2,1,0:T(8,128)(2,1)S(1)} %all-to-all-done.rows, bf16[32,256,256]{2,1,0:T(8,128)(2,1)} %coupling.1, ...), custom_call_target="tpu_custom_call" | custom-call | tf_op jit(solution)/shard_map/image/pallas_call | solution.py:147
  100.8 19.5 %all_to_all.20.received = f32[16,2,128]{2,1,0:T(2,128)S(1)} all-to-all(f32[16,2,128]{2,1,0:T(2,128)S(1)} %bitcast.58), channel_id=1, replica_groups=mesh['y'=8,'x'=4,'core'=2,'rad'=8] {'core','rad'}, dimensions={0} | all-to-all | bytes 32768 | tf_op jit(solution)/shard_map/all_to_all | solution.py:245
  120.3 13.8 %all_to_all.21.received = f32[32,6,128]{2,1,0:T(8,128)S(1)} all-to-all(f32[32,6,128]{2,1,0:T(8,128)S(1)} %middle.1), channel_id=1, replica_groups=mesh['y'=8,'x'=4,'core'=2,'rad'=8] {'y','x'}, dimensions={0} | all-to-all | bytes 196608 | tf_op jit(solution)/shard_map/all_to_all | solution.py:254
  134.1 0.6 last.1
  134.7 5.5 %all-to-all-start.3 = ((f32[16,2,128]{2,1,0:T(2,128)}), f32[16,2,128]{2,1,0:T(2,128)S(1)}, u32[]{:S(2)}, u32[]{:S(2)}) async-start(f32[16,2,128]{2,1,0:T(2,128)} %get-tuple-element.50), calls=%async_computation.3 | async-start | bytes 32768 | tf_op jit(solution)/shard_map/all_to_all | solution.py:259
  140.2 5.3 %inverse.1 = f32[64,64]{1,0:T(8,128)S(1)} custom-call(f32[64,64]{1,0:T(8,128)S(1)} %get-tuple-element.49.square), custom_call_target="tpu_custom_call" | custom-call | tf_op jit(solution)/shard_map/inverse/pallas_call | solution.py:147
  145.5 1.6 %all-to-all-done.3 = f32[16,2,128]{2,1,0:T(2,128)S(1)} async-done(((f32[16,2,128]{2,1,0:T(2,128)}), f32[16,2,128]{2,1,0:T(2,128)S(1)}, u32[]{:S(2)}, u32[]{:S(2)}) %all-to-all-start.3) | async-done | bytes 16416 | tf_op jit(solution)/shard_map/all_to_all | solution.py:259
  147.1 0.9 residual.1
  148.0 0.8 copy.14
  (7 shorter events, 0.1 us)
Async XLA Ops:
  1.6 41.3 %collective-permute-start = (bf16[4,64,256]{2,1,0:T(8,128)(2,1)S(1)}, bf16[4,64,256]{2,1,0:T(8,128)(2,1)S(1)}, u32[]{:S(2)}, u32[]{:S(2)}) collective-permute-start(bf16[4,64,256]{2,1,0:T(8,128)(2,1)S(1)} %bitcast.43), channel_id=1, source_target_pairs={{0,64},{64,128},{128,192},{192,256},{256,320},{320,384},{384,448},... | collective-permute-start | bytes 393224 | tf_op jit(solution)/shard_map/ppermute | solution.py:189
  5.6 42.2 %collective-permute-start.1 = (bf16[4,64,256]{2,1,0:T(8,128)(2,1)S(1)}, bf16[4,64,256]{2,1,0:T(8,128)(2,1)S(1)}, u32[]{:S(2)}, u32[]{:S(2)}) collective-permute-start(bf16[4,64,256]{2,1,0:T(8,128)(2,1)S(1)} %bitcast.44), channel_id=1, source_target_pairs={{0,128},{64,192},{128,256},{192,320},{256,384},{320,448},{384,0},{... | collective-permute-start | bytes 393224 | tf_op jit(solution)/shard_map/ppermute | solution.py:189
  9.8 42.7 %collective-permute-start.2 = (bf16[4,64,256]{2,1,0:T(8,128)(2,1)S(1)}, bf16[4,64,256]{2,1,0:T(8,128)(2,1)S(1)}, u32[]{:S(2)}, u32[]{:S(2)}) collective-permute-start(bf16[4,64,256]{2,1,0:T(8,128)(2,1)S(1)} %bitcast.45), channel_id=1, source_target_pairs={{0,192},{64,256},{128,320},{192,384},{256,448},{320,0},{384,64},{4... | collective-permute-start | bytes 393224 | tf_op jit(solution)/shard_map/ppermute | solution.py:189
  14.6 19.8 %collective-permute-start.7 = (bf16[4,64,8]{2,1,0:T(8,128)(2,1)S(1)}, bf16[4,64,8]{2,1,0:T(8,128)(2,1)S(1)}, u32[]{:S(2)}, u32[]{:S(2)}) collective-permute-start(bf16[4,64,8]{2,1,0:T(8,128)(2,1)S(1)} %get-tuple-element.62), channel_id=1, source_target_pairs={{0,1},{1,2},{2,3},{3,4},{4,5},{5,6},{6,7},{8,9},{9,10},{10,11},{11... | collective-permute-start | bytes 12296 | tf_op jit(solution)/shard_map/ppermute | solution.py:192
  18.6 19.4 %collective-permute-start.8 = (bf16[4,64,8]{2,1,0:T(8,128)(2,1)S(1)}, bf16[4,64,8]{2,1,0:T(8,128)(2,1)S(1)}, u32[]{:S(2)}, u32[]{:S(2)}) collective-permute-start(bf16[4,64,8]{2,1,0:T(8,128)(2,1)S(1)} %get-tuple-element.63), channel_id=1, source_target_pairs={{1,0},{2,1},{3,2},{4,3},{5,4},{6,5},{7,6},{9,8},{10,9},{11,10},{12... | collective-permute-start | bytes 12296 | tf_op jit(solution)/shard_map/ppermute | solution.py:193
  34.4 18.1 %collective-permute-start.3 = (bf16[4,64,256]{2,1,0:T(8,128)(2,1)S(1)}, bf16[4,64,256]{2,1,0:T(8,128)(2,1)S(1)}, u32[]{:S(2)}, u32[]{:S(2)}) collective-permute-start(bf16[4,64,256]{2,1,0:T(8,128)(2,1)S(1)} %bitcast.47), channel_id=1, source_target_pairs={{0,256},{64,320},{128,384},{192,448},{256,0},{320,64},{384,128},{4... | collective-permute-start | bytes 393224 | tf_op jit(solution)/shard_map/ppermute | solution.py:189
  37.9 17.8 %collective-permute-start.4 = (bf16[4,64,256]{2,1,0:T(8,128)(2,1)S(1)}, bf16[4,64,256]{2,1,0:T(8,128)(2,1)S(1)}, u32[]{:S(2)}, u32[]{:S(2)}) collective-permute-start(bf16[4,64,256]{2,1,0:T(8,128)(2,1)S(1)} %bitcast.48), channel_id=1, source_target_pairs={{0,320},{64,384},{128,448},{192,0},{256,64},{320,128},{384,192},{4... | collective-permute-start | bytes 393224 | tf_op jit(solution)/shard_map/ppermute | solution.py:189
  42.8 18.6 %collective-permute-start.5 = (bf16[4,64,256]{2,1,0:T(8,128)(2,1)S(1)}, bf16[4,64,256]{2,1,0:T(8,128)(2,1)S(1)}, u32[]{:S(2)}, u32[]{:S(2)}) collective-permute-start(bf16[4,64,256]{2,1,0:T(8,128)(2,1)S(1)} %bitcast.49), channel_id=1, source_target_pairs={{0,384},{64,448},{128,0},{192,64},{256,128},{320,192},{384,256},{4... | collective-permute-start | bytes 393224 | tf_op jit(solution)/shard_map/ppermute | solution.py:189
  47.8 15.0 %collective-permute-start.6 = (bf16[4,64,256]{2,1,0:T(8,128)(2,1)S(1)}, bf16[4,64,256]{2,1,0:T(8,128)(2,1)S(1)}, u32[]{:S(2)}, u32[]{:S(2)}) collective-permute-start(bf16[4,64,256]{2,1,0:T(8,128)(2,1)S(1)} %bitcast.50), channel_id=1, source_target_pairs={{0,448},{64,0},{128,64},{192,128},{256,192},{320,256},{384,320},{4... | collective-permute-start | bytes 393224 | tf_op jit(solution)/shard_map/ppermute | solution.py:189
  63.7 1.4 copy-start
  65.1 5.1 %copy-start.1 = (s32[32]{0:T(128)S(1)}, s32[32]{0:T(128)}, u32[]{:S(2)}) copy-start(s32[32]{0:T(128)} %param.14) | copy-start | bytes 388
  65.1 31.4 %all-to-all-start = ((bf16[64,64,256]{2,1,0:T(8,128)(2,1)}), bf16[64,64,256]{2,1,0:T(8,128)(2,1)S(1)}, u32[]{:S(2)}, u32[]{:S(2)}) async-start(bf16[64,64,256]{2,1,0:T(8,128)(2,1)} %copy-done), calls=%async_computation | async-start | bytes 4194304 | tf_op jit(solution)/shard_map/all_to_all | solution.py:216
  134.7 12.4 %all-to-all-start.3 = ((f32[16,2,128]{2,1,0:T(2,128)}), f32[16,2,128]{2,1,0:T(2,128)S(1)}, u32[]{:S(2)}, u32[]{:S(2)}) async-start(f32[16,2,128]{2,1,0:T(2,128)} %get-tuple-element.50), calls=%async_computation.3 | async-start | bytes 32768 | tf_op jit(solution)/shard_map/all_to_all | solution.py:259

commit v7 on v5

--- a/solution.py
+++ b/solution.py
@@ -62,12 +62,21 @@
     down = lax.broadcasted_iota(jnp.int32, (size, size), 0)
     across = lax.broadcasted_iota(jnp.int32, (size, size), 1)
     value = square[...]
-    for k in range(size):
-        scale = 1.0 / value[k : k + 1, k : k + 1]
-        row = jnp.where(across[:1] == k, 1.0, value[k : k + 1]) * scale
-        column = jnp.where(down[:, :1] == k, -1.0, value[:, k : k + 1])
-        rest = jnp.where((down == k) | (across == k), 0.0, value)
-        value = rest - column * row
+    for k in range(0, size, 2):
+        at = [across[:1] == k, across[:1] == k + 1]
+        first = 1.0 / value[k : k + 1, k : k + 1]
+        beside = value[k : k + 1, k + 1 : k + 2]
+        below = value[k + 1 : k + 2, k : k + 1] * first
+        second = 1.0 / (value[k + 1 : k + 2, k + 1 : k + 2] - below * beside)
+        top = jnp.where(at[0], 1.0, jnp.where(at[1], 0.0, value[k : k + 1]))
+        low = jnp.where(at[0], 0.0, jnp.where(at[1], 1.0, value[k + 1 : k + 2]))
+        low = (low - below * top) * second
+        top = (top - beside * low) * first
+        here = [down[:, :1] == k, down[:, :1] == k + 1]
+        left = jnp.where(here[0], -1.0, jnp.where(here[1], 0.0, value[:, k : k + 1]))
+        right = jnp.where(here[0], 0.0, jnp.where(here[1], -1.0, value[:, k + 1 : k + 2]))
+        pivots = (down // 2 == k // 2) | (across // 2 == k // 2)
+        value = jnp.where(pivots, 0.0, value) - left * top - right * low
     inverse[...] = value
 
 
@@ -195,7 +204,7 @@
     column, banded = lax.optimization_barrier((column, banded))
     mine = (lax.axis_index("x") * cores + lax.axis_index("core")).reshape(1)
     picked = call(
-        pick_kernel, "pick", bf16(columns * ys, vecs, slab), [SMEM, SMEM, VMEM], mine, needed, column
+        pick_kernel, "pick", pltpu.HBM((columns * ys, vecs, slab), jnp.bfloat16), [SMEM, SMEM, VMEM], mine, needed, column
     )
     column, picked = lax.optimization_barrier((column, picked))
     rows = lax.all_to_all(picked, INNER, 0, 0, tiled=True)

time: 122 us -> 123 us (level)
  Pallas kernels: 12 us -> 15.4 us
  waiting for transfers between devices: 13.5 us -> 11.9 us
  local copies, waits for them, and re-layouts: 5.88 us -> 4.54 us
    pallas_call x7, Pallas kernels: 12 us -> 15.4 us  [call(): pl.pallas_call(kernel, out_shape=shapes, in_specs=specs, out_specs=(VMEM,...]
    all_to_all x1, waiting for transfers between devices: 1.62 us -> 0.01 us  [body(): lax.all_to_all(spread, ('core', 'rad'), 0, 0, tiled=True)]
    unnamed x21 -> x19, local copies, waits for them, and re-layouts: 4.6 us -> 3.26 us
  transfers between devices with their start and end apart: 5 -> 5, of which waited for: 3 -> 2; matrix products, arithmetic and copies ran while one was open for 3% -> 3% of each run, Pallas kernels for 5% -> 6%
where the time goes in v7:
time: 123 us; the launch traced here: 122 us
  blocking collectives  62.3 us (51%)
  starting transfers between devices  25.3 us (21%)
  Pallas kernels  15.4 us (13%)
  waiting for transfers between devices  11.9 us (10%)
  local copies, waits for them, and re-layouts  4.54 us (4%)
  other arithmetic  1.52 us (1%)
  between operations  1.49 us (1%)
    psum x2, blocking collectives, body(): gram = lax.psum(lax.psum(gram, 'core'), 'rad')  23.1 us
    all_to_all x1, blocking collectives, body(): received = lax.all_to_all(sent, ('core', 'rad'), 0, 0, tiled=True)  18 us
    pallas_call x7, Pallas kernels, call(): pl.pallas_call(kernel, out_shape=shapes, in_specs=specs, out_specs=(VMEM,...  15.4 us
    all_to_all x1, blocking collectives, body(): received = lax.all_to_all(spread, ('y', 'x'), 0, 0, tiled=True)  12.4 us
    all_to_all x1, waiting for transfers between devices, body(): lax.all_to_all(jnp.broadcast_to(by_slot[None], (ys,) + by_slot.shape), 'y...  9.13 us
    unnamed x1, blocking collectives  8.83 us
    all_to_all x1, starting transfers between devices, body(): lax.all_to_all(jnp.broadcast_to(by_slot[None], (ys,) + by_slot.shape), 'y...  7.65 us
    all_to_all x1, starting transfers between devices, body(): rows = lax.all_to_all(picked, INNER, 0, 0, tiled=True)  6.93 us
  transfers between devices with their start and end apart: 5, of which 2 were waited for; matrix products, arithmetic and copies ran while one was open for 3% of the time, Pallas kernels for 6%

profile of v7, /device:TPU:1, one launch (start us, length us, event | category | flops | bytes accessed | tf_op | source)
XLA Modules:
  0.0 122.4 jit_solution(4366799658070745454)
XLA Ops:
  0.6 0.0 copy-start.3
  0.6 0.0 copy-start.4
  0.7 0.0 copy-start.1
  0.7 0.0 copy-start.2
  0.7 0.0 copy-start
  0.7 0.0 copy-start.5
  0.7 1.0 copy.16
  1.6 1.1 broadcast_in_dim.32
  2.7 7.7 %all-to-all-start = ((bf16[8,4,64,256]{3,2,1,0:T(8,128)(2,1)}), bf16[8,4,64,256]{3,2,1,0:T(8,128)(2,1)S(1)}, u32[]{:S(2)}, u32[]{:S(2)}) async-start(bf16[8,4,64,256]{3,2,1,0:T(8,128)(2,1)} %broadcast_in_dim.32), calls=%async_computation | async-start | bytes 2097152 | tf_op jit(solution)/shard_map/all_to_all | solution.py:190
  10.4 0.1 fusion.31
  10.5 4.0 %collective-permute-start = (bf16[4,64,8]{2,1,0:T(8,128)(2,1)S(1)}, bf16[4,64,8]{2,1,0:T(8,128)(2,1)S(1)}, u32[]{:S(2)}, u32[]{:S(2)}) collective-permute-start(bf16[4,64,8]{2,1,0:T(8,128)(2,1)S(1)} %get-tuple-element.34), channel_id=1, source_target_pairs={{0,1},{1,2},{2,3},{3,4},{4,5},{5,6},{6,7},{8,9},{9,10},{10,11},{11... | collective-permute-start | bytes 12296 | tf_op jit(solution)/shard_map/ppermute | solution.py:195
  14.5 1.3 %collective-permute-start.1 = (bf16[4,64,8]{2,1,0:T(8,128)(2,1)S(1)}, bf16[4,64,8]{2,1,0:T(8,128)(2,1)S(1)}, u32[]{:S(2)}, u32[]{:S(2)}) collective-permute-start(bf16[4,64,8]{2,1,0:T(8,128)(2,1)S(1)} %get-tuple-element.35), channel_id=1, source_target_pairs={{1,0},{2,1},{3,2},{4,3},{5,4},{6,5},{7,6},{9,8},{10,9},{11,10},{12... | collective-permute-start | bytes 12296 | tf_op jit(solution)/shard_map/ppermute | solution.py:196
  15.8 0.0 copy-done.3
  15.8 0.0 copy-done.4
  15.8 0.0 copy-done.1
  15.8 0.2 select_reduce_fusion
  16.0 0.0 copy-done.2
  16.0 0.0 copy-done
  16.1 0.1 multiply_bitcast_fusion.15
  16.1 0.1 multiply_bitcast_fusion.16
  16.2 0.1 select_reduce_fusion.2
  16.3 1.3 %dynamic-slice = u32[1]{0:T(128)} dynamic-slice(u32[512]{0:T(512)} %constant.73, u32[]{:T(128)S(6)} %add.101), dynamic_slice_sizes={1} | dynamic-slice | bytes 12
  18.2 0.2 dynamic-update-slice
  18.5 8.8 %all-reduce = s32[512]{0:T(512)S(1)} all-reduce(s32[512]{0:T(512)S(1)} %dynamic-update-slice), channel_id=2, replica_groups=mesh['y'=8,'x'=4,'core'=2,'rad'=8] {'x','core'}, use_global_device_ids=true, to_apply=%add | all-reduce | flops 512 | bytes 4096
  27.3 0.1 reshape.132.need
  27.4 0.0 collective-permute-done
  27.4 0.0 collective-permute-done.1
  27.4 0.0 copy-done.5
  27.4 1.0 fusion.16.banded
  28.4 9.1 %all-to-all-done = bf16[8,4,64,256]{3,2,1,0:T(8,128)(2,1)S(1)} async-done(((bf16[8,4,64,256]{3,2,1,0:T(8,128)(2,1)}), bf16[8,4,64,256]{3,2,1,0:T(8,128)(2,1)S(1)}, u32[]{:S(2)}, u32[]{:S(2)}) %all-to-all-start) | async-done | bytes 1048608 | tf_op jit(solution)/shard_map/all_to_all | solution.py:190
  37.6 2.2 %pick.1 = bf16[64,64,256]{2,1,0:T(8,128)(2,1)} custom-call(s32[1]{0:T(128)} %bitcast.19.mine, s32[8,64]{1,0:T(8,128)S(1)} %reshape.132.need, bf16[32,64,256]{2,1,0:T(8,128)(2,1)S(1)} %bitcast.43), custom_call_target="tpu_custom_call" | custom-call | tf_op jit(solution)/shard_map/pick/pallas_call | solution.py:150
  39.8 0.0 copy-start.6
  39.8 6.9 %all-to-all-start.1 = ((bf16[64,64,256]{2,1,0:T(8,128)(2,1)}), bf16[64,64,256]{2,1,0:T(8,128)(2,1)S(1)}, u32[]{:S(2)}, u32[]{:S(2)}) async-start(bf16[64,64,256]{2,1,0:T(8,128)(2,1)} %pick.1), calls=%async_computation.1 | async-start | bytes 4194304 | tf_op jit(solution)/shard_map/all_to_all | solution.py:210
  46.7 0.0 copy-done.6
  46.7 0.5 gram.1
  47.2 2.5 %psum.14 = f32[4,128]{1,0:T(4,128)S(1)} all-reduce(f32[4,128]{1,0:T(4,128)S(1)} %constant_dynamic-slice_fusion), channel_id=1, replica_groups=mesh['y'=8,'x'=4,'core'=2,'rad'=8] {'core'}, use_global_device_ids=true, to_apply=%region_3.4 | all-reduce | flops 512 | bytes 4096 | tf_op jit(solution)/shard_map/psum | solution.py:214
  49.7 20.6 %psum.15.gram = f32[4,128]{1,0:T(4,128)S(1)} all-reduce(f32[4,128]{1,0:T(4,128)S(1)} %psum.14), channel_id=1, replica_groups=mesh['y'=8,'x'=4,'core'=2,'rad'=8] {'rad'}, use_global_device_ids=true, to_apply=%region_4.5 | all-reduce | flops 512 | bytes 4096 | tf_op jit(solution)/shard_map/psum | solution.py:214
  70.3 2.7 %all-to-all-done.1.rows = bf16[64,64,256]{2,1,0:T(8,128)(2,1)S(1)} async-done(((bf16[64,64,256]{2,1,0:T(8,128)(2,1)}), bf16[64,64,256]{2,1,0:T(8,128)(2,1)S(1)}, u32[]{:S(2)}, u32[]{:S(2)}) %all-to-all-start.1) | async-done | bytes 2097184 | tf_op jit(solution)/shard_map/all_to_all | solution.py:210
  73.0 3.9 %image.1 = (bf16[4,64,256]{2,1,0:T(8,128)(2,1)S(1)}, f32[32,128]{1,0:T(8,128)S(1)}) custom-call(s32[32]{0:T(128)S(1)} %multiply_add_fusion.slot, s32[32]{0:T(128)S(1)} %broadcast_subtract_fusion.target, f32[32]{0:T(128)S(1)} %compare_convert_fusion.9.live, bf16[64,64,256]{2,1,0:T(8,128)(2,1)S(1)} %all-to-all-done.1.rows, bf16[32,256,256]{2,1,0:T(8,128)(2,1)} %coupling.1, ...), custom_call_target="tpu_custom_call" | custom-call | tf_op jit(solution)/shard_map/image/pallas_call | solution.py:150
  76.9 18.0 %all_to_all.25.received = f32[16,2,128]{2,1,0:T(2,128)S(1)} all-to-all(f32[16,2,128]{2,1,0:T(2,128)S(1)} %bitcast.52), channel_id=1, replica_groups=mesh['y'=8,'x'=4,'core'=2,'rad'=8] {'core','rad'}, dimensions={0} | all-to-all | bytes 32768 | tf_op jit(solution)/shard_map/all_to_all | solution.py:239
  94.9 12.4 %all_to_all.26.received = f32[32,6,128]{2,1,0:T(8,128)S(1)} all-to-all(f32[32,6,128]{2,1,0:T(8,128)S(1)} %middle.1), channel_id=1, replica_groups=mesh['y'=8,'x'=4,'core'=2,'rad'=8] {'y','x'}, dimensions={0} | all-to-all | bytes 196608 | tf_op jit(solution)/shard_map/all_to_all | solution.py:248
  107.4 0.6 last.1
  108.0 5.4 %all-to-all-start.4 = ((f32[16,2,128]{2,1,0:T(2,128)}), f32[16,2,128]{2,1,0:T(2,128)S(1)}, u32[]{:S(2)}, u32[]{:S(2)}) async-start(f32[16,2,128]{2,1,0:T(2,128)} %get-tuple-element.22), calls=%async_computation.4 | async-start | bytes 32768 | tf_op jit(solution)/shard_map/all_to_all | solution.py:253
  113.4 7.4 %inverse.1 = f32[64,64]{1,0:T(8,128)S(1)} custom-call(f32[64,64]{1,0:T(8,128)S(1)} %get-tuple-element.21.square), custom_call_target="tpu_custom_call" | custom-call | tf_op jit(solution)/shard_map/inverse/pallas_call | solution.py:150
  120.8 0.0 all-to-all-done.4
  120.8 0.9 residual.1
  121.6 0.8 copy.14
  (8 shorter events, 0.1 us)
Async XLA Ops:
  0.6 15.2 %copy-start.3 = (s32[32]{0:T(128)S(1)}, s32[32]{0:T(128)}, u32[]{:S(2)}) copy-start(s32[32]{0:T(128)} %param.15) | copy-start | bytes 388
  0.6 15.2 %copy-start.4 = (s32[32]{0:T(128)S(1)}, s32[32]{0:T(128)}, u32[]{:S(2)}) copy-start(s32[32]{0:T(128)} %param.16) | copy-start | bytes 388
  0.7 15.2 %copy-start.1 = (s32[256]{0:T(256)S(1)}, s32[256]{0:T(256)}, u32[]{:S(2)}) copy-start(s32[256]{0:T(256)} %param.17) | copy-start | bytes 3076
  0.7 15.4 %copy-start.2 = (s32[4]{0:T(128)S(1)}, s32[4]{0:T(128)}, u32[]{:S(2)}) copy-start(s32[4]{0:T(128)} %param.11) | copy-start | bytes 52
  0.7 15.4 %copy-start = (bf16[4,17,256]{2,0,1:T(4,128)(2,1)S(1)}, bf16[4,17,256]{2,0,1:T(4,128)(2,1)}, u32[]{:S(2)}) copy-start(bf16[4,17,256]{2,0,1:T(4,128)(2,1)} %param.10) | copy-start | bytes 104452
  0.7 26.7 %copy-start.5 = (f32[4]{0:T(128)S(1)}, f32[4]{0:T(128)}, u32[]{:S(2)}) copy-start(f32[4]{0:T(128)} %param.12) | copy-start | bytes 52
  2.7 34.8 %all-to-all-start = ((bf16[8,4,64,256]{3,2,1,0:T(8,128)(2,1)}), bf16[8,4,64,256]{3,2,1,0:T(8,128)(2,1)S(1)}, u32[]{:S(2)}, u32[]{:S(2)}) async-start(bf16[8,4,64,256]{3,2,1,0:T(8,128)(2,1)} %broadcast_in_dim.32), calls=%async_computation | async-start | bytes 2097152 | tf_op jit(solution)/shard_map/all_to_all | solution.py:190
  10.5 16.9 %collective-permute-start = (bf16[4,64,8]{2,1,0:T(8,128)(2,1)S(1)}, bf16[4,64,8]{2,1,0:T(8,128)(2,1)S(1)}, u32[]{:S(2)}, u32[]{:S(2)}) collective-permute-start(bf16[4,64,8]{2,1,0:T(8,128)(2,1)S(1)} %get-tuple-element.34), channel_id=1, source_target_pairs={{0,1},{1,2},{2,3},{3,4},{4,5},{5,6},{6,7},{8,9},{9,10},{10,11},{11... | collective-permute-start | bytes 12296 | tf_op jit(solution)/shard_map/ppermute | solution.py:195
  14.5 12.9 %collective-permute-start.1 = (bf16[4,64,8]{2,1,0:T(8,128)(2,1)S(1)}, bf16[4,64,8]{2,1,0:T(8,128)(2,1)S(1)}, u32[]{:S(2)}, u32[]{:S(2)}) collective-permute-start(bf16[4,64,8]{2,1,0:T(8,128)(2,1)S(1)} %get-tuple-element.35), channel_id=1, source_target_pairs={{1,0},{2,1},{3,2},{4,3},{5,4},{6,5},{7,6},{9,8},{10,9},{11,10},{12... | collective-permute-start | bytes 12296 | tf_op jit(solution)/shard_map/ppermute | solution.py:196
  39.8 7.0 %copy-start.6 = (s32[32]{0:T(128)S(1)}, s32[32]{0:T(128)}, u32[]{:S(2)}) copy-start(s32[32]{0:T(128)} %param.14) | copy-start | bytes 388
  39.8 33.3 %all-to-all-start.1 = ((bf16[64,64,256]{2,1,0:T(8,128)(2,1)}), bf16[64,64,256]{2,1,0:T(8,128)(2,1)S(1)}, u32[]{:S(2)}, u32[]{:S(2)}) async-start(bf16[64,64,256]{2,1,0:T(8,128)(2,1)} %pick.1), calls=%async_computation.1 | async-start | bytes 4194304 | tf_op jit(solution)/shard_map/all_to_all | solution.py:210
  108.0 12.8 %all-to-all-start.4 = ((f32[16,2,128]{2,1,0:T(2,128)}), f32[16,2,128]{2,1,0:T(2,128)S(1)}, u32[]{:S(2)}, u32[]{:S(2)}) async-start(f32[16,2,128]{2,1,0:T(2,128)} %get-tuple-element.22), calls=%async_computation.4 | async-start | bytes 32768 | tf_op jit(solution)/shard_map/all_to_all | solution.py:253

commit v8 on v5

--- a/solution.py
+++ b/solution.py
@@ -82,15 +82,11 @@
         copy(chunk).start()
     total[...] = banded[...]
 
-    @pl.loop(0, sems.shape[0])
-    def _(chunk):
-        copy(chunk).wait()
-        for i in range(CHUNK):
-            p = chunk * CHUNK + i
-            part = lax.dot_general(
-                rows[slot[p]], held[p], NT, preferred_element_type=jnp.float32
-            )
-            total[target[p]] += part * live[p]
+    for p in range(coupling.shape[0]):
+        if p % CHUNK == 0:
+            copy(p // CHUNK).wait()
+        part = lax.dot_general(rows[slot[p]], held[p], NT, preferred_element_type=jnp.float32)
+        total[target[p]] += part * live[p]
 
     acc = jnp.zeros((trial.shape[1], trial.shape[1]), jnp.float32)
     for c in range(total.shape[0]):
@@ -102,24 +98,29 @@
 
 def middle_kernel(received, gram, spread):
     whole = jnp.concatenate([gram[...], jnp.sum(received[...], axis=0)], axis=0)
+    width = spread.shape[1]
+    count = whole.shape[0] // width
+    for j in range(spread.shape[0]):
+        spread[j] = whole[j % count * width : (j % count + 1) * width]
+
+
+def last_kernel(over_y, over_x, received, spread, gram):
+    count = received.shape[0] // (over_y * over_x)
+
+    def added(number, senders):
+        first = received[senders[0] * count + number]
+        for sender in senders[1:]:
+            first += received[sender * count + number]
+        return first
+
+    whole = added(count - 1, range(over_y * over_x))
     for j in range(spread.shape[0]):
         spread[j] = whole
-
-
-def last_kernel(received, spread, gram):
-    piece = spread.shape[1]
-    part = received.shape[1] - piece
-    count = gram.shape[0] // 2 // part
-    over_x = received.shape[0] // count
     found = []
-    for y in range(count):
-        found.append(jnp.sum(received[y * over_x : (y + 1) * over_x], axis=0))
-    whole = found[0][part:]
-    for y in range(1, count):
-        whole += found[y][part:]
-    for j in range(spread.shape[0]):
-        spread[j] = whole
-    gram[...] = unpack(jnp.concatenate([f[:part] for f in found], axis=0))
+    for y in range(over_y):
+        for number in range(count - 1):
+            found.append(added(number, range(y * over_x, (y + 1) * over_x)))
+    gram[...] = unpack(jnp.concatenate(found, axis=0))
 
 
 def residual_kernel(inverse, projected, trial, image, residual, rayleigh):
@@ -231,14 +232,14 @@
     spread = call(
         middle_kernel,
         "middle",
-        f32(ys * xs, half // ys + piece, 2 * vecs),
+        f32(ys * xs * (half // ys // piece + 1), piece, 2 * vecs),
         [VMEM, VMEM],
         received,
         gram,
     )
     received = lax.all_to_all(spread, ("y", "x"), 0, 0, tiled=True)
     spread, gram = call(
-        last_kernel, "last", (f32(shared, piece, 2 * vecs), f32(vecs, vecs)), [VMEM], received
+        functools.partial(last_kernel, ys, xs), "last", (f32(shared, piece, 2 * vecs), f32(vecs, vecs)), [VMEM], received
     )
     inverse = call(inverse_kernel, "inverse", f32(vecs, vecs), [VMEM], gram)
     projected = lax.all_to_all(spread, ("core", "rad"), 0, 0, tiled=True).reshape(half, 2 * vecs)

time: 122 us -> 122 us (level)
  no operation moved by 1% of the time
where the time goes in v8:
time: 122 us; the launch traced here: 121 us
  blocking collectives  62 us (51%)
  starting transfers between devices  25.1 us (21%)
  waiting for transfers between devices  13.5 us (11%)
  Pallas kernels  12 us (10%)
  local copies, waits for them, and re-layouts  5.88 us (5%)
  other arithmetic  1.52 us (1%)
  between operations  1.5 us (1%)
    psum x2, blocking collectives, body(): gram = lax.psum(lax.psum(gram, 'core'), 'rad')  23.1 us
    all_to_all x1, blocking collectives, body(): received = lax.all_to_all(sent, ('core', 'rad'), 0, 0, tiled=True)  18 us
    all_to_all x1, blocking collectives, body(): received = lax.all_to_all(spread, ('y', 'x'), 0, 0, tiled=True)  12.1 us
    pallas_call x7, Pallas kernels, call(): pl.pallas_call(kernel, out_shape=shapes, in_specs=specs, out_specs=(VMEM,...  12 us
    all_to_all x1, waiting for transfers between devices, body(): lax.all_to_all(jnp.broadcast_to(by_slot[None], (ys,) + by_slot.shape), 'y...  9.13 us
    unnamed x1, blocking collectives  8.83 us
    all_to_all x1, starting transfers between devices, body(): lax.all_to_all(jnp.broadcast_to(by_slot[None], (ys,) + by_slot.shape), 'y...  7.65 us
    all_to_all x1, starting transfers between devices, body(): rows = lax.all_to_all(picked, INNER, 0, 0, tiled=True)  6.93 us
  transfers between devices with their start and end apart: 5, of which 3 were waited for; matrix products, arithmetic and copies ran while one was open for 3% of the time, Pallas kernels for 5%

profile of v8, /device:TPU:1, one launch (start us, length us, event | category | flops | bytes accessed | tf_op | source)
XLA Modules:
  0.0 121.5 jit_solution(11097320724325253119)
XLA Ops:
  0.6 0.0 copy-start.4
  0.6 0.0 copy-start.5
  0.7 0.0 copy-start.2
  0.7 0.0 copy-start.3
  0.7 0.0 copy-start.1
  0.7 0.0 copy-start.6
  0.7 1.0 copy.16
  1.6 1.1 broadcast_in_dim.32
  2.7 7.7 %all-to-all-start = ((bf16[8,4,64,256]{3,2,1,0:T(8,128)(2,1)}), bf16[8,4,64,256]{3,2,1,0:T(8,128)(2,1)S(1)}, u32[]{:S(2)}, u32[]{:S(2)}) async-start(bf16[8,4,64,256]{3,2,1,0:T(8,128)(2,1)} %broadcast_in_dim.32), calls=%async_computation | async-start | bytes 2097152 | tf_op jit(solution)/shard_map/all_to_all | solution.py:182
  10.4 0.1 fusion.31
  10.5 4.0 %collective-permute-start = (bf16[4,64,8]{2,1,0:T(8,128)(2,1)S(1)}, bf16[4,64,8]{2,1,0:T(8,128)(2,1)S(1)}, u32[]{:S(2)}, u32[]{:S(2)}) collective-permute-start(bf16[4,64,8]{2,1,0:T(8,128)(2,1)S(1)} %get-tuple-element.34), channel_id=1, source_target_pairs={{0,1},{1,2},{2,3},{3,4},{4,5},{5,6},{6,7},{8,9},{9,10},{10,11},{11... | collective-permute-start | bytes 12296 | tf_op jit(solution)/shard_map/ppermute | solution.py:187
  14.5 1.3 %collective-permute-start.1 = (bf16[4,64,8]{2,1,0:T(8,128)(2,1)S(1)}, bf16[4,64,8]{2,1,0:T(8,128)(2,1)S(1)}, u32[]{:S(2)}, u32[]{:S(2)}) collective-permute-start(bf16[4,64,8]{2,1,0:T(8,128)(2,1)S(1)} %get-tuple-element.35), channel_id=1, source_target_pairs={{1,0},{2,1},{3,2},{4,3},{5,4},{6,5},{7,6},{9,8},{10,9},{11,10},{12... | collective-permute-start | bytes 12296 | tf_op jit(solution)/shard_map/ppermute | solution.py:188
  15.8 0.0 copy-done.4
  15.8 0.0 copy-done.5
  15.8 0.0 copy-done.2
  15.8 0.2 select_reduce_fusion
  16.0 0.0 copy-done.3
  16.0 0.0 copy-done.1
  16.1 0.1 multiply_bitcast_fusion.15
  16.1 0.1 multiply_bitcast_fusion.16
  16.2 0.1 select_reduce_fusion.2
  16.3 1.3 %dynamic-slice = u32[1]{0:T(128)} dynamic-slice(u32[512]{0:T(512)} %constant.73, u32[]{:T(128)S(6)} %add.101), dynamic_slice_sizes={1} | dynamic-slice | bytes 12
  18.2 0.2 dynamic-update-slice
  18.5 8.8 %all-reduce = s32[512]{0:T(512)S(1)} all-reduce(s32[512]{0:T(512)S(1)} %dynamic-update-slice), channel_id=2, replica_groups=mesh['y'=8,'x'=4,'core'=2,'rad'=8] {'x','core'}, use_global_device_ids=true, to_apply=%add | all-reduce | flops 512 | bytes 4096
  27.3 0.1 reshape.132.need
  27.4 0.0 collective-permute-done
  27.4 0.0 collective-permute-done.1
  27.4 0.0 copy-done.6
  27.4 1.0 fusion.16.banded
  28.4 9.1 %all-to-all-done = bf16[8,4,64,256]{3,2,1,0:T(8,128)(2,1)S(1)} async-done(((bf16[8,4,64,256]{3,2,1,0:T(8,128)(2,1)}), bf16[8,4,64,256]{3,2,1,0:T(8,128)(2,1)S(1)}, u32[]{:S(2)}, u32[]{:S(2)}) %all-to-all-start) | async-done | bytes 1048608 | tf_op jit(solution)/shard_map/all_to_all | solution.py:182
  37.6 0.8 pick.1
  38.4 0.0 copy-start
  38.4 1.3 %copy-done = bf16[64,64,256]{2,1,0:T(8,128)(2,1)} copy-done((bf16[64,64,256]{2,1,0:T(8,128)(2,1)}, bf16[64,64,256]{2,1,0:T(8,128)(2,1)S(1)}, u32[]{:S(2)}) %copy-start) | copy-done | bytes 2097176
  39.7 0.0 copy-start.7
  39.8 6.9 %all-to-all-start.1 = ((bf16[64,64,256]{2,1,0:T(8,128)(2,1)}), bf16[64,64,256]{2,1,0:T(8,128)(2,1)S(1)}, u32[]{:S(2)}, u32[]{:S(2)}) async-start(bf16[64,64,256]{2,1,0:T(8,128)(2,1)} %copy-done), calls=%async_computation.1 | async-start | bytes 4194304 | tf_op jit(solution)/shard_map/all_to_all | solution.py:202
  46.7 0.0 copy-done.7
  46.7 0.5 gram.1
  47.2 2.5 %psum.14 = f32[4,128]{1,0:T(4,128)S(1)} all-reduce(f32[4,128]{1,0:T(4,128)S(1)} %constant_dynamic-slice_fusion), channel_id=1, replica_groups=mesh['y'=8,'x'=4,'core'=2,'rad'=8] {'core'}, use_global_device_ids=true, to_apply=%region_3.4 | all-reduce | flops 512 | bytes 4096 | tf_op jit(solution)/shard_map/psum | solution.py:206
  49.7 20.6 %psum.15.gram = f32[4,128]{1,0:T(4,128)S(1)} all-reduce(f32[4,128]{1,0:T(4,128)S(1)} %psum.14), channel_id=1, replica_groups=mesh['y'=8,'x'=4,'core'=2,'rad'=8] {'rad'}, use_global_device_ids=true, to_apply=%region_4.5 | all-reduce | flops 512 | bytes 4096 | tf_op jit(solution)/shard_map/psum | solution.py:206
  70.3 2.7 %all-to-all-done.1.rows = bf16[64,64,256]{2,1,0:T(8,128)(2,1)S(1)} async-done(((bf16[64,64,256]{2,1,0:T(8,128)(2,1)}), bf16[64,64,256]{2,1,0:T(8,128)(2,1)S(1)}, u32[]{:S(2)}, u32[]{:S(2)}) %all-to-all-start.1) | async-done | bytes 2097184 | tf_op jit(solution)/shard_map/all_to_all | solution.py:202
  73.0 3.9 %image.1 = (bf16[4,64,256]{2,1,0:T(8,128)(2,1)S(1)}, f32[32,128]{1,0:T(8,128)S(1)}) custom-call(s32[32]{0:T(128)S(1)} %multiply_add_fusion.slot, s32[32]{0:T(128)S(1)} %broadcast_subtract_fusion.target, f32[32]{0:T(128)S(1)} %compare_convert_fusion.9.live, bf16[64,64,256]{2,1,0:T(8,128)(2,1)S(1)} %all-to-all-done.1.rows, bf16[32,256,256]{2,1,0:T(8,128)(2,1)} %coupling.1, ...), custom_call_target="tpu_custom_call" | custom-call | tf_op jit(solution)/shard_map/image/pallas_call | solution.py:142
  76.9 18.0 %all_to_all.25.received = f32[16,2,128]{2,1,0:T(2,128)S(1)} all-to-all(f32[16,2,128]{2,1,0:T(2,128)S(1)} %bitcast.52), channel_id=1, replica_groups=mesh['y'=8,'x'=4,'core'=2,'rad'=8] {'core','rad'}, dimensions={0} | all-to-all | bytes 32768 | tf_op jit(solution)/shard_map/all_to_all | solution.py:231
  94.9 12.1 %all_to_all.26.received = f32[96,2,128]{2,1,0:T(2,128)S(1)} all-to-all(f32[96,2,128]{2,1,0:T(2,128)S(1)} %middle.1), channel_id=1, replica_groups=mesh['y'=8,'x'=4,'core'=2,'rad'=8] {'y','x'}, dimensions={0} | all-to-all | bytes 196608 | tf_op jit(solution)/shard_map/all_to_all | solution.py:240
  107.0 0.7 last.1
  107.7 5.2 %all-to-all-start.4 = ((f32[16,2,128]{2,1,0:T(2,128)}), f32[16,2,128]{2,1,0:T(2,128)S(1)}, u32[]{:S(2)}, u32[]{:S(2)}) async-start(f32[16,2,128]{2,1,0:T(2,128)} %get-tuple-element.22), calls=%async_computation.4 | async-start | bytes 32768 | tf_op jit(solution)/shard_map/all_to_all | solution.py:245
  112.9 5.3 %inverse.1 = f32[64,64]{1,0:T(8,128)S(1)} custom-call(f32[64,64]{1,0:T(8,128)S(1)} %get-tuple-element.21.square), custom_call_target="tpu_custom_call" | custom-call | tf_op jit(solution)/shard_map/inverse/pallas_call | solution.py:142
  118.2 1.6 %all-to-all-done.4 = f32[16,2,128]{2,1,0:T(2,128)S(1)} async-done(((f32[16,2,128]{2,1,0:T(2,128)}), f32[16,2,128]{2,1,0:T(2,128)S(1)}, u32[]{:S(2)}, u32[]{:S(2)}) %all-to-all-start.4) | async-done | bytes 16416 | tf_op jit(solution)/shard_map/all_to_all | solution.py:245
  119.8 0.9 residual.1
  120.7 0.8 copy.14
  (8 shorter events, 0.1 us)
Async XLA Ops:
  0.6 15.2 %copy-start.4 = (s32[32]{0:T(128)S(1)}, s32[32]{0:T(128)}, u32[]{:S(2)}) copy-start(s32[32]{0:T(128)} %param.15) | copy-start | bytes 388
  0.6 15.2 %copy-start.5 = (s32[32]{0:T(128)S(1)}, s32[32]{0:T(128)}, u32[]{:S(2)}) copy-start(s32[32]{0:T(128)} %param.16) | copy-start | bytes 388
  0.7 15.2 %copy-start.2 = (s32[256]{0:T(256)S(1)}, s32[256]{0:T(256)}, u32[]{:S(2)}) copy-start(s32[256]{0:T(256)} %param.17) | copy-start | bytes 3076
  0.7 15.4 %copy-start.3 = (s32[4]{0:T(128)S(1)}, s32[4]{0:T(128)}, u32[]{:S(2)}) copy-start(s32[4]{0:T(128)} %param.11) | copy-start | bytes 52
  0.7 15.4 %copy-start.1 = (bf16[4,17,256]{2,0,1:T(4,128)(2,1)S(1)}, bf16[4,17,256]{2,0,1:T(4,128)(2,1)}, u32[]{:S(2)}) copy-start(bf16[4,17,256]{2,0,1:T(4,128)(2,1)} %param.10) | copy-start | bytes 104452
  0.7 26.7 %copy-start.6 = (f32[4]{0:T(128)S(1)}, f32[4]{0:T(128)}, u32[]{:S(2)}) copy-start(f32[4]{0:T(128)} %param.12) | copy-start | bytes 52
  2.7 34.8 %all-to-all-start = ((bf16[8,4,64,256]{3,2,1,0:T(8,128)(2,1)}), bf16[8,4,64,256]{3,2,1,0:T(8,128)(2,1)S(1)}, u32[]{:S(2)}, u32[]{:S(2)}) async-start(bf16[8,4,64,256]{3,2,1,0:T(8,128)(2,1)} %broadcast_in_dim.32), calls=%async_computation | async-start | bytes 2097152 | tf_op jit(solution)/shard_map/all_to_all | solution.py:182
  10.5 16.9 %collective-permute-start = (bf16[4,64,8]{2,1,0:T(8,128)(2,1)S(1)}, bf16[4,64,8]{2,1,0:T(8,128)(2,1)S(1)}, u32[]{:S(2)}, u32[]{:S(2)}) collective-permute-start(bf16[4,64,8]{2,1,0:T(8,128)(2,1)S(1)} %get-tuple-element.34), channel_id=1, source_target_pairs={{0,1},{1,2},{2,3},{3,4},{4,5},{5,6},{6,7},{8,9},{9,10},{10,11},{11... | collective-permute-start | bytes 12296 | tf_op jit(solution)/shard_map/ppermute | solution.py:187
  14.5 12.9 %collective-permute-start.1 = (bf16[4,64,8]{2,1,0:T(8,128)(2,1)S(1)}, bf16[4,64,8]{2,1,0:T(8,128)(2,1)S(1)}, u32[]{:S(2)}, u32[]{:S(2)}) collective-permute-start(bf16[4,64,8]{2,1,0:T(8,128)(2,1)S(1)} %get-tuple-element.35), channel_id=1, source_target_pairs={{1,0},{2,1},{3,2},{4,3},{5,4},{6,5},{7,6},{9,8},{10,9},{11,10},{12... | collective-permute-start | bytes 12296 | tf_op jit(solution)/shard_map/ppermute | solution.py:188
  38.4 1.3 %copy-start = (bf16[64,64,256]{2,1,0:T(8,128)(2,1)}, bf16[64,64,256]{2,1,0:T(8,128)(2,1)S(1)}, u32[]{:S(2)}) copy-start(bf16[64,64,256]{2,1,0:T(8,128)(2,1)S(1)} %pick.1) | copy-start | bytes 6291460
  39.7 7.0 %copy-start.7 = (s32[32]{0:T(128)S(1)}, s32[32]{0:T(128)}, u32[]{:S(2)}) copy-start(s32[32]{0:T(128)} %param.14) | copy-start | bytes 388
  39.8 33.3 %all-to-all-start.1 = ((bf16[64,64,256]{2,1,0:T(8,128)(2,1)}), bf16[64,64,256]{2,1,0:T(8,128)(2,1)S(1)}, u32[]{:S(2)}, u32[]{:S(2)}) async-start(bf16[64,64,256]{2,1,0:T(8,128)(2,1)} %copy-done), calls=%async_computation.1 | async-start | bytes 4194304 | tf_op jit(solution)/shard_map/all_to_all | solution.py:202
  107.7 12.2 %all-to-all-start.4 = ((f32[16,2,128]{2,1,0:T(2,128)}), f32[16,2,128]{2,1,0:T(2,128)S(1)}, u32[]{:S(2)}, u32[]{:S(2)}) async-start(f32[16,2,128]{2,1,0:T(2,128)} %get-tuple-element.22), calls=%async_computation.4 | async-start | bytes 32768 | tf_op jit(solution)/shard_map/all_to_all | solution.py:245

commit v9 on v8

--- a/solution.py
+++ b/solution.py
@@ -11,7 +11,6 @@
 BLK = 256
 CORES = 2
 X_CHIPS = 4
-CHUNK = 8
 INNER = ("x", "core")
 CHAN = ("y", "x", "core")
 VMEM = pl.BlockSpec(memory_space=pltpu.VMEM)
@@ -40,17 +39,23 @@
     return acc
 
 
-def pick_kernel(mine, need, rows, out):
+def pick_kernel(mine, need, rows, out, held, sems):
     receivers = need.shape[0]
     groups = out.shape[0] // receivers
     per_group = rows.shape[0] // groups
     columns = need.shape[1] // groups
 
-    @pl.loop(0, receivers)
-    def _(receiver):
+    def copy(receiver):
+        part = pl.ds(receiver * groups, groups)
+        return pltpu.make_async_copy(held.at[part], out.at[part], sems.at[receiver])
+
+    for receiver in range(receivers):
         for group in range(groups):
             chosen = group * per_group + need[receiver, group * columns + mine[0]]
-            out[receiver * groups + group] = rows[chosen]
+            held[receiver * groups + group] = rows[chosen]
+        copy(receiver).start()
+    for receiver in range(receivers):
+        copy(receiver).wait()
 
 
 def gram_kernel(rows, gram):
@@ -71,20 +76,24 @@
     inverse[...] = value
 
 
+def chunk_starts(pairs):
+    return [0] + sorted({pairs * part // 16 for part in (6, 11, 14)} - {0}) + [pairs]
+
+
 def image_kernel(
     slot, target, live, rows, coupling, banded, trial, image, sent, total, held, sems
 ):
-    def copy(chunk):
-        part = pl.ds(chunk * CHUNK, CHUNK)
-        return pltpu.make_async_copy(coupling.at[part], held.at[part], sems.at[chunk])
-
-    for chunk in range(sems.shape[0]):
-        copy(chunk).start()
+    starts = chunk_starts(coupling.shape[0])
+    copies = {}
+    for i, first in enumerate(starts[:-1]):
+        part = pl.ds(first, starts[i + 1] - first)
+        copies[first] = pltpu.make_async_copy(coupling.at[part], held.at[part], sems.at[i])
+        copies[first].start()
     total[...] = banded[...]
 
     for p in range(coupling.shape[0]):
-        if p % CHUNK == 0:
-            copy(p // CHUNK).wait()
+        if p in copies:
+            copies[p].wait()
         part = lax.dot_general(rows[slot[p]], held[p], NT, preferred_element_type=jnp.float32)
         total[target[p]] += part * live[p]
 
@@ -195,9 +204,18 @@
 
     column, banded = lax.optimization_barrier((column, banded))
     mine = (lax.axis_index("x") * cores + lax.axis_index("core")).reshape(1)
-    picked = call(
-        pick_kernel, "pick", bf16(columns * ys, vecs, slab), [SMEM, SMEM, VMEM], mine, needed, column
-    )
+    picked = pl.pallas_call(
+        pick_kernel,
+        out_shape=pltpu.HBM((columns * ys, vecs, slab), jnp.bfloat16),
+        in_specs=[SMEM, SMEM, VMEM],
+        out_specs=ANY,
+        scratch_shapes=[
+            pltpu.VMEM((columns * ys, vecs, slab), jnp.bfloat16),
+            pltpu.SemaphoreType.DMA((columns,)),
+        ],
+        compiler_params=pltpu.CompilerParams(vmem_limit_bytes=40 * MIB),
+        name="pick",
+    )(mine, needed, column)
     column, picked = lax.optimization_barrier((column, picked))
     rows = lax.all_to_all(picked, INNER, 0, 0, tiled=True)
     half = vecs // 2
@@ -221,7 +239,7 @@
         scratch=[
             pltpu.VMEM(by_slot.shape, jnp.float32),
             pltpu.VMEM(coupling.shape, jnp.bfloat16),
-            pltpu.SemaphoreType.DMA((coupling.shape[0] // CHUNK,)),
+            pltpu.SemaphoreType.DMA((len(chunk_starts(coupling.shape[0])) - 1,)),
         ],
         limit=50,
     )

time: 122 us -> 122 us (level)
  Pallas kernels: 12 us -> 13.4 us
  local copies, waits for them, and re-layouts: 5.88 us -> 4.55 us
    pallas_call x0 -> x1, Pallas kernels: none -> 2.04 us  [body(): pl.pallas_call(pick_kernel, out_shape=pltpu.HBM((columns * ys, vecs, slab...]
    unnamed x21 -> x19, local copies, waits for them, and re-layouts: 4.6 us -> 3.26 us
    pallas_call x7 -> x6, Pallas kernels: 12 us -> 11.4 us  [call(): pl.pallas_call(kernel, out_shape=shapes, in_specs=specs, out_specs=(VMEM,...]
where the time goes in v9:
time: 122 us; the launch traced here: 121 us
  blocking collectives  62 us (51%)
  starting transfers between devices  25 us (20%)
  waiting for transfers between devices  13.5 us (11%)
  Pallas kernels  13.4 us (11%)
  local copies, waits for them, and re-layouts  4.55 us (4%)
  other arithmetic  1.52 us (1%)
  between operations  1.49 us (1%)
    psum x2, blocking collectives, body(): gram = lax.psum(lax.psum(gram, 'core'), 'rad')  23.1 us
    all_to_all x1, blocking collectives, body(): received = lax.all_to_all(sent, ('core', 'rad'), 0, 0, tiled=True)  18 us
    all_to_all x1, blocking collectives, body(): received = lax.all_to_all(spread, ('y', 'x'), 0, 0, tiled=True)  12.1 us
    pallas_call x6, Pallas kernels, call(): pl.pallas_call(kernel, out_shape=shapes, in_specs=specs, out_specs=(VMEM,...  11.4 us
    all_to_all x1, waiting for transfers between devices, body(): lax.all_to_all(jnp.broadcast_to(by_slot[None], (ys,) + by_slot.shape), 'y...  9.13 us
    unnamed x1, blocking collectives  8.83 us
    all_to_all x1, starting transfers between devices, body(): lax.all_to_all(jnp.broadcast_to(by_slot[None], (ys,) + by_slot.shape), 'y...  7.65 us
    all_to_all x1, starting transfers between devices, body(): rows = lax.all_to_all(picked, INNER, 0, 0, tiled=True)  6.81 us
  transfers between devices with their start and end apart: 5, of which 3 were waited for; matrix products, arithmetic and copies ran while one was open for 3% of the time, Pallas kernels for 5%

profile of v9, /device:TPU:1, one launch (start us, length us, event | category | flops | bytes accessed | tf_op | source)
XLA Modules:
  0.0 121.4 jit_solution(14596964160882112341)
XLA Ops:
  0.6 0.0 copy-start.3
  0.6 0.0 copy-start.4
  0.7 0.0 copy-start.1
  0.7 0.0 copy-start.2
  0.7 0.0 copy-start
  0.7 0.0 copy-start.5
  0.7 1.0 copy.16
  1.6 1.1 broadcast_in_dim.32
  2.7 7.7 %all-to-all-start = ((bf16[8,4,64,256]{3,2,1,0:T(8,128)(2,1)}), bf16[8,4,64,256]{3,2,1,0:T(8,128)(2,1)S(1)}, u32[]{:S(2)}, u32[]{:S(2)}) async-start(bf16[8,4,64,256]{3,2,1,0:T(8,128)(2,1)} %broadcast_in_dim.32), calls=%async_computation | async-start | bytes 2097152 | tf_op jit(solution)/shard_map/all_to_all | solution.py:191
  10.4 0.1 fusion.31
  10.5 4.0 %collective-permute-start = (bf16[4,64,8]{2,1,0:T(8,128)(2,1)S(1)}, bf16[4,64,8]{2,1,0:T(8,128)(2,1)S(1)}, u32[]{:S(2)}, u32[]{:S(2)}) collective-permute-start(bf16[4,64,8]{2,1,0:T(8,128)(2,1)S(1)} %get-tuple-element.34), channel_id=1, source_target_pairs={{0,1},{1,2},{2,3},{3,4},{4,5},{5,6},{6,7},{8,9},{9,10},{10,11},{11... | collective-permute-start | bytes 12296 | tf_op jit(solution)/shard_map/ppermute | solution.py:196
  14.5 1.3 %collective-permute-start.1 = (bf16[4,64,8]{2,1,0:T(8,128)(2,1)S(1)}, bf16[4,64,8]{2,1,0:T(8,128)(2,1)S(1)}, u32[]{:S(2)}, u32[]{:S(2)}) collective-permute-start(bf16[4,64,8]{2,1,0:T(8,128)(2,1)S(1)} %get-tuple-element.35), channel_id=1, source_target_pairs={{1,0},{2,1},{3,2},{4,3},{5,4},{6,5},{7,6},{9,8},{10,9},{11,10},{12... | collective-permute-start | bytes 12296 | tf_op jit(solution)/shard_map/ppermute | solution.py:197
  15.8 0.0 copy-done.3
  15.8 0.0 copy-done.4
  15.8 0.0 copy-done.1
  15.8 0.2 select_reduce_fusion
  16.0 0.0 copy-done.2
  16.0 0.0 copy-done
  16.1 0.1 multiply_bitcast_fusion.15
  16.1 0.1 multiply_bitcast_fusion.16
  16.2 0.1 select_reduce_fusion.2
  16.3 1.3 %dynamic-slice = u32[1]{0:T(128)} dynamic-slice(u32[512]{0:T(512)} %constant.73, u32[]{:T(128)S(6)} %add.101), dynamic_slice_sizes={1} | dynamic-slice | bytes 12
  18.2 0.2 dynamic-update-slice
  18.5 8.8 %all-reduce = s32[512]{0:T(512)S(1)} all-reduce(s32[512]{0:T(512)S(1)} %dynamic-update-slice), channel_id=2, replica_groups=mesh['y'=8,'x'=4,'core'=2,'rad'=8] {'x','core'}, use_global_device_ids=true, to_apply=%add | all-reduce | flops 512 | bytes 4096
  27.3 0.1 reshape.132.need
  27.4 0.0 collective-permute-done
  27.4 0.0 collective-permute-done.1
  27.4 0.0 copy-done.5
  27.4 1.0 fusion.16.banded
  28.4 9.1 %all-to-all-done = bf16[8,4,64,256]{3,2,1,0:T(8,128)(2,1)S(1)} async-done(((bf16[8,4,64,256]{3,2,1,0:T(8,128)(2,1)}), bf16[8,4,64,256]{3,2,1,0:T(8,128)(2,1)S(1)}, u32[]{:S(2)}, u32[]{:S(2)}) %all-to-all-start) | async-done | bytes 1048608 | tf_op jit(solution)/shard_map/all_to_all | solution.py:191
  37.6 2.0 %pick.1 = bf16[64,64,256]{2,1,0:T(8,128)(2,1)} custom-call(s32[1]{0:T(128)} %bitcast.19.mine, s32[8,64]{1,0:T(8,128)S(1)} %reshape.132.need, bf16[32,64,256]{2,1,0:T(8,128)(2,1)S(1)} %bitcast.43), custom_call_target="tpu_custom_call" | custom-call | tf_op jit(solution)/shard_map/pick/pallas_call | solution.py:207
  39.6 0.0 copy-start.6
  39.6 6.8 %all-to-all-start.1 = ((bf16[64,64,256]{2,1,0:T(8,128)(2,1)}), bf16[64,64,256]{2,1,0:T(8,128)(2,1)S(1)}, u32[]{:S(2)}, u32[]{:S(2)}) async-start(bf16[64,64,256]{2,1,0:T(8,128)(2,1)} %pick.1), calls=%async_computation.1 | async-start | bytes 4194304 | tf_op jit(solution)/shard_map/all_to_all | solution.py:220
  46.5 0.0 copy-done.6
  46.5 0.5 gram.1
  47.0 2.5 %psum.14 = f32[4,128]{1,0:T(4,128)S(1)} all-reduce(f32[4,128]{1,0:T(4,128)S(1)} %constant_dynamic-slice_fusion), channel_id=1, replica_groups=mesh['y'=8,'x'=4,'core'=2,'rad'=8] {'core'}, use_global_device_ids=true, to_apply=%region_3.4 | all-reduce | flops 512 | bytes 4096 | tf_op jit(solution)/shard_map/psum | solution.py:224
  49.5 20.6 %psum.15.gram = f32[4,128]{1,0:T(4,128)S(1)} all-reduce(f32[4,128]{1,0:T(4,128)S(1)} %psum.14), channel_id=1, replica_groups=mesh['y'=8,'x'=4,'core'=2,'rad'=8] {'rad'}, use_global_device_ids=true, to_apply=%region_4.5 | all-reduce | flops 512 | bytes 4096 | tf_op jit(solution)/shard_map/psum | solution.py:224
  70.1 2.7 %all-to-all-done.1.rows = bf16[64,64,256]{2,1,0:T(8,128)(2,1)S(1)} async-done(((bf16[64,64,256]{2,1,0:T(8,128)(2,1)}), bf16[64,64,256]{2,1,0:T(8,128)(2,1)S(1)}, u32[]{:S(2)}, u32[]{:S(2)}) %all-to-all-start.1) | async-done | bytes 2097184 | tf_op jit(solution)/shard_map/all_to_all | solution.py:220
  72.8 4.1 %image.1 = (bf16[4,64,256]{2,1,0:T(8,128)(2,1)S(1)}, f32[32,128]{1,0:T(8,128)S(1)}) custom-call(s32[32]{0:T(128)S(1)} %multiply_add_fusion.slot, s32[32]{0:T(128)S(1)} %broadcast_subtract_fusion.target, f32[32]{0:T(128)S(1)} %compare_convert_fusion.9.live, bf16[64,64,256]{2,1,0:T(8,128)(2,1)S(1)} %all-to-all-done.1.rows, bf16[32,256,256]{2,1,0:T(8,128)(2,1)} %coupling.1, ...), custom_call_target="tpu_custom_call" | custom-call | tf_op jit(solution)/shard_map/image/pallas_call | solution.py:151
  76.8 18.0 %all_to_all.25.received = f32[16,2,128]{2,1,0:T(2,128)S(1)} all-to-all(f32[16,2,128]{2,1,0:T(2,128)S(1)} %bitcast.52), channel_id=1, replica_groups=mesh['y'=8,'x'=4,'core'=2,'rad'=8] {'core','rad'}, dimensions={0} | all-to-all | bytes 32768 | tf_op jit(solution)/shard_map/all_to_all | solution.py:249
  94.9 12.1 %all_to_all.26.received = f32[96,2,128]{2,1,0:T(2,128)S(1)} all-to-all(f32[96,2,128]{2,1,0:T(2,128)S(1)} %middle.1), channel_id=1, replica_groups=mesh['y'=8,'x'=4,'core'=2,'rad'=8] {'y','x'}, dimensions={0} | all-to-all | bytes 196608 | tf_op jit(solution)/shard_map/all_to_all | solution.py:258
  107.0 0.7 last.1
  107.6 5.2 %all-to-all-start.4 = ((f32[16,2,128]{2,1,0:T(2,128)}), f32[16,2,128]{2,1,0:T(2,128)S(1)}, u32[]{:S(2)}, u32[]{:S(2)}) async-start(f32[16,2,128]{2,1,0:T(2,128)} %get-tuple-element.22), calls=%async_computation.4 | async-start | bytes 32768 | tf_op jit(solution)/shard_map/all_to_all | solution.py:263
  112.8 5.3 %inverse.1 = f32[64,64]{1,0:T(8,128)S(1)} custom-call(f32[64,64]{1,0:T(8,128)S(1)} %get-tuple-element.21.square), custom_call_target="tpu_custom_call" | custom-call | tf_op jit(solution)/shard_map/inverse/pallas_call | solution.py:151
  118.2 1.6 %all-to-all-done.4 = f32[16,2,128]{2,1,0:T(2,128)S(1)} async-done(((f32[16,2,128]{2,1,0:T(2,128)}), f32[16,2,128]{2,1,0:T(2,128)S(1)}, u32[]{:S(2)}, u32[]{:S(2)}) %all-to-all-start.4) | async-done | bytes 16416 | tf_op jit(solution)/shard_map/all_to_all | solution.py:263
  119.8 0.9 residual.1
  120.7 0.8 copy.14
  (8 shorter events, 0.1 us)
Async XLA Ops:
  0.6 15.2 %copy-start.3 = (s32[32]{0:T(128)S(1)}, s32[32]{0:T(128)}, u32[]{:S(2)}) copy-start(s32[32]{0:T(128)} %param.15) | copy-start | bytes 388
  0.6 15.2 %copy-start.4 = (s32[32]{0:T(128)S(1)}, s32[32]{0:T(128)}, u32[]{:S(2)}) copy-start(s32[32]{0:T(128)} %param.16) | copy-start | bytes 388
  0.7 15.2 %copy-start.1 = (s32[256]{0:T(256)S(1)}, s32[256]{0:T(256)}, u32[]{:S(2)}) copy-start(s32[256]{0:T(256)} %param.17) | copy-start | bytes 3076
  0.7 15.4 %copy-start.2 = (s32[4]{0:T(128)S(1)}, s32[4]{0:T(128)}, u32[]{:S(2)}) copy-start(s32[4]{0:T(128)} %param.11) | copy-start | bytes 52
  0.7 15.4 %copy-start = (bf16[4,17,256]{2,0,1:T(4,128)(2,1)S(1)}, bf16[4,17,256]{2,0,1:T(4,128)(2,1)}, u32[]{:S(2)}) copy-start(bf16[4,17,256]{2,0,1:T(4,128)(2,1)} %param.10) | copy-start | bytes 104452
  0.7 26.7 %copy-start.5 = (f32[4]{0:T(128)S(1)}, f32[4]{0:T(128)}, u32[]{:S(2)}) copy-start(f32[4]{0:T(128)} %param.12) | copy-start | bytes 52
  2.7 34.8 %all-to-all-start = ((bf16[8,4,64,256]{3,2,1,0:T(8,128)(2,1)}), bf16[8,4,64,256]{3,2,1,0:T(8,128)(2,1)S(1)}, u32[]{:S(2)}, u32[]{:S(2)}) async-start(bf16[8,4,64,256]{3,2,1,0:T(8,128)(2,1)} %broadcast_in_dim.32), calls=%async_computation | async-start | bytes 2097152 | tf_op jit(solution)/shard_map/all_to_all | solution.py:191
  10.5 16.9 %collective-permute-start = (bf16[4,64,8]{2,1,0:T(8,128)(2,1)S(1)}, bf16[4,64,8]{2,1,0:T(8,128)(2,1)S(1)}, u32[]{:S(2)}, u32[]{:S(2)}) collective-permute-start(bf16[4,64,8]{2,1,0:T(8,128)(2,1)S(1)} %get-tuple-element.34), channel_id=1, source_target_pairs={{0,1},{1,2},{2,3},{3,4},{4,5},{5,6},{6,7},{8,9},{9,10},{10,11},{11... | collective-permute-start | bytes 12296 | tf_op jit(solution)/shard_map/ppermute | solution.py:196
  14.5 12.9 %collective-permute-start.1 = (bf16[4,64,8]{2,1,0:T(8,128)(2,1)S(1)}, bf16[4,64,8]{2,1,0:T(8,128)(2,1)S(1)}, u32[]{:S(2)}, u32[]{:S(2)}) collective-permute-start(bf16[4,64,8]{2,1,0:T(8,128)(2,1)S(1)} %get-tuple-element.35), channel_id=1, source_target_pairs={{1,0},{2,1},{3,2},{4,3},{5,4},{6,5},{7,6},{9,8},{10,9},{11,10},{12... | collective-permute-start | bytes 12296 | tf_op jit(solution)/shard_map/ppermute | solution.py:197
  39.6 6.8 %copy-start.6 = (s32[32]{0:T(128)S(1)}, s32[32]{0:T(128)}, u32[]{:S(2)}) copy-start(s32[32]{0:T(128)} %param.14) | copy-start | bytes 388
  39.6 33.1 %all-to-all-start.1 = ((bf16[64,64,256]{2,1,0:T(8,128)(2,1)}), bf16[64,64,256]{2,1,0:T(8,128)(2,1)S(1)}, u32[]{:S(2)}, u32[]{:S(2)}) async-start(bf16[64,64,256]{2,1,0:T(8,128)(2,1)} %pick.1), calls=%async_computation.1 | async-start | bytes 4194304 | tf_op jit(solution)/shard_map/all_to_all | solution.py:220
  107.6 12.2 %all-to-all-start.4 = ((f32[16,2,128]{2,1,0:T(2,128)}), f32[16,2,128]{2,1,0:T(2,128)S(1)}, u32[]{:S(2)}, u32[]{:S(2)}) async-start(f32[16,2,128]{2,1,0:T(2,128)} %get-tuple-element.22), calls=%async_computation.4 | async-start | bytes 32768 | tf_op jit(solution)/shard_map/all_to_all | solution.py:263

commit v10 on v9

--- a/solution.py
+++ b/solution.py
@@ -11,6 +11,7 @@
 BLK = 256
 CORES = 2
 X_CHIPS = 4
+CHUNK = 8
 INNER = ("x", "core")
 CHAN = ("y", "x", "core")
 VMEM = pl.BlockSpec(memory_space=pltpu.VMEM)
@@ -76,24 +77,20 @@
     inverse[...] = value
 
 
-def chunk_starts(pairs):
-    return [0] + sorted({pairs * part // 16 for part in (6, 11, 14)} - {0}) + [pairs]
-
-
 def image_kernel(
     slot, target, live, rows, coupling, banded, trial, image, sent, total, held, sems
 ):
-    starts = chunk_starts(coupling.shape[0])
-    copies = {}
-    for i, first in enumerate(starts[:-1]):
-        part = pl.ds(first, starts[i + 1] - first)
-        copies[first] = pltpu.make_async_copy(coupling.at[part], held.at[part], sems.at[i])
-        copies[first].start()
+    def copy(chunk):
+        part = pl.ds(chunk * CHUNK, CHUNK)
+        return pltpu.make_async_copy(coupling.at[part], held.at[part], sems.at[chunk])
+
+    for chunk in range(sems.shape[0]):
+        copy(chunk).start()
     total[...] = banded[...]
 
     for p in range(coupling.shape[0]):
-        if p in copies:
-            copies[p].wait()
+        if p % CHUNK == 0:
+            copy(p // CHUNK).wait()
         part = lax.dot_general(rows[slot[p]], held[p], NT, preferred_element_type=jnp.float32)
         total[target[p]] += part * live[p]
 
@@ -239,7 +236,7 @@
         scratch=[
             pltpu.VMEM(by_slot.shape, jnp.float32),
             pltpu.VMEM(coupling.shape, jnp.bfloat16),
-            pltpu.SemaphoreType.DMA((len(chunk_starts(coupling.shape[0])) - 1,)),
+            pltpu.SemaphoreType.DMA((coupling.shape[0] // CHUNK,)),
         ],
         limit=50,
     )

time: 122 us -> 122 us (level)
  no operation moved by 1% of the time
where the time goes in v10:
time: 122 us; the launch traced here: 121 us
  blocking collectives  62 us (51%)
  starting transfers between devices  25 us (20%)
  waiting for transfers between devices  13.5 us (11%)
  Pallas kernels  13.2 us (11%)
  local copies, waits for them, and re-layouts  4.55 us (4%)
  other arithmetic  1.52 us (1%)
  between operations  1.49 us (1%)
    psum x2, blocking collectives, body(): gram = lax.psum(lax.psum(gram, 'core'), 'rad')  23.1 us
    all_to_all x1, blocking collectives, body(): received = lax.all_to_all(sent, ('core', 'rad'), 0, 0, tiled=True)  18 us
    all_to_all x1, blocking collectives, body(): received = lax.all_to_all(spread, ('y', 'x'), 0, 0, tiled=True)  12.1 us
    pallas_call x6, Pallas kernels, call(): pl.pallas_call(kernel, out_shape=shapes, in_specs=specs, out_specs=(VMEM,...  11.2 us
    all_to_all x1, waiting for transfers between devices, body(): lax.all_to_all(jnp.broadcast_to(by_slot[None], (ys,) + by_slot.shape), 'y...  9.13 us
    unnamed x1, blocking collectives  8.83 us
    all_to_all x1, starting transfers between devices, body(): lax.all_to_all(jnp.broadcast_to(by_slot[None], (ys,) + by_slot.shape), 'y...  7.65 us
    all_to_all x1, starting transfers between devices, body(): rows = lax.all_to_all(picked, INNER, 0, 0, tiled=True)  6.81 us
  transfers between devices with their start and end apart: 5, of which 3 were waited for; matrix products, arithmetic and copies ran while one was open for 3% of the time, Pallas kernels for 5%

profile of v10, /device:TPU:1, one launch (start us, length us, event | category | flops | bytes accessed | tf_op | source)
XLA Modules:
  0.0 121.2 jit_solution(10311744779364866337)
XLA Ops:
  0.6 0.0 copy-start.3
  0.6 0.0 copy-start.4
  0.7 0.0 copy-start.1
  0.7 0.0 copy-start.2
  0.7 0.0 copy-start
  0.7 0.0 copy-start.5
  0.7 1.0 copy.16
  1.6 1.1 broadcast_in_dim.32
  2.7 7.7 %all-to-all-start = ((bf16[8,4,64,256]{3,2,1,0:T(8,128)(2,1)}), bf16[8,4,64,256]{3,2,1,0:T(8,128)(2,1)S(1)}, u32[]{:S(2)}, u32[]{:S(2)}) async-start(bf16[8,4,64,256]{3,2,1,0:T(8,128)(2,1)} %broadcast_in_dim.32), calls=%async_computation | async-start | bytes 2097152 | tf_op jit(solution)/shard_map/all_to_all | solution.py:188
  10.4 0.1 fusion.31
  10.5 4.0 %collective-permute-start = (bf16[4,64,8]{2,1,0:T(8,128)(2,1)S(1)}, bf16[4,64,8]{2,1,0:T(8,128)(2,1)S(1)}, u32[]{:S(2)}, u32[]{:S(2)}) collective-permute-start(bf16[4,64,8]{2,1,0:T(8,128)(2,1)S(1)} %get-tuple-element.34), channel_id=1, source_target_pairs={{0,1},{1,2},{2,3},{3,4},{4,5},{5,6},{6,7},{8,9},{9,10},{10,11},{11... | collective-permute-start | bytes 12296 | tf_op jit(solution)/shard_map/ppermute | solution.py:193
  14.5 1.3 %collective-permute-start.1 = (bf16[4,64,8]{2,1,0:T(8,128)(2,1)S(1)}, bf16[4,64,8]{2,1,0:T(8,128)(2,1)S(1)}, u32[]{:S(2)}, u32[]{:S(2)}) collective-permute-start(bf16[4,64,8]{2,1,0:T(8,128)(2,1)S(1)} %get-tuple-element.35), channel_id=1, source_target_pairs={{1,0},{2,1},{3,2},{4,3},{5,4},{6,5},{7,6},{9,8},{10,9},{11,10},{12... | collective-permute-start | bytes 12296 | tf_op jit(solution)/shard_map/ppermute | solution.py:194
  15.8 0.0 copy-done.3
  15.8 0.0 copy-done.4
  15.8 0.0 copy-done.1
  15.8 0.2 select_reduce_fusion
  16.0 0.0 copy-done.2
  16.0 0.0 copy-done
  16.1 0.1 multiply_bitcast_fusion.15
  16.1 0.1 multiply_bitcast_fusion.16
  16.2 0.1 select_reduce_fusion.2
  16.3 1.3 %dynamic-slice = u32[1]{0:T(128)} dynamic-slice(u32[512]{0:T(512)} %constant.73, u32[]{:T(128)S(6)} %add.101), dynamic_slice_sizes={1} | dynamic-slice | bytes 12
  18.2 0.2 dynamic-update-slice
  18.5 8.8 %all-reduce = s32[512]{0:T(512)S(1)} all-reduce(s32[512]{0:T(512)S(1)} %dynamic-update-slice), channel_id=2, replica_groups=mesh['y'=8,'x'=4,'core'=2,'rad'=8] {'x','core'}, use_global_device_ids=true, to_apply=%add | all-reduce | flops 512 | bytes 4096
  27.3 0.1 reshape.132.need
  27.4 0.0 collective-permute-done
  27.4 0.0 collective-permute-done.1
  27.4 0.0 copy-done.5
  27.4 1.0 fusion.16.banded
  28.4 9.1 %all-to-all-done = bf16[8,4,64,256]{3,2,1,0:T(8,128)(2,1)S(1)} async-done(((bf16[8,4,64,256]{3,2,1,0:T(8,128)(2,1)}), bf16[8,4,64,256]{3,2,1,0:T(8,128)(2,1)S(1)}, u32[]{:S(2)}, u32[]{:S(2)}) %all-to-all-start) | async-done | bytes 1048608 | tf_op jit(solution)/shard_map/all_to_all | solution.py:188
  37.6 2.0 %pick.1 = bf16[64,64,256]{2,1,0:T(8,128)(2,1)} custom-call(s32[1]{0:T(128)} %bitcast.19.mine, s32[8,64]{1,0:T(8,128)S(1)} %reshape.132.need, bf16[32,64,256]{2,1,0:T(8,128)(2,1)S(1)} %bitcast.43), custom_call_target="tpu_custom_call" | custom-call | tf_op jit(solution)/shard_map/pick/pallas_call | solution.py:204
  39.6 0.0 copy-start.6
  39.6 6.8 %all-to-all-start.1 = ((bf16[64,64,256]{2,1,0:T(8,128)(2,1)}), bf16[64,64,256]{2,1,0:T(8,128)(2,1)S(1)}, u32[]{:S(2)}, u32[]{:S(2)}) async-start(bf16[64,64,256]{2,1,0:T(8,128)(2,1)} %pick.1), calls=%async_computation.1 | async-start | bytes 4194304 | tf_op jit(solution)/shard_map/all_to_all | solution.py:217
  46.5 0.0 copy-done.6
  46.5 0.5 gram.1
  47.0 2.5 %psum.14 = f32[4,128]{1,0:T(4,128)S(1)} all-reduce(f32[4,128]{1,0:T(4,128)S(1)} %constant_dynamic-slice_fusion), channel_id=1, replica_groups=mesh['y'=8,'x'=4,'core'=2,'rad'=8] {'core'}, use_global_device_ids=true, to_apply=%region_3.4 | all-reduce | flops 512 | bytes 4096 | tf_op jit(solution)/shard_map/psum | solution.py:221
  49.5 20.6 %psum.15.gram = f32[4,128]{1,0:T(4,128)S(1)} all-reduce(f32[4,128]{1,0:T(4,128)S(1)} %psum.14), channel_id=1, replica_groups=mesh['y'=8,'x'=4,'core'=2,'rad'=8] {'rad'}, use_global_device_ids=true, to_apply=%region_4.5 | all-reduce | flops 512 | bytes 4096 | tf_op jit(solution)/shard_map/psum | solution.py:221
  70.1 2.7 %all-to-all-done.1.rows = bf16[64,64,256]{2,1,0:T(8,128)(2,1)S(1)} async-done(((bf16[64,64,256]{2,1,0:T(8,128)(2,1)}), bf16[64,64,256]{2,1,0:T(8,128)(2,1)S(1)}, u32[]{:S(2)}, u32[]{:S(2)}) %all-to-all-start.1) | async-done | bytes 2097184 | tf_op jit(solution)/shard_map/all_to_all | solution.py:217
  72.8 3.9 %image.1 = (bf16[4,64,256]{2,1,0:T(8,128)(2,1)S(1)}, f32[32,128]{1,0:T(8,128)S(1)}) custom-call(s32[32]{0:T(128)S(1)} %multiply_add_fusion.slot, s32[32]{0:T(128)S(1)} %broadcast_subtract_fusion.target, f32[32]{0:T(128)S(1)} %compare_convert_fusion.9.live, bf16[64,64,256]{2,1,0:T(8,128)(2,1)S(1)} %all-to-all-done.1.rows, bf16[32,256,256]{2,1,0:T(8,128)(2,1)} %coupling.1, ...), custom_call_target="tpu_custom_call" | custom-call | tf_op jit(solution)/shard_map/image/pallas_call | solution.py:148
  76.7 18.0 %all_to_all.25.received = f32[16,2,128]{2,1,0:T(2,128)S(1)} all-to-all(f32[16,2,128]{2,1,0:T(2,128)S(1)} %bitcast.52), channel_id=1, replica_groups=mesh['y'=8,'x'=4,'core'=2,'rad'=8] {'core','rad'}, dimensions={0} | all-to-all | bytes 32768 | tf_op jit(solution)/shard_map/all_to_all | solution.py:246
  94.7 12.1 %all_to_all.26.received = f32[96,2,128]{2,1,0:T(2,128)S(1)} all-to-all(f32[96,2,128]{2,1,0:T(2,128)S(1)} %middle.1), channel_id=1, replica_groups=mesh['y'=8,'x'=4,'core'=2,'rad'=8] {'y','x'}, dimensions={0} | all-to-all | bytes 196608 | tf_op jit(solution)/shard_map/all_to_all | solution.py:255
  106.8 0.7 last.1
  107.4 5.2 %all-to-all-start.4 = ((f32[16,2,128]{2,1,0:T(2,128)}), f32[16,2,128]{2,1,0:T(2,128)S(1)}, u32[]{:S(2)}, u32[]{:S(2)}) async-start(f32[16,2,128]{2,1,0:T(2,128)} %get-tuple-element.22), calls=%async_computation.4 | async-start | bytes 32768 | tf_op jit(solution)/shard_map/all_to_all | solution.py:260
  112.6 5.3 %inverse.1 = f32[64,64]{1,0:T(8,128)S(1)} custom-call(f32[64,64]{1,0:T(8,128)S(1)} %get-tuple-element.21.square), custom_call_target="tpu_custom_call" | custom-call | tf_op jit(solution)/shard_map/inverse/pallas_call | solution.py:148
  118.0 1.6 %all-to-all-done.4 = f32[16,2,128]{2,1,0:T(2,128)S(1)} async-done(((f32[16,2,128]{2,1,0:T(2,128)}), f32[16,2,128]{2,1,0:T(2,128)S(1)}, u32[]{:S(2)}, u32[]{:S(2)}) %all-to-all-start.4) | async-done | bytes 16416 | tf_op jit(solution)/shard_map/all_to_all | solution.py:260
  119.6 0.9 residual.1
  120.5 0.8 copy.14
  (8 shorter events, 0.1 us)
Async XLA Ops:
  0.6 15.2 %copy-start.3 = (s32[32]{0:T(128)S(1)}, s32[32]{0:T(128)}, u32[]{:S(2)}) copy-start(s32[32]{0:T(128)} %param.15) | copy-start | bytes 388
  0.6 15.2 %copy-start.4 = (s32[32]{0:T(128)S(1)}, s32[32]{0:T(128)}, u32[]{:S(2)}) copy-start(s32[32]{0:T(128)} %param.16) | copy-start | bytes 388
  0.7 15.2 %copy-start.1 = (s32[256]{0:T(256)S(1)}, s32[256]{0:T(256)}, u32[]{:S(2)}) copy-start(s32[256]{0:T(256)} %param.17) | copy-start | bytes 3076
  0.7 15.4 %copy-start.2 = (s32[4]{0:T(128)S(1)}, s32[4]{0:T(128)}, u32[]{:S(2)}) copy-start(s32[4]{0:T(128)} %param.11) | copy-start | bytes 52
  0.7 15.4 %copy-start = (bf16[4,17,256]{2,0,1:T(4,128)(2,1)S(1)}, bf16[4,17,256]{2,0,1:T(4,128)(2,1)}, u32[]{:S(2)}) copy-start(bf16[4,17,256]{2,0,1:T(4,128)(2,1)} %param.10) | copy-start | bytes 104452
  0.7 26.7 %copy-start.5 = (f32[4]{0:T(128)S(1)}, f32[4]{0:T(128)}, u32[]{:S(2)}) copy-start(f32[4]{0:T(128)} %param.12) | copy-start | bytes 52
  2.7 34.8 %all-to-all-start = ((bf16[8,4,64,256]{3,2,1,0:T(8,128)(2,1)}), bf16[8,4,64,256]{3,2,1,0:T(8,128)(2,1)S(1)}, u32[]{:S(2)}, u32[]{:S(2)}) async-start(bf16[8,4,64,256]{3,2,1,0:T(8,128)(2,1)} %broadcast_in_dim.32), calls=%async_computation | async-start | bytes 2097152 | tf_op jit(solution)/shard_map/all_to_all | solution.py:188
  10.5 16.9 %collective-permute-start = (bf16[4,64,8]{2,1,0:T(8,128)(2,1)S(1)}, bf16[4,64,8]{2,1,0:T(8,128)(2,1)S(1)}, u32[]{:S(2)}, u32[]{:S(2)}) collective-permute-start(bf16[4,64,8]{2,1,0:T(8,128)(2,1)S(1)} %get-tuple-element.34), channel_id=1, source_target_pairs={{0,1},{1,2},{2,3},{3,4},{4,5},{5,6},{6,7},{8,9},{9,10},{10,11},{11... | collective-permute-start | bytes 12296 | tf_op jit(solution)/shard_map/ppermute | solution.py:193
  14.5 12.9 %collective-permute-start.1 = (bf16[4,64,8]{2,1,0:T(8,128)(2,1)S(1)}, bf16[4,64,8]{2,1,0:T(8,128)(2,1)S(1)}, u32[]{:S(2)}, u32[]{:S(2)}) collective-permute-start(bf16[4,64,8]{2,1,0:T(8,128)(2,1)S(1)} %get-tuple-element.35), channel_id=1, source_target_pairs={{1,0},{2,1},{3,2},{4,3},{5,4},{6,5},{7,6},{9,8},{10,9},{11,10},{12... | collective-permute-start | bytes 12296 | tf_op jit(solution)/shard_map/ppermute | solution.py:194
  39.6 6.8 %copy-start.6 = (s32[32]{0:T(128)S(1)}, s32[32]{0:T(128)}, u32[]{:S(2)}) copy-start(s32[32]{0:T(128)} %param.14) | copy-start | bytes 388
  39.6 33.1 %all-to-all-start.1 = ((bf16[64,64,256]{2,1,0:T(8,128)(2,1)}), bf16[64,64,256]{2,1,0:T(8,128)(2,1)S(1)}, u32[]{:S(2)}, u32[]{:S(2)}) async-start(bf16[64,64,256]{2,1,0:T(8,128)(2,1)} %pick.1), calls=%async_computation.1 | async-start | bytes 4194304 | tf_op jit(solution)/shard_map/all_to_all | solution.py:217
  107.4 12.2 %all-to-all-start.4 = ((f32[16,2,128]{2,1,0:T(2,128)}), f32[16,2,128]{2,1,0:T(2,128)S(1)}, u32[]{:S(2)}, u32[]{:S(2)}) async-start(f32[16,2,128]{2,1,0:T(2,128)} %get-tuple-element.22), calls=%async_computation.4 | async-start | bytes 32768 | tf_op jit(solution)/shard_map/all_to_all | solution.py:260
